TPU v7x, 32 devices: a whole 2x2x4 slice. The times are simulated.
32 devices in a mesh: along: 4 (over z), cross: 2 (over core), batch: 4 (over y, x).
Axes of the slice: x: 2, y: 2, z: 4, core: 2. Of those that a mesh axis runs over, the one named last changes fastest.
Arguments:
- pressure_start: float32 [4, 16, 256, 256], P('batch', None, 'along', 'cross'), may hold values from -6 to 6
- along_start: float32 [4, 16, 256, 256], P('batch', None, 'along', 'cross'), may hold values from -6 to 6
- cross_start: float32 [4, 16, 256, 256], P('batch', None, 'along', 'cross'), may hold values from -6 to 6
- depth_layers: int32 [256, 256], P('along', 'cross'), may hold values from 1 to 16
- stiffness: float32 [256, 256], P('along', 'cross'), may hold values from 0.1 to 0.45
- patch_lists: int32 [4, 512], P('batch'), may hold values from 0 to 1023, all different within a row
- owner_map: int32 [8, 128], P(('along', 'cross')), may hold values from 0 to 7, as said below
Outputs:
- adjoint_pressure: float32 [4, 16, 256, 256], P('batch', None, 'along', 'cross')
- panel_store: float32 [8, 136, 4, 512], P(('along', 'cross'), None, 'batch')
Inputs may be any that keep to these rules, and one draw needn't show every extreme that they name: `owner_map`: each entry is an owner, numbered as the grid blocks. Of the 128 patches of one block at most 17 have one owner, and in every draw some owner holds exactly 17 patches of every block. `patch_lists`: each row names 512 different patch ids; every patch is named by some row.
All inputs are finite; a program needn't handle non-finite values.
Results may differ from a plain program's by a relative error of at most 0.0003.
Values sent between devices are 32-bit elements; how exact they have to be, the bound alone decides.
No kernel may reach another device: no remote copies, remote signals or barrier semaphores. Data moves between devices by JAX's collectives and lax.ppermute only.
A program may use at most 64 MiB of HBM per device.

v0:
```python
import jax
import jax.numpy as jnp
from jax import lax
from jax.sharding import PartitionSpec as P

STEPS = 8


def padded(block, sides, width):
    for axis, dim in sides:
        count = lax.axis_size(axis)
        forward = [(i, i + 1) for i in range(count - 1)]
        backward = [(target, source) for source, target in forward]
        low = lax.ppermute(
            lax.slice_in_dim(block, block.shape[dim] - width, None, axis=dim), axis, forward
        )
        high = lax.ppermute(lax.slice_in_dim(block, 0, width, axis=dim), axis, backward)
        block = jnp.concatenate([low, block, high], axis=dim)
    return block


def column_masks(depth, layers):
    row_count, col_count = depth.shape
    layer_index = lax.broadcasted_iota(jnp.int32, (layers, row_count, col_count), 0)
    wet_mask = (layer_index < depth[None]).astype(jnp.float32)
    onehot = (layer_index == depth[None] - 1).astype(jnp.float32)
    zero_layer = jnp.zeros((1, row_count, col_count), jnp.float32)
    wet_upper = jnp.concatenate([zero_layer, wet_mask[:-1]], 0)
    wet_lower = jnp.concatenate([wet_mask[1:], zero_layer], 0)
    return (wet_mask, onehot, wet_upper, wet_lower)


def run_steps(pressure, flow_along, flow_cross, depth, stiffness, edges_ahead, edges_behind):
    sensors, layers, row_count, col_count = pressure.shape
    wet_mask, onehot, wet_upper, wet_lower = column_masks(depth, layers)
    zero_sensor_layer = jnp.zeros((sensors, 1, row_count, col_count), jnp.float32)
    traces = []
    for step_index in range(STEPS):
        ahead_row, ahead_col = edges_ahead(pressure)
        flow_along = wet_mask * (
            flow_along - (jnp.concatenate([pressure[:, :, 1:, :], ahead_row], 2) - pressure)
        )
        flow_cross = wet_mask * (
            flow_cross - (jnp.concatenate([pressure[:, :, :, 1:], ahead_col], 3) - pressure)
        )
        behind_row, behind_col = edges_behind(flow_along, flow_cross)
        behind = jnp.concatenate([behind_row, flow_along[:, :, :-1, :]], 2)
        before = jnp.concatenate([behind_col, flow_cross[:, :, :, :-1]], 3)
        upper_layer = jnp.concatenate([zero_sensor_layer, pressure[:, :-1]], 1)
        lower_layer = jnp.concatenate([pressure[:, 1:], zero_sensor_layer], 1)
        vertical = wet_upper * (upper_layer - pressure) + wet_lower * (lower_layer - pressure)
        pressure = wet_mask * (
            pressure
            - stiffness * (flow_along - behind + (flow_cross - before))
            + 0.5 * stiffness * vertical
        )
        traces.append(jnp.sum(pressure * onehot, axis=1))
    return (pressure, jnp.stack(traces, 1))


def shards(
    pressure_start, along_start, cross_start, depth_layers, stiffness, patch_lists, owner_map
):
    sensors, layers, row_count, col_count = pressure_start.shape
    margin = STEPS
    columns = jnp.stack([depth_layers.astype(jnp.float32), stiffness])
    columns_wide = padded(columns, (("along", 1), ("cross", 2)), margin)
    depth_wide = columns_wide[0].astype(jnp.int32)
    stiff_wide = columns_wide[1]
    fields = jnp.stack([pressure_start, along_start, cross_start])
    fields_wide = padded(fields, (("along", 3), ("cross", 4)), margin)
    wide_rows = row_count + 2 * margin
    wide_cols = col_count + 2 * margin

    def zero_ahead(pressure):
        return (
            jnp.zeros((sensors, layers, 1, wide_cols), jnp.float32),
            jnp.zeros((sensors, layers, wide_rows, 1), jnp.float32),
        )

    def zero_behind(flow_along, flow_cross):
        return (
            jnp.zeros((sensors, layers, 1, wide_cols), jnp.float32),
            jnp.zeros((sensors, layers, wide_rows, 1), jnp.float32),
        )

    pressure_wide, trace_wide = run_steps(
        fields_wide[0],
        fields_wide[1],
        fields_wide[2],
        depth_wide,
        stiff_wide,
        zero_ahead,
        zero_behind,
    )
    pressure = pressure_wide[:, :, margin : margin + row_count, margin : margin + col_count]
    trace_all = trace_wide[:, :, margin : margin + row_count, margin : margin + col_count]
    patch_count = 2 * row_count
    patch_width = col_count // 2
    owner_count = lax.axis_size("along") * lax.axis_size("cross")
    capacity = patch_count // owner_count + 1
    slot_count = owner_count * capacity
    first_patch = (
        lax.axis_index("along") * lax.axis_size("cross") + lax.axis_index("cross")
    ) * patch_count
    local_ids = patch_lists - first_patch
    positions = jnp.arange(patch_count, dtype=jnp.int32)
    member = jnp.any(local_ids[:, :, None] == positions[None, None, :], axis=1).astype(jnp.float32)
    panels = trace_all.reshape(sensors, STEPS, patch_count, patch_width) * member[:, None, :, None]
    owners = owner_map[0]
    earlier = positions[None, :] < positions[:, None]
    slot_rank = jnp.sum(((owners[:, None] == owners[None, :]) & earlier).astype(jnp.int32), axis=1)
    target = owners * capacity + slot_rank
    placement = (jnp.arange(slot_count, dtype=jnp.int32)[:, None] == target[None, :]).astype(
        jnp.float32
    )
    outgoing = jnp.einsum("nj,stjc->nstc", placement, panels, precision=lax.Precision.HIGHEST)
    outgoing = outgoing.reshape(slot_count, sensors, STEPS * patch_width)
    received = lax.all_to_all(outgoing, ("along", "cross"), split_axis=0, concat_axis=0, tiled=True)
    return (pressure, received[None])


def solution(mesh):
    in_specs = (
        P("batch", None, "along", "cross"),
        P("batch", None, "along", "cross"),
        P("batch", None, "along", "cross"),
        P("along", "cross"),
        P("along", "cross"),
        P("batch", None),
        P(("along", "cross"), None),
    )
    out_specs = (P("batch", None, "along", "cross"), P(("along", "cross"), None, "batch", None))
    return jax.shard_map(shards, mesh=mesh, in_specs=in_specs, out_specs=out_specs, check_vma=False)
```

profile of v0, /device:TPU:0, one launch (start us, length us, event | category | flops | bytes accessed | tf_op | source)
XLA Modules:
  0.0 94.3 jit_solution(7264263156540161137)
XLA Ops:
  0.7 0.8 convert_bitcast_fusion
  1.4 0.7 pad_maximum_fusion.8
  2.1 4.9 %collective-permute-start = (f32[2,8,128]{2,1,0:T(8,128)S(1)}, f32[2,8,128]{2,1,0:T(8,128)S(1)}, u32[]{:S(2)}, u32[]{:S(2)}) collective-permute-start(f32[2,8,128]{2,1,0:T(8,128)S(1)} %get-tuple-element.59), channel_id=1, source_target_pairs={{0,8},{8,16},{16,24},{1,9},{9,17},{17,25},{2,10},{10,18},{18,26},{... | collective-permute-start | bytes 24584 | tf_op jit(solution)/shard_map/ppermute | solution.py:14
  7.1 1.3 %collective-permute-start.1 = (f32[2,8,128]{2,1,0:T(8,128)S(1)}, f32[2,8,128]{2,1,0:T(8,128)S(1)}, u32[]{:S(2)}, u32[]{:S(2)}) collective-permute-start(f32[2,8,128]{2,1,0:T(8,128)S(1)} %get-tuple-element.60), channel_id=1, source_target_pairs={{8,0},{16,8},{24,16},{9,1},{17,9},{25,17},{10,2},{18,10},{26,18},{... | collective-permute-start | bytes 24584 | tf_op jit(solution)/shard_map/ppermute | solution.py:17
  8.4 1.8 %pad_maximum_fusion.4 = (f32[3,1,16,8,128]{4,3,2,1,0:T(8,128)}, f32[3,1,16,8,128]{4,3,2,1,0:T(8,128)}) fusion(f32[1,1,16,64,128]{4,3,2,1,0:T(8,128)} %bitcast.199, f32[1,1,16,64,128]{4,3,2,1,0:T(8,128)} %bitcast.202, f32[1,1,16,64,128]{4,3,2,1,0:T(8,128)} %bitcast.205), kind=kLoop, calls=%fused_computation.89 | loop fusion | flops 196608 | bytes 1966080 | tf_op jit(solution)/shard_map/slice | solution.py:15
  10.1 5.2 %collective-permute-start.4 = (f32[3,1,16,8,128]{4,3,2,1,0:T(8,128)}, f32[3,1,16,8,128]{4,3,2,1,0:T(8,128)}, u32[]{:S(2)}, u32[]{:S(2)}) collective-permute-start(f32[3,1,16,8,128]{4,3,2,1,0:T(8,128)} %get-tuple-element.21), channel_id=1, source_target_pairs={{0,8},{8,16},{16,24},{1,9},{9,17},{17,25},{2,10},{10,18},{18,26},{... | collective-permute-start | bytes 589832 | tf_op jit(solution)/shard_map/ppermute | solution.py:14
  15.4 1.3 %collective-permute-start.5 = (f32[3,1,16,8,128]{4,3,2,1,0:T(8,128)}, f32[3,1,16,8,128]{4,3,2,1,0:T(8,128)}, u32[]{:S(2)}, u32[]{:S(2)}) collective-permute-start(f32[3,1,16,8,128]{4,3,2,1,0:T(8,128)} %get-tuple-element.22), channel_id=1, source_target_pairs={{8,0},{16,8},{24,16},{9,1},{17,9},{25,17},{10,2},{18,10},{26,18},{... | collective-permute-start | bytes 589832 | tf_op jit(solution)/shard_map/ppermute | solution.py:17
  16.7 0.2 convert_reduce_fusion
  17.0 1.3 %collective-permute-start.2 = (f32[2,80,8]{2,1,0:T(8,128)S(1)}, f32[2,80,8]{2,1,0:T(8,128)S(1)}, u32[]{:S(2)}, u32[]{:S(2)}) collective-permute-start(f32[2,80,8]{2,1,0:T(8,128)S(1)} %get-tuple-element.57), channel_id=1, source_target_pairs={{0,4},{1,5},{2,6},{3,7},{8,12},{9,13},{10,14},{11,15},{16,20},{17,... | collective-permute-start | bytes 15368 | tf_op jit(solution)/shard_map/ppermute | solution.py:14
  18.3 1.3 %collective-permute-start.3 = (f32[2,80,8]{2,1,0:T(8,128)S(1)}, f32[2,80,8]{2,1,0:T(8,128)S(1)}, u32[]{:S(2)}, u32[]{:S(2)}) collective-permute-start(f32[2,80,8]{2,1,0:T(8,128)S(1)} %get-tuple-element.58), channel_id=1, source_target_pairs={{4,0},{5,1},{6,2},{7,3},{12,8},{13,9},{14,10},{15,11},{20,16},{21,... | collective-permute-start | bytes 15368 | tf_op jit(solution)/shard_map/ppermute | solution.py:17
  19.8 1.7 %collective-permute-done.3 = f32[2,80,8]{2,1,0:T(8,128)S(1)} collective-permute-done((f32[2,80,8]{2,1,0:T(8,128)S(1)}, f32[2,80,8]{2,1,0:T(8,128)S(1)}, u32[]{:S(2)}, u32[]{:S(2)}) %collective-permute-start.3) | collective-permute-done | bytes 5152 | tf_op jit(solution)/shard_map/ppermute | solution.py:17
  21.8 0.3 fusion.51
  22.1 1.2 %collective-permute-done.5 = f32[3,1,16,8,128]{4,3,2,1,0:T(8,128)} collective-permute-done((f32[3,1,16,8,128]{4,3,2,1,0:T(8,128)}, f32[3,1,16,8,128]{4,3,2,1,0:T(8,128)}, u32[]{:S(2)}, u32[]{:S(2)}) %collective-permute-start.5) | collective-permute-done | bytes 196640 | tf_op jit(solution)/shard_map/ppermute | solution.py:17
  23.4 1.2 %pad_maximum_fusion.1 = f32[3,1,16,80,128]{4,3,2,1,0:T(8,128)S(1)} fusion(f32[3,1,16,8,128]{4,3,2,1,0:T(8,128)} %collective-permute-done.5, f32[1,1,16,64,128]{4,3,2,1,0:T(8,128)S(1)} %bitcast.200, f32[1,1,16,64,128]{4,3,2,1,0:T(8,128)S(1)} %bitcast.204, f32[1,1,16,64,128]{4,3,2,1,0:T(8,128)S(1)} %bitcast.207, f32[3,1,16,8,128]{4,3,2,1,0:T(8,128)} %collective-permute-done.4), kind=kLoop, calls=%fused_computation.1 | loop fusion | flops 1966080 | bytes 3932160 | tf_op jit(solution)/shard_map/concatenate | solution.py:18
  24.5 2.5 %fusion.43 = (f32[3,1,16,80,8]{4,3,2,1,0:T(8,128)}, f32[3,1,16,80,8]{4,3,2,1,0:T(8,128)}) fusion(f32[3,1,16,80,128]{4,3,2,1,0:T(8,128)S(1)} %pad_maximum_fusion.1), kind=kLoop, calls=%fused_computation.116 | loop fusion | bytes 491520 | tf_op jit(solution)/shard_map/slice | solution.py:15
  27.0 2.8 %copy.38 = f32[3,1,16,80,8]{3,4,2,1,0:T(8,128)} copy(f32[3,1,16,80,8]{4,3,2,1,0:T(8,128)} %get-tuple-element.19) | data formatting | bytes 245760 | tf_op jit(solution)/shard_map/slice | solution.py:15
  29.8 2.8 %copy.39 = f32[3,1,16,80,8]{3,4,2,1,0:T(8,128)} copy(f32[3,1,16,80,8]{4,3,2,1,0:T(8,128)} %get-tuple-element.20) | data formatting | bytes 245760 | tf_op jit(solution)/shard_map/slice | solution.py:17
  32.6 1.3 %collective-permute-start.7 = (f32[3,1,16,80,8]{3,4,2,1,0:T(8,128)}, f32[3,1,16,80,8]{3,4,2,1,0:T(8,128)}, u32[]{:S(2)}, u32[]{:S(2)}) collective-permute-start(f32[3,1,16,80,8]{3,4,2,1,0:T(8,128)} %copy.39), channel_id=1, source_target_pairs={{4,0},{5,1},{6,2},{7,3},{12,8},{13,9},{14,10},{15,11},{20,16},{21,... | collective-permute-start | bytes 368648 | tf_op jit(solution)/shard_map/ppermute | solution.py:17
  33.9 4.4 %collective-permute-start.6 = (f32[3,1,16,80,8]{3,4,2,1,0:T(8,128)}, f32[3,1,16,80,8]{3,4,2,1,0:T(8,128)}, u32[]{:S(2)}, u32[]{:S(2)}) collective-permute-start(f32[3,1,16,80,8]{3,4,2,1,0:T(8,128)} %copy.38), channel_id=1, source_target_pairs={{0,4},{1,5},{2,6},{3,7},{8,12},{9,13},{10,14},{11,15},{16,20},{17,... | collective-permute-start | bytes 368648 | tf_op jit(solution)/shard_map/ppermute | solution.py:14
  38.3 0.7 collective-permute-done.6
  38.9 2.8 %copy.40 = f32[3,1,16,80,8]{4,3,2,1,0:T(8,128)} copy(f32[3,1,16,80,8]{3,4,2,1,0:T(8,128)} %collective-permute-done.6) | data formatting | bytes 245760 | tf_op jit(solution)/shard_map/ppermute | solution.py:14
  41.8 2.8 %copy.41 = f32[3,1,16,80,8]{4,3,2,1,0:T(8,128)} copy(f32[3,1,16,80,8]{3,4,2,1,0:T(8,128)} %collective-permute-done.7) | data formatting | bytes 245760 | tf_op jit(solution)/shard_map/ppermute | solution.py:17
  44.5 5.0 %pad_maximum_fusion = f32[3,1,16,80,144]{4,3,2,1,0:T(8,128)S(1)} fusion(f32[3,1,16,80,8]{4,3,2,1,0:T(8,128)} %copy.41, f32[3,1,16,8,128]{4,3,2,1,0:T(8,128)} %collective-permute-done.5, f32[1,1,16,64,128]{4,3,2,1,0:T(8,128)S(1)} %bitcast.201, f32[1,1,16,64,128]{4,3,2,1,0:T(8,128)} %bitcast.203, f32[1,1,16,64,128]{4,3,2,1,0:T(8,128)} %bitcast.206, ...), kind=kLoop, calls=%fused_computation | loop fusion | flops 3317760 | bytes 4423680 | tf_op jit(solution)/shard_map/concatenate | solution.py:18
  49.6 0.4 slice.271
  50.2 0.3 fusion.52
  50.4 0.6 fusion.3
  51.0 1.4 %fusion.7 = f32[1,16,80,144]{3,2,1,0:T(8,128)S(1)} fusion(f32[1,15,80,144]{3,2,1,0:T(8,128)S(1)} %get-tuple-element.54, f32[1,15,80,144]{3,2,1,0:T(8,128)S(1)} %get-tuple-element.53, f32[1,16,80,144]{3,2,1,0:T(8,128)S(1)} %get-tuple-element.18, f32[1,16,80,143]{3,2,1,0:T(8,128)S(1)} %bitcast.184, f32[1,16,80,144]{3,2,1,0:T(8,128)S(1)} %get-tuple-element.17, ...), kind=kLoop, calls=%fused_computation.20 | loop fusion | flops 2580480 | bytes 7312384 | tf_op jit(solution)/shard_map/mul | solution.py:52
  52.5 0.4 slice.279
  53.0 0.3 fusion.50
  53.3 0.6 subtract_select_fusion.13
  53.9 1.4 %fusion.11 = f32[1,16,80,144]{3,2,1,0:T(8,128)S(1)} fusion(f32[1,16,80,144]{3,2,1,0:T(8,128)S(1)} %fusion.7, f32[1,15,80,144]{3,2,1,0:T(8,128)S(1)} %get-tuple-element.50, f32[1,15,80,144]{3,2,1,0:T(8,128)S(1)} %get-tuple-element.49, f32[1,16,80,144]{3,2,1,0:T(8,128)S(1)} %get-tuple-element.36, f32[1,16,80,143]{3,2,1,0:T(8,128)S(1)} %bitcast.186, ...), kind=kLoop, calls=%fused_computation.24 | loop fusion | flops 2580480 | bytes 7312384 | tf_op jit(solution)/shard_map/mul | solution.py:52
  55.3 0.4 slice.285
  55.8 0.3 fusion.49
  56.1 0.6 subtract_select_fusion.11
  56.7 1.4 %fusion.15 = f32[1,16,80,144]{3,2,1,0:T(8,128)S(1)} fusion(f32[1,16,80,144]{3,2,1,0:T(8,128)S(1)} %fusion.11, f32[1,15,80,144]{3,2,1,0:T(8,128)S(1)} %get-tuple-element.48, f32[1,15,80,144]{3,2,1,0:T(8,128)S(1)} %get-tuple-element.47, f32[1,16,80,144]{3,2,1,0:T(8,128)S(1)} %get-tuple-element.34, f32[1,16,80,143]{3,2,1,0:T(8,128)S(1)} %bitcast.188, ...), kind=kLoop, calls=%fused_computation.28 | loop fusion | flops 2580480 | bytes 7312384 | tf_op jit(solution)/shard_map/mul | solution.py:52
  58.2 0.4 slice.291
  58.7 0.3 fusion.48
  59.0 0.6 subtract_select_fusion.9
  59.5 1.4 %fusion.19 = f32[1,16,80,144]{3,2,1,0:T(8,128)S(1)} fusion(f32[1,16,80,144]{3,2,1,0:T(8,128)S(1)} %fusion.15, f32[1,15,80,144]{3,2,1,0:T(8,128)S(1)} %get-tuple-element.46, f32[1,15,80,144]{3,2,1,0:T(8,128)S(1)} %get-tuple-element.45, f32[1,16,80,144]{3,2,1,0:T(8,128)S(1)} %get-tuple-element.32, f32[1,16,80,143]{3,2,1,0:T(8,128)S(1)} %bitcast.190, ...), kind=kLoop, calls=%fused_computation.32 | loop fusion | flops 2580480 | bytes 7312384 | tf_op jit(solution)/shard_map/mul | solution.py:52
  61.0 0.4 slice.297
  61.5 0.3 fusion.47
  61.8 0.8 subtract_select_fusion.7
  62.6 1.4 %fusion.23 = f32[1,16,80,144]{3,2,1,0:T(8,128)S(1)} fusion(f32[1,16,80,144]{3,2,1,0:T(8,128)S(1)} %fusion.19, f32[1,15,80,144]{3,2,1,0:T(8,128)S(1)} %get-tuple-element.44, f32[1,15,80,144]{3,2,1,0:T(8,128)S(1)} %get-tuple-element.43, f32[1,16,80,144]{3,2,1,0:T(8,128)S(1)} %get-tuple-element.30, f32[1,16,80,143]{3,2,1,0:T(8,128)S(1)} %bitcast.192, ...), kind=kLoop, calls=%fused_computation.36 | loop fusion | flops 2580480 | bytes 7312384 | tf_op jit(solution)/shard_map/mul | solution.py:52
  64.1 0.4 slice.303
  64.6 0.3 fusion.46
  64.9 0.6 subtract_select_fusion.5
  65.5 1.4 %fusion.27 = f32[1,16,80,144]{3,2,1,0:T(8,128)S(1)} fusion(f32[1,16,80,144]{3,2,1,0:T(8,128)S(1)} %fusion.23, f32[1,15,80,144]{3,2,1,0:T(8,128)S(1)} %get-tuple-element.42, f32[1,15,80,144]{3,2,1,0:T(8,128)S(1)} %get-tuple-element.41, f32[1,16,80,144]{3,2,1,0:T(8,128)S(1)} %get-tuple-element.28, f32[1,16,80,143]{3,2,1,0:T(8,128)S(1)} %bitcast.194, ...), kind=kLoop, calls=%fused_computation.40 | loop fusion | flops 2580480 | bytes 7312384 | tf_op jit(solution)/shard_map/mul | solution.py:52
  66.9 0.4 slice.309
  67.4 0.3 fusion.45
  67.7 0.6 subtract_select_fusion.3
  68.3 1.4 %fusion.31 = f32[1,16,80,144]{3,2,1,0:T(8,128)S(1)} fusion(f32[1,16,80,144]{3,2,1,0:T(8,128)S(1)} %fusion.27, f32[1,15,80,144]{3,2,1,0:T(8,128)S(1)} %get-tuple-element.40, f32[1,15,80,144]{3,2,1,0:T(8,128)S(1)} %get-tuple-element.39, f32[1,16,80,144]{3,2,1,0:T(8,128)S(1)} %get-tuple-element.26, f32[1,16,80,143]{3,2,1,0:T(8,128)S(1)} %bitcast.196, ...), kind=kLoop, calls=%fused_computation.44 | loop fusion | flops 2580480 | bytes 7312384 | tf_op jit(solution)/shard_map/mul | solution.py:52
  69.7 0.4 slice.315
  70.3 0.3 fusion.44
  70.5 0.6 subtract_select_fusion.1
  71.1 3.5 %select_reduce_fusion = (f32[80,144]{1,0:T(8,128)S(1)}, f32[80,144]{1,0:T(8,128)S(1)}, f32[80,144]{1,0:T(8,128)S(1)}, f32[80,144]{1,0:T(8,128)S(1)}, f32[80,144]...) fusion(s32[80,144]{1,0:T(8,128)S(1)} %add_bitcast_fusion, ...), kind=kLoop, calls=%fused_computation.57 | loop fusion | flops 5621760 | bytes 12150784 | tf_op jit(solution)/shard_map/reduce_sum | solution.py:57
  75.6 0.2 slice.320
  75.8 0.2 copy.50
  76.2 0.2 copy.51
  76.4 0.3 convolution_bitcast_fusion
  76.7 1.0 %copy.52 = f32[136,1,512]{2,1,0:T(1,128)} copy(f32[136,1,512]{2,0,1:T(8,128)S(1)} %convolution_bitcast_fusion) | data formatting | bytes 557056 | tf_op jit(solution)/shard_map/nj,stjc->nstc/dot_general | solution.py:117
  77.7 5.7 %all-to-all-start = ((f32[136,1,512]{2,1,0:T(1,128)}), f32[136,1,512]{2,1,0:T(1,128)S(1)}, u32[]{:S(2)}, u32[]{:S(2)}) async-start(f32[136,1,512]{2,1,0:T(1,128)} %copy.52), calls=%async_computation | async-start | bytes 557056 | tf_op jit(solution)/shard_map/all_to_all | solution.py:119
  83.5 2.2 %slice.319 = f32[1,16,64,128]{3,2,1,0:T(8,128)} slice(f32[1,16,80,144]{3,2,1,0:T(8,128)} %get-tuple-element.16), slice={[0:1], [0:16], [8:72], [8:136]} | slice | bytes 1048576 | tf_op jit(solution)/shard_map/slice | solution.py:96
  85.7 7.9 %all-to-all-done = f32[136,1,512]{2,1,0:T(1,128)S(1)} async-done(((f32[136,1,512]{2,1,0:T(1,128)}), f32[136,1,512]{2,1,0:T(1,128)S(1)}, u32[]{:S(2)}, u32[]{:S(2)}) %all-to-all-start) | async-done | bytes 278560 | tf_op jit(solution)/shard_map/all_to_all | solution.py:119
  93.5 0.7 copy.69
  (55 shorter events, 2.6 us)
Async XLA Ops:
  0.6 16.3 %copy-start.3 = (f32[64,128]{1,0:T(8,128)S(1)}, f32[64,128]{1,0:T(8,128)}, u32[]{:S(2)}) copy-start(f32[64,128]{1,0:T(8,128)} %param.11) | copy-start | bytes 98308
  0.6 16.0 %copy-start.5 = (s32[1,128]{1,0:T(1,128)S(1)}, s32[1,128]{1,0:T(1,128)}, u32[]{:S(2)}) copy-start(s32[1,128]{1,0:T(1,128)} %param.13) | copy-start | bytes 1540
  0.7 16.2 %copy-start.4 = (s32[1,512]{1,0:T(1,128)S(1)}, s32[1,512]{1,0:T(1,128)}, u32[]{:S(2)}) copy-start(s32[1,512]{1,0:T(1,128)} %param.12) | copy-start | bytes 6148
  2.1 14.7 %collective-permute-start = (f32[2,8,128]{2,1,0:T(8,128)S(1)}, f32[2,8,128]{2,1,0:T(8,128)S(1)}, u32[]{:S(2)}, u32[]{:S(2)}) collective-permute-start(f32[2,8,128]{2,1,0:T(8,128)S(1)} %get-tuple-element.59), channel_id=1, source_target_pairs={{0,8},{8,16},{16,24},{1,9},{9,17},{17,25},{2,10},{10,18},{18,26},{... | collective-permute-start | bytes 24584 | tf_op jit(solution)/shard_map/ppermute | solution.py:14
  7.1 9.8 %collective-permute-start.1 = (f32[2,8,128]{2,1,0:T(8,128)S(1)}, f32[2,8,128]{2,1,0:T(8,128)S(1)}, u32[]{:S(2)}, u32[]{:S(2)}) collective-permute-start(f32[2,8,128]{2,1,0:T(8,128)S(1)} %get-tuple-element.60), channel_id=1, source_target_pairs={{8,0},{16,8},{24,16},{9,1},{17,9},{25,17},{10,2},{18,10},{26,18},{... | collective-permute-start | bytes 24584 | tf_op jit(solution)/shard_map/ppermute | solution.py:17
  10.1 12.0 %collective-permute-start.4 = (f32[3,1,16,8,128]{4,3,2,1,0:T(8,128)}, f32[3,1,16,8,128]{4,3,2,1,0:T(8,128)}, u32[]{:S(2)}, u32[]{:S(2)}) collective-permute-start(f32[3,1,16,8,128]{4,3,2,1,0:T(8,128)} %get-tuple-element.21), channel_id=1, source_target_pairs={{0,8},{8,16},{16,24},{1,9},{9,17},{17,25},{2,10},{10,18},{18,26},{... | collective-permute-start | bytes 589832 | tf_op jit(solution)/shard_map/ppermute | solution.py:14
  15.4 8.0 %collective-permute-start.5 = (f32[3,1,16,8,128]{4,3,2,1,0:T(8,128)}, f32[3,1,16,8,128]{4,3,2,1,0:T(8,128)}, u32[]{:S(2)}, u32[]{:S(2)}) collective-permute-start(f32[3,1,16,8,128]{4,3,2,1,0:T(8,128)} %get-tuple-element.22), channel_id=1, source_target_pairs={{8,0},{16,8},{24,16},{9,1},{17,9},{25,17},{10,2},{18,10},{26,18},{... | collective-permute-start | bytes 589832 | tf_op jit(solution)/shard_map/ppermute | solution.py:17
  17.0 2.8 %collective-permute-start.2 = (f32[2,80,8]{2,1,0:T(8,128)S(1)}, f32[2,80,8]{2,1,0:T(8,128)S(1)}, u32[]{:S(2)}, u32[]{:S(2)}) collective-permute-start(f32[2,80,8]{2,1,0:T(8,128)S(1)} %get-tuple-element.57), channel_id=1, source_target_pairs={{0,4},{1,5},{2,6},{3,7},{8,12},{9,13},{10,14},{11,15},{16,20},{17,... | collective-permute-start | bytes 15368 | tf_op jit(solution)/shard_map/ppermute | solution.py:14
  18.3 3.2 %collective-permute-start.3 = (f32[2,80,8]{2,1,0:T(8,128)S(1)}, f32[2,80,8]{2,1,0:T(8,128)S(1)}, u32[]{:S(2)}, u32[]{:S(2)}) collective-permute-start(f32[2,80,8]{2,1,0:T(8,128)S(1)} %get-tuple-element.58), channel_id=1, source_target_pairs={{4,0},{5,1},{6,2},{7,3},{12,8},{13,9},{14,10},{15,11},{20,16},{21,... | collective-permute-start | bytes 15368 | tf_op jit(solution)/shard_map/ppermute | solution.py:17
  21.8 1.6 %copy-start = (f32[1,16,64,128]{3,2,1,0:T(8,128)S(1)}, f32[1,16,64,128]{3,2,1,0:T(8,128)}, u32[]{:S(2)}) copy-start(f32[1,16,64,128]{3,2,1,0:T(8,128)} %param.9) | copy-start | bytes 1572868
  21.8 1.6 %copy-start.1 = (f32[1,16,64,128]{3,2,1,0:T(8,128)S(1)}, f32[1,16,64,128]{3,2,1,0:T(8,128)}, u32[]{:S(2)}) copy-start(f32[1,16,64,128]{3,2,1,0:T(8,128)} %param.8) | copy-start | bytes 1572868
  21.8 1.6 %copy-start.2 = (f32[1,16,64,128]{3,2,1,0:T(8,128)S(1)}, f32[1,16,64,128]{3,2,1,0:T(8,128)}, u32[]{:S(2)}) copy-start(f32[1,16,64,128]{3,2,1,0:T(8,128)} %param.7) | copy-start | bytes 1572868
  32.6 9.2 %collective-permute-start.7 = (f32[3,1,16,80,8]{3,4,2,1,0:T(8,128)}, f32[3,1,16,80,8]{3,4,2,1,0:T(8,128)}, u32[]{:S(2)}, u32[]{:S(2)}) collective-permute-start(f32[3,1,16,80,8]{3,4,2,1,0:T(8,128)} %copy.39), channel_id=1, source_target_pairs={{4,0},{5,1},{6,2},{7,3},{12,8},{13,9},{14,10},{15,11},{20,16},{21,... | collective-permute-start | bytes 368648 | tf_op jit(solution)/shard_map/ppermute | solution.py:17
  33.9 5.1 %collective-permute-start.6 = (f32[3,1,16,80,8]{3,4,2,1,0:T(8,128)}, f32[3,1,16,80,8]{3,4,2,1,0:T(8,128)}, u32[]{:S(2)}, u32[]{:S(2)}) collective-permute-start(f32[3,1,16,80,8]{3,4,2,1,0:T(8,128)} %copy.38), channel_id=1, source_target_pairs={{0,4},{1,5},{2,6},{3,7},{8,12},{9,13},{10,14},{11,15},{16,20},{17,... | collective-permute-start | bytes 368648 | tf_op jit(solution)/shard_map/ppermute | solution.py:14
  77.7 15.8 %all-to-all-start = ((f32[136,1,512]{2,1,0:T(1,128)}), f32[136,1,512]{2,1,0:T(1,128)S(1)}, u32[]{:S(2)}, u32[]{:S(2)}) async-start(f32[136,1,512]{2,1,0:T(1,128)} %copy.52), calls=%async_computation | async-start | bytes 557056 | tf_op jit(solution)/shard_map/all_to_all | solution.py:119
where the time goes:
time: 95 us; the launch traced here: 94.3 us
  other arithmetic  28.7 us (30%)
  starting transfers between devices  26.7 us (28%)
  local copies, waits for them, and re-layouts  25.8 us (27%)
  waiting for transfers between devices  11.5 us (12%)
  between operations  1.26 us (1%)
    ppermute x4, starting transfers between devices, padded(): lax.ppermute(lax.slice_in_dim(block, block.shape[dim] - width, None, axis...  15.8 us
    mul x7, other arithmetic, run_steps(): wet_mask * (pressure - stiffness * (flow_along - behind + (flow_cross - b...  10.1 us
    all_to_all x1, waiting for transfers between devices, shards(): lax.all_to_all(outgoing, ('along', 'cross'), split_axis=0, concat_axis=0,...  7.87 us
    concatenate x4, other arithmetic, padded(): block = jnp.concatenate([low, block, high], axis=dim)  6.27 us
    all_to_all x1, starting transfers between devices, shards(): lax.all_to_all(outgoing, ('along', 'cross'), split_axis=0, concat_axis=0,...  5.73 us
    slice x3, local copies, waits for them, and re-layouts, padded(): lax.slice_in_dim(block, block.shape[dim] - width, None, axis=dim)  5.34 us
    ppermute x4, starting transfers between devices, padded(): lax.ppermute(lax.slice_in_dim(block, 0, width, axis=dim), axis, backward)  5.14 us
    mul x8, other arithmetic, run_steps(): wet_mask * (flow_along - (jnp.concatenate([pressure[:, :, 1:, :], ahead_r...  4.97 us
  transfers between devices with their start and end apart: 9, of which 4 were waited for; matrix products, arithmetic and copies ran while one was open for 8% of the time, Pallas kernels for 0%

commit v1 on v0

v1 whole, which is shorter than its diff:
```python
import functools

import jax
import jax.numpy as jnp
from jax import lax
from jax.experimental import pallas as pl
from jax.experimental.pallas import tpu as pltpu
from jax.sharding import PartitionSpec as P

STEPS = 8
SUB = 8
VMEM = pltpu.VMEM


def lanes_of(shape):
    return lax.broadcasted_iota(jnp.int32, shape, len(shape) - 1)


def edges_kernel(p_ref, fa_ref, fc_ref, depth_ref, stiff_ref, w_ref, strip_ref, up_ref, down_ref):
    layers, rows, cols = p_ref.shape
    core = lax.axis_index("cross")
    width = cols // layers
    last = rows - SUB
    lane = lanes_of((rows, cols))
    row = lax.broadcasted_iota(jnp.int32, (rows, cols), 0)
    row_sub = lax.broadcasted_iota(jnp.int32, (SUB, cols), 0)
    depth = depth_ref[...]
    stiff = stiff_ref[...]
    first_lane = lane == 0
    seam_first = jnp.logical_and(first_lane, core == 0)
    group = lane // width
    group_sub = lanes_of((SUB, cols)) // width
    strip_p = strip_w = strip_s = jnp.zeros((rows, cols), jnp.float32)
    strip_v = jnp.zeros((SUB, cols), jnp.float32)
    for z in range(layers):
        wet = depth > z
        p = p_ref[z]
        va = jnp.where(wet, fa_ref[z], 0.0)
        vc = jnp.where(wet, fc_ref[z], 0.0)
        behind = jnp.where(row == 0, 0.0, pltpu.roll(va, 1, 0))
        turned = pltpu.roll(vc, 1, 1)
        w = (va - behind) + (vc - jnp.where(first_lane, 0.0, turned))
        w_ref[z] = w
        base = 2 * SUB * z
        up_ref[base : base + SUB] = p[last:]
        up_ref[base + SUB : base + 2 * SUB] = jnp.where(
            row_sub == 0, pltpu.roll(va[last:], 1, 0), w[last:]
        )
        down_ref[base : base + SUB] = p[:SUB]
        down_ref[base + SUB : base + 2 * SUB] = w[:SUB]
        shift = (width * z + width * (1 - core)) % cols
        shift_w = (width * z + (width - 1) * (1 - core)) % cols
        here = group == z
        seam_w = jnp.where(seam_first, turned, w)
        strip_p = jnp.where(here, pltpu.roll(p, shift, 1), strip_p)
        strip_w = jnp.where(here, pltpu.roll(seam_w, shift_w, 1), strip_w)
        strip_s = jnp.where(here, pltpu.roll(jnp.where(wet, stiff, 0.0), shift, 1), strip_s)
        strip_v = jnp.where(
            group_sub == z, pltpu.roll(pltpu.roll(va[last:], 1, 0), shift_w, 1), strip_v
        )
    strip_v = jnp.where(row_sub == 0, strip_v, strip_w[last:])
    strip_ref[0:rows] = strip_p
    strip_ref[rows : 2 * rows] = strip_w
    strip_ref[2 * rows : 3 * rows] = strip_s
    strip_ref[3 * rows : 3 * rows + SUB] = strip_v
    base = 2 * SUB * layers
    for ref, part in ((up_ref, slice(last, rows)), (down_ref, slice(0, SUB))):
        ref[base : base + SUB] = depth[part].astype(jnp.float32)
        ref[base + SUB : base + 2 * SUB] = stiff[part]
        ref[base + 2 * SUB : base + 3 * SUB] = strip_p[part]
        ref[base + 4 * SUB : base + 5 * SUB] = strip_s[part]
    up_ref[base + 3 * SUB : base + 4 * SUB] = strip_v
    down_ref[base + 3 * SUB : base + 4 * SUB] = strip_w[:SUB]


def steps_kernel(
    p_ref,
    w_in_ref,
    depth_ref,
    stiff_ref,
    own_up_ref,
    own_ref,
    other_ref,
    above_ref,
    below_ref,
    place_ref,
    p_out_ref,
    panel_ref,
    p_buf,
    w_buf,
    g_buf,
    d_buf,
    s_buf,
    seam_p,
    seam_w,
    seam_s,
    seam_h,
    seam_g,
    v_buf,
    trace,
):
    layers, rows, cols = p_ref.shape
    core = lax.axis_index("cross")
    width = cols // layers
    wide = rows + 2 * SUB
    blocks = wide // SUB
    lane = lanes_of((SUB, cols))
    slot = lane % width
    low = core == 0
    base = 2 * SUB * layers

    for z in range(layers):
        at = 2 * SUB * z
        p_buf[z, 0:SUB] = above_ref[at : at + SUB]
        p_buf[z, SUB : SUB + rows] = p_ref[z]
        p_buf[z, SUB + rows : wide] = below_ref[at : at + SUB]
        p_buf[z, wide : wide + SUB] = jnp.zeros((SUB, cols), jnp.float32)
        w_buf[z, 0:SUB] = above_ref[at + SUB : at + 2 * SUB]
        w_buf[z, SUB : SUB + rows] = w_in_ref[z]
        w_buf[z, SUB + rows : wide] = below_ref[at + SUB : at + 2 * SUB]
        w_buf[z, SUB : SUB + 1] = w_buf[z, SUB : SUB + 1] - above_ref[at + SUB : at + SUB + 1]
        w_buf[z, SUB + rows : SUB + rows + 1] = (
            w_buf[z, SUB + rows : SUB + rows + 1] - own_up_ref[at + SUB : at + SUB + 1]
        )
        g_buf[z, 0:SUB] = jnp.zeros((SUB, cols), jnp.float32)
    d_buf[0:SUB] = above_ref[base : base + SUB]
    d_buf[SUB : SUB + rows] = depth_ref[...].astype(jnp.float32)
    d_buf[SUB + rows : wide] = below_ref[base : base + SUB]
    s_buf[0:SUB] = above_ref[base + SUB : base + 2 * SUB]
    s_buf[SUB : SUB + rows] = stiff_ref[...]
    s_buf[SUB + rows : wide] = below_ref[base + SUB : base + 2 * SUB]

    def sides(own, other):
        return jnp.where(low, own, other), jnp.where(low, other, own)

    for buf, part in ((seam_p, 0), (seam_w, 1), (seam_s, 2)):
        own_at = base + (2 + part) * SUB
        other_at = base + (5 + part) * SUB
        top = sides(above_ref[own_at : own_at + SUB], above_ref[other_at : other_at + SUB])
        end = sides(below_ref[own_at : own_at + SUB], below_ref[other_at : other_at + SUB])
        middle = sides(
            own_ref[part * rows : (part + 1) * rows], other_ref[part * rows : (part + 1) * rows]
        )
        for side in range(2):
            buf[side, 0:SUB] = top[side]
            buf[side, SUB : SUB + rows] = middle[side]
            buf[side, SUB + rows : wide] = end[side]
    for side in range(2):
        seam_p[side, wide : wide + SUB] = jnp.zeros((SUB, cols), jnp.float32)
        seam_g[side, 0:SUB] = jnp.zeros((SUB, cols), jnp.float32)
    raw = seam_w[0]
    wide_slot = lanes_of((wide, cols)) % width
    v_buf[...] = jnp.where(wide_slot == width - 1, raw, 0.0)
    seam_w[0] = pltpu.roll(raw, 1, 1)
    wide_row = lax.broadcasted_iota(jnp.int32, (wide, cols), 0)
    seam_w[1] = seam_w[1] - jnp.where(
        jnp.logical_and(wide_slot == 0, wide_row > 0), pltpu.roll(raw, cols - width + 1, 1), 0.0
    )
    last_own = own_ref[3 * rows : 3 * rows + 1]
    last_other = other_ref[3 * rows : 3 * rows + 1]
    last_sides = sides(last_own, last_other)
    for side in range(2):
        fix_end = pltpu.roll(last_sides[0], 1, 1) if side == 0 else last_sides[1]
        seam_w[side, SUB : SUB + 1] = seam_w[side, SUB : SUB + 1] - seam_w[side, 0:1]
        seam_w[side, SUB + rows : SUB + rows + 1] = (
            seam_w[side, SUB + rows : SUB + rows + 1] - fix_end
        )
        wet = jnp.where(seam_s[side] > 0.0, 0.5, 0.0)
        deeper = pltpu.roll(wet, cols - width, 1)
        seam_h[side] = jnp.where(lanes_of((wide, cols)) < cols - width, deeper, 0.0)

    last_lane = lane == cols - 1
    first_lane = lane == 0
    last_slot = slot == width - 1
    first_slot = slot == 0
    keep = slot == jnp.where(low, width - 2, width - 1)

    def step(t, carry):
        for r in range(blocks):
            at = r * SUB
            here = slice(at, at + SUB)
            ahead = slice(at + 1, at + 1 + SUB)
            g_here = slice(at + SUB, at + 2 * SUB)
            g_behind = slice(at + SUB - 1, at + 2 * SUB - 1)
            sp = [seam_p[0, here], seam_p[1, here]]
            ss = [seam_s[0, here], seam_s[1, here]]
            wet_s = [s > 0.0 for s in ss]
            right = [
                jnp.where(last_slot, pltpu.roll(sp[1], width - 1, 1), pltpu.roll(sp[0], cols - 1, 1)),
                pltpu.roll(sp[1], cols - 1, 1),
            ]
            gy = [jnp.where(wet_s[i], right[i] - sp[i], 0.0) for i in range(2)]
            left = [
                pltpu.roll(gy[0], 1, 1),
                jnp.where(
                    first_slot, pltpu.roll(gy[0], cols - width + 1, 1), pltpu.roll(gy[1], 1, 1)
                ),
            ]
            inject = jnp.where(low, pltpu.roll(sp[1], width - 2, 1), gy[0] - v_buf[here])
            inject = jnp.where(keep, inject, 0.0)
            v_buf[here] = jnp.zeros((SUB, cols), jnp.float32)
            for i in range(2):
                gx = jnp.where(wet_s[i], seam_p[i, ahead] - sp[i], 0.0)
                seam_g[i, g_here] = gx
                w = seam_w[i, here] - ((gx - seam_g[i, g_behind]) + (gy[i] - left[i]))
                seam_w[i, here] = w
                hz = seam_h[i, here] * (pltpu.roll(sp[i], cols - width, 1) - sp[i])
                flux = w - (hz - pltpu.roll(hz, width, 1))
                seam_p[i, here] = jnp.where(wet_s[i], sp[i] - ss[i] * flux, 0.0)
            depth = d_buf[here]
            stiff = s_buf[here]
            surface = jnp.zeros((SUB, cols), jnp.float32)
            hz_before = None
            p = p_buf[0, here]
            wet = depth > 0.0
            for z in range(layers):
                gx = jnp.where(wet, p_buf[z, ahead] - p, 0.0)
                g_buf[z, g_here] = gx
                edge = pltpu.roll(inject, (cols - width + 1 - width * z) % cols, 1)
                p_right = jnp.where(last_lane, edge, pltpu.roll(p, cols - 1, 1))
                gy = jnp.where(wet, p_right - p, 0.0)
                gy_left = jnp.where(first_lane, edge, pltpu.roll(gy, 1, 1))
                w = w_buf[z, here] - ((gx - g_buf[z, g_behind]) + (gy - gy_left))
                w_buf[z, here] = w
                flux = w
                if z < layers - 1:
                    p_next = p_buf[z + 1, here]
                    wet_next = depth > float(z + 1)
                    hz = jnp.where(wet_next, 0.5 * (p_next - p), 0.0)
                    flux = w - (hz if hz_before is None else hz - hz_before)
                    hz_before = hz
                else:
                    flux = w + hz_before
                p_new = jnp.where(wet, p - stiff * flux, 0.0)
                p_buf[z, here] = p_new
                surface = jnp.where(wet, p_new, surface)
                if z < layers - 1:
                    p, wet = p_next, wet_next
            if 0 < r < blocks - 1:
                trace[t, at - SUB : at] = surface
        return carry

    lax.fori_loop(0, STEPS, step, 0)
    for z in range(layers):
        p_out_ref[z] = p_buf[z, SUB : SUB + rows]

    half = cols // 2
    lane_rows = lanes_of((rows, cols))
    place = place_ref[...]
    for j in range(STEPS // 2):
        one = trace[2 * j]
        two = trace[2 * j + 1]
        near = jnp.where(lane_rows < half, one, pltpu.roll(two, half, 1))
        far = jnp.where(lane_rows < half, pltpu.roll(one, half, 1), two)
        both = jnp.concatenate([near, far], 0)
        part_a = both.astype(jnp.bfloat16)
        rest = both - part_a.astype(jnp.float32)
        part_b = rest.astype(jnp.bfloat16)
        part_c = (rest - part_b.astype(jnp.float32)).astype(jnp.bfloat16)
        total = jnp.dot(place, part_a, preferred_element_type=jnp.float32)
        total += jnp.dot(place, part_b, preferred_element_type=jnp.float32)
        total += jnp.dot(place, part_c, preferred_element_type=jnp.float32)
        panel_ref[pl.ds(j, place.shape[0], stride=STEPS // 2)] = total


def shards(
    pressure_start, along_start, cross_start, depth_layers, stiffness, patch_lists, owner_map
):
    sensors, layers, rows, cols = pressure_start.shape
    f32 = jnp.float32
    along_count = lax.axis_size("along")
    cross_count = lax.axis_size("cross")
    forward = [(i, i + 1) for i in range(along_count - 1)]
    backward = [(target, source) for source, target in forward]
    swap = [(0, 1), (1, 0)]
    wide = rows + 2 * SUB
    strip_rows = 3 * rows + SUB
    pack_rows = 2 * SUB * layers + 5 * SUB

    spec = pl.BlockSpec(memory_space=VMEM)
    w, strips, up, down = pl.pallas_call(
        edges_kernel,
        out_shape=[
            jax.ShapeDtypeStruct((layers, rows, cols), f32),
            jax.ShapeDtypeStruct((strip_rows, cols), f32),
            jax.ShapeDtypeStruct((pack_rows, cols), f32),
            jax.ShapeDtypeStruct((pack_rows, cols), f32),
        ],
        in_specs=[spec] * 5,
        out_specs=[spec] * 4,
        name="edges",
    )(pressure_start[0], along_start[0], cross_start[0], depth_layers, stiffness)

    other = lax.ppermute(strips, "cross", swap)
    last = rows - SUB
    up_rest = jnp.concatenate(
        [other[last:rows], other[3 * rows :], other[3 * rows - SUB : 3 * rows]], 0
    )
    down_rest = jnp.concatenate(
        [other[:SUB], other[rows : rows + SUB], other[2 * rows : 2 * rows + SUB]], 0
    )
    above = lax.ppermute(jnp.concatenate([up, up_rest], 0), "along", forward)
    below = lax.ppermute(jnp.concatenate([down, down_rest], 0), "along", backward)

    patch_count = 2 * rows
    owner_count = along_count * cross_count
    capacity = patch_count // owner_count + 1
    slots = owner_count * capacity
    first_patch = (lax.axis_index("along") * cross_count + lax.axis_index("cross")) * patch_count
    positions = jnp.arange(patch_count, dtype=jnp.int32)
    member = jnp.any((patch_lists[0] - first_patch)[:, None] == positions[None, :], axis=0)
    owners = owner_map[0]
    earlier = positions[None, :] < positions[:, None]
    rank = jnp.sum(((owners[:, None] == owners[None, :]) & earlier).astype(jnp.int32), axis=1)
    target = jnp.where(member, owners * capacity + rank, -1)
    target = target.reshape(rows, 2).T.reshape(patch_count)
    place = (jnp.arange(slots, dtype=jnp.int32)[:, None] == target[None, :]).astype(jnp.bfloat16)

    parts = STEPS // 2
    pressure, panels = pl.pallas_call(
        steps_kernel,
        out_shape=[
            jax.ShapeDtypeStruct((layers, rows, cols), f32),
            jax.ShapeDtypeStruct((slots * parts, cols), f32),
        ],
        in_specs=[spec] * 10,
        out_specs=[spec] * 2,
        scratch_shapes=[
            VMEM((layers, wide + SUB, cols), f32),
            VMEM((layers, wide, cols), f32),
            VMEM((layers, wide + SUB, cols), f32),
            VMEM((wide, cols), f32),
            VMEM((wide, cols), f32),
            VMEM((2, wide + SUB, cols), f32),
            VMEM((2, wide, cols), f32),
            VMEM((2, wide, cols), f32),
            VMEM((2, wide, cols), f32),
            VMEM((2, wide + SUB, cols), f32),
            VMEM((wide, cols), f32),
            VMEM((STEPS, rows, cols), f32),
        ],
        compiler_params=pltpu.CompilerParams(vmem_limit_bytes=32 * 1024 * 1024),
        name="steps",
    )(
        pressure_start[0],
        w,
        depth_layers,
        stiffness,
        up,
        strips,
        other,
        above,
        below,
        place,
    )
    outgoing = panels.reshape(slots, 1, parts * cols)
    received = lax.all_to_all(outgoing, ("along", "cross"), split_axis=0, concat_axis=0, tiled=True)
    return (pressure[None], received[None])


def solution(mesh):
    in_specs = (
        P("batch", None, "along", "cross"),
        P("batch", None, "along", "cross"),
        P("batch", None, "along", "cross"),
        P("along", "cross"),
        P("along", "cross"),
        P("batch", None),
        P(("along", "cross"), None),
    )
    out_specs = (P("batch", None, "along", "cross"), P(("along", "cross"), None, "batch", None))
    return jax.shard_map(shards, mesh=mesh, in_specs=in_specs, out_specs=out_specs, check_vma=False)
```

time: 95 us -> 109 us (1.15)
  Pallas kernels: 0 us -> 76.1 us
  other arithmetic: 28.7 us -> 2.26 us
  local copies, waits for them, and re-layouts: 25.8 us -> 2.36 us
  starting transfers between devices: 26.7 us -> 6.59 us
  blocking collectives: 0 us -> 13.7 us
  waiting for transfers between devices: 11.5 us -> 6.72 us
    pallas_call x0 -> x2, Pallas kernels: none -> 76.1 us  [the longest x1 72.6 us: shards(): pl.pallas_call(steps_kernel, out_shape=[jax.ShapeDtypeStruct((layers, row...]
    slice x32 -> x1, local copies, waits for them, and re-layouts: 17.3 us -> 0.01 us  [shards(): other[:SUB]]
    mul x17 -> x1, other arithmetic: 15.1 us -> 0.02 us  [shards(): target = jnp.where(member, owners * capacity + rank, -1)]
    ppermute x8 -> x3, starting transfers between devices: 21 us -> 6.59 us  [the longest x1 4.84 us: shards(): above = lax.ppermute(jnp.concatenate([up, up_rest], 0), 'along', forward)]
    all_to_all x0 -> x1, blocking collectives: none -> 13.7 us  [shards(): lax.all_to_all(outgoing, ('along', 'cross'), split_axis=0, concat_axis=0,...]
    all_to_all x1 -> x0, waiting for transfers between devices: 7.87 us -> none  [shards(): lax.all_to_all(outgoing, ('along', 'cross'), split_axis=0, concat_axis=0,...]
    all_to_all x1 -> x0, starting transfers between devices: 5.73 us -> none  [shards(): lax.all_to_all(outgoing, ('along', 'cross'), split_axis=0, concat_axis=0,...]
    ppermute x2 -> x0, local copies, waits for them, and re-layouts: 5.6 us -> none  [the longest x1 2.82 us: padded(): lax.ppermute(lax.slice_in_dim(block, block.shape[dim] - width, None, axis...]
  transfers between devices with their start and end apart: 9 -> 3, of which waited for: 4 -> 3; matrix products, arithmetic and copies ran while one was open for 8% -> 2% of each run, Pallas kernels for 0% -> 0%
where the time goes in v1:
time: 109 us
  Pallas kernels  76.1 us (70%)
  blocking collectives  13.7 us (13%)
  waiting for transfers between devices  6.72 us (6%)
  starting transfers between devices  6.59 us (6%)
  local copies, waits for them, and re-layouts  2.36 us (2%)
  other arithmetic  2.26 us (2%)
    pallas_call x1, Pallas kernels, shards(): pl.pallas_call(steps_kernel, out_shape=[jax.ShapeDtypeStruct((layers, row...  72.6 us
    all_to_all x1, blocking collectives, shards(): lax.all_to_all(outgoing, ('along', 'cross'), split_axis=0, concat_axis=0,...  13.7 us
    ppermute x1, waiting for transfers between devices, shards(): lax.ppermute(jnp.concatenate([down, down_rest], 0), 'along', backward)  5.14 us
    ppermute x1, starting transfers between devices, shards(): above = lax.ppermute(jnp.concatenate([up, up_rest], 0), 'along', forward)  4.84 us
    pallas_call x1, Pallas kernels, shards(): pl.pallas_call(edges_kernel, out_shape=[jax.ShapeDtypeStruct((layers, row...  3.53 us
  transfers between devices with their start and end apart: 3, of which 3 were waited for; matrix products, arithmetic and copies ran while one was open for 2% of the time, Pallas kernels for 0%

profile of v1, /device:TPU:0, one launch (start us, length us, event | category | flops | bytes accessed | tf_op | source)
XLA Modules:
  0.0 108.6 jit_solution(6812216372133117761)
XLA Ops:
  0.6 0.0 copy-start.7
  0.6 0.0 copy-start.6
  0.7 3.5 %edges.1 = (f32[16,64,128]{2,1,0:T(8,128)}, f32[200,128]{1,0:T(8,128)}, f32[296,128]{1,0:T(8,128)}, f32[296,128]{1,0:T(8,128)}) custom-call(f32[16,64,128]{2,1,0:T(8,128)} %bitcast.10, f32[16,64,128]{2,1,0:T(8,128)} %bitcast.14, f32[16,64,128]{2,1,0:T(8,128)} %bitcast.15, s32[64,128]{1,0:T(8,128)} %depth_ref.3, f32[64,128]{1,0:T(8,128)} %stiff_ref.3), custom_call_target="tpu_custom_call" | custom-call | tf_op jit(solution)/shard_map/edges/pallas_call | solution.py:281
  4.2 0.0 copy-start
  4.2 0.5 collective-permute-start
  4.6 0.0 copy-done.7
  4.7 0.2 convert_reduce_fusion
  4.8 0.0 copy-done.6
  4.9 0.1 fusion
  5.0 0.2 reduce_or.12
  5.2 0.1 mul.20
  5.3 0.1 reduce_sum.12
  5.5 0.1 copy.13
  5.5 0.1 eq.51
  5.6 0.2 collective-permute-done.other_ref
  5.8 0.9 pad_maximum_fusion
  6.7 4.8 %collective-permute-start.1 = (f32[320,128]{1,0:T(8,128)S(1)}, f32[320,128]{1,0:T(8,128)S(1)}, u32[]{:S(2)}, u32[]{:S(2)}) collective-permute-start(f32[320,128]{1,0:T(8,128)S(1)} %pad_maximum_fusion), channel_id=1, source_target_pairs={{0,8},{8,16},{16,24},{1,9},{9,17},{17,25},{2,10},{10,18},{18,26},{... | collective-permute-start | bytes 491528 | tf_op jit(solution)/shard_map/ppermute | solution.py:302
  11.6 0.0 copy-start.1
  11.6 0.0 copy-start.4
  11.6 0.0 copy-start.5
  11.6 1.0 pad_maximum_fusion.1
  12.6 0.0 copy-start.3
  12.6 1.3 %collective-permute-start.2 = (f32[320,128]{1,0:T(8,128)S(1)}, f32[320,128]{1,0:T(8,128)S(1)}, u32[]{:S(2)}, u32[]{:S(2)}) collective-permute-start(f32[320,128]{1,0:T(8,128)S(1)} %pad_maximum_fusion.1), channel_id=1, source_target_pairs={{8,0},{16,8},{24,16},{9,1},{17,9},{25,17},{10,2},{18,10},{26,18},{... | collective-permute-start | bytes 491528 | tf_op jit(solution)/shard_map/ppermute | solution.py:303
  13.9 1.4 %collective-permute-done.1.above_ref = f32[320,128]{1,0:T(8,128)S(1)} collective-permute-done((f32[320,128]{1,0:T(8,128)S(1)}, f32[320,128]{1,0:T(8,128)S(1)}, u32[]{:S(2)}, u32[]{:S(2)}) %collective-permute-start.1) | collective-permute-done | bytes 163872 | tf_op jit(solution)/shard_map/ppermute | solution.py:302
  15.3 5.1 %collective-permute-done.2.below_ref = f32[320,128]{1,0:T(8,128)S(1)} collective-permute-done((f32[320,128]{1,0:T(8,128)S(1)}, f32[320,128]{1,0:T(8,128)S(1)}, u32[]{:S(2)}, u32[]{:S(2)}) %collective-permute-start.2) | collective-permute-done | bytes 163872 | tf_op jit(solution)/shard_map/ppermute | solution.py:303
  20.5 0.0 copy-done
  20.5 0.0 copy-done.1
  20.5 0.0 copy-done.4
  20.5 0.0 copy-done.5
  20.5 0.0 copy-done.3
  20.5 0.0 copy-start.2
  20.5 1.0 copy-done.2
  21.5 72.6 %steps.1 = (f32[16,64,128]{2,1,0:T(8,128)}, f32[544,128]{1,0:T(8,128)S(1)}) custom-call(f32[16,64,128]{2,1,0:T(8,128)S(1)} %bitcast.11, f32[16,64,128]{2,1,0:T(8,128)S(1)} %copy-done.2, s32[64,128]{1,0:T(8,128)S(1)} %copy-done.3, f32[64,128]{1,0:T(8,128)S(1)} %copy-done.4, f32[296,128]{1,0:T(8,128)S(1)} %copy-done.1, f32[200,128]{1,0:T(8,128)S(1)} %copy-done.5, ...), custom_call_target="tpu_custom_call" | custom-call | tf_op jit(solution)/shard_map/steps/pallas_call | solution.py:320
  94.1 13.7 %all_to_all.5 = f32[136,1,512]{2,1,0:T(1,128)S(1)} all-to-all(f32[136,1,512]{2,1,0:T(1,128)S(1)} %bitcast.12), channel_id=1, replica_groups=mesh['along'=4,'cross'=2,'batch'=4] {'along','cross'}, dimensions={0} | all-to-all | bytes 557056 | tf_op jit(solution)/shard_map/all_to_all | solution.py:357
  107.9 0.7 copy.16
  (5 shorter events, 0.1 us)
Async XLA Ops:
  0.6 4.0 %copy-start.7 = (s32[1,128]{1,0:T(1,128)S(1)}, s32[1,128]{1,0:T(1,128)}, u32[]{:S(2)}) copy-start(s32[1,128]{1,0:T(1,128)} %param.13) | copy-start | bytes 1540
  0.6 4.2 %copy-start.6 = (s32[1,512]{1,0:T(1,128)S(1)}, s32[1,512]{1,0:T(1,128)}, u32[]{:S(2)}) copy-start(s32[1,512]{1,0:T(1,128)} %param.12) | copy-start | bytes 6148
  4.2 16.3 %copy-start = (f32[1,16,64,128]{3,2,1,0:T(8,128)S(1)}, f32[1,16,64,128]{3,2,1,0:T(8,128)}, u32[]{:S(2)}) copy-start(f32[1,16,64,128]{3,2,1,0:T(8,128)} %param.7) | copy-start | bytes 1572868
  4.2 1.6 %collective-permute-start = (f32[200,128]{1,0:T(8,128)}, f32[200,128]{1,0:T(8,128)S(1)}, u32[]{:S(2)}, u32[]{:S(2)}) collective-permute-start(f32[200,128]{1,0:T(8,128)} %get-tuple-element.10.own_ref), channel_id=1, source_target_pairs={{0,4},{4,0},{1,5},{5,1},{2,6},{6,2},{3,7},{7,3},{8,12},{12,8},{9,1... | collective-permute-start | bytes 307208 | tf_op jit(solution)/shard_map/ppermute | solution.py:294
  6.7 8.6 %collective-permute-start.1 = (f32[320,128]{1,0:T(8,128)S(1)}, f32[320,128]{1,0:T(8,128)S(1)}, u32[]{:S(2)}, u32[]{:S(2)}) collective-permute-start(f32[320,128]{1,0:T(8,128)S(1)} %pad_maximum_fusion), channel_id=1, source_target_pairs={{0,8},{8,16},{16,24},{1,9},{9,17},{17,25},{2,10},{10,18},{18,26},{... | collective-permute-start | bytes 491528 | tf_op jit(solution)/shard_map/ppermute | solution.py:302
  11.6 8.9 %copy-start.1 = (f32[296,128]{1,0:T(8,128)S(1)}, f32[296,128]{1,0:T(8,128)}, u32[]{:S(2)}) copy-start(f32[296,128]{1,0:T(8,128)} %get-tuple-element.9.own_up_ref) | copy-start | bytes 454660
  11.6 8.9 %copy-start.4 = (f32[64,128]{1,0:T(8,128)S(1)}, f32[64,128]{1,0:T(8,128)}, u32[]{:S(2)}) copy-start(f32[64,128]{1,0:T(8,128)} %stiff_ref.3) | copy-start | bytes 98308
  11.6 8.9 %copy-start.5 = (f32[200,128]{1,0:T(8,128)S(1)}, f32[200,128]{1,0:T(8,128)}, u32[]{:S(2)}) copy-start(f32[200,128]{1,0:T(8,128)} %get-tuple-element.10.own_ref) | copy-start | bytes 307204
  12.6 7.9 %copy-start.3 = (s32[64,128]{1,0:T(8,128)S(1)}, s32[64,128]{1,0:T(8,128)}, u32[]{:S(2)}) copy-start(s32[64,128]{1,0:T(8,128)} %depth_ref.3) | copy-start | bytes 98308
  12.6 7.9 %collective-permute-start.2 = (f32[320,128]{1,0:T(8,128)S(1)}, f32[320,128]{1,0:T(8,128)S(1)}, u32[]{:S(2)}, u32[]{:S(2)}) collective-permute-start(f32[320,128]{1,0:T(8,128)S(1)} %pad_maximum_fusion.1), channel_id=1, source_target_pairs={{8,0},{16,8},{24,16},{9,1},{17,9},{25,17},{10,2},{18,10},{26,18},{... | collective-permute-start | bytes 491528 | tf_op jit(solution)/shard_map/ppermute | solution.py:303
  20.5 1.0 copy-start.2

commit v2 on v0

v2 whole, which is shorter than its diff:
```python
import jax
import jax.numpy as jnp
from jax import lax
from jax.experimental import pallas as pl
from jax.experimental.pallas import tpu as pltpu
from jax.sharding import PartitionSpec as P

STEPS = 8
SUB = 8
VMEM = pltpu.VMEM


def lanes_of(shape):
    return lax.broadcasted_iota(jnp.int32, shape, len(shape) - 1)


def rows_of(shape):
    return lax.broadcasted_iota(jnp.int32, shape, len(shape) - 2)


def edges_kernel(p_ref, fa_ref, fc_ref, depth_ref, stiff_ref, keep_ref, send_ref, one_ref, two_ref):
    layers, rows, cols = p_ref.shape
    low = lax.axis_index("cross") == 0
    span = rows // 2 + SUB
    last = rows - SUB
    lane = lanes_of((rows, cols))
    row = rows_of((rows, cols))
    row_sub = rows_of((SUB, cols))
    depth = depth_ref[...]
    stiff = stiff_ref[...]
    first_lane = lane == 0
    slot_one = row_sub == jnp.where(low, 0, -1)
    slot_two = row_sub == jnp.where(low, -1, 0)
    base = 2 * span * layers
    base_z = 2 * SUB * layers
    velocity = jnp.zeros((rows, cols), jnp.float32)

    def halves(array):
        first, second = array[:span], array[rows - span :]
        return jnp.where(low, first, second), jnp.where(low, second, first)

    def ends(array):
        first, second = array[:SUB], array[last:]
        return jnp.where(low, second, first), jnp.where(low, first, second)

    for z in range(layers):
        wet = depth > z
        p = p_ref[z]
        va = jnp.where(wet, fa_ref[z], 0.0)
        vc = jnp.where(wet, fc_ref[z], 0.0)
        behind = jnp.where(row == 0, 0.0, pltpu.roll(va, 1, 0))
        before = jnp.where(first_lane, 0.0, pltpu.roll(vc, 1, 1))
        w = (va - behind) + (vc - before)
        velocity = jnp.where(lane == z, pltpu.roll(vc, z + 1, 1), velocity)
        at = 2 * span * z
        keep_ref[at : at + span], send_ref[at : at + span] = halves(p)
        at += span
        keep_ref[at : at + span], send_ref[at : at + span] = halves(w)
        final = va[rows - 1 : rows]
        at = base + 3 * span + z
        keep_ref[at : at + 1] = final
        send_ref[at : at + 1] = final
        at = 2 * SUB * z
        one_ref[at : at + SUB], two_ref[at : at + SUB] = ends(p)
        at += SUB
        one, two = ends(w)
        final = jnp.broadcast_to(final, (SUB, cols))
        one_ref[at : at + SUB] = jnp.where(slot_one, final, one)
        two_ref[at : at + SUB] = jnp.where(slot_two, final, two)
    for i, array in enumerate((depth.astype(jnp.float32), stiff, velocity)):
        at = base + span * i
        keep_ref[at : at + span], send_ref[at : at + span] = halves(array)
        at = base_z + SUB * i
        one_ref[at : at + SUB], two_ref[at : at + SUB] = ends(array)


def steps_kernel(
    keep_ref,
    other_ref,
    one_ref,
    two_ref,
    place_ref,
    p_keep_ref,
    p_send_ref,
    panel_keep_ref,
    panel_send_ref,
    p_buf,
    w_buf,
    d_buf,
    s_buf,
    trace,
    wet_buf,
    scale_buf,
    half_buf,
    p_two,
    w_two,
):
    layers, half_rows, cols = p_keep_ref.shape
    core = lax.axis_index("cross")
    low = core == 0
    span = half_rows + SUB
    wide = span + SUB
    blocks = wide // SUB
    base = 2 * span * layers
    base_z = 2 * SUB * layers
    lane = lanes_of((SUB, cols))
    row = rows_of((SUB, cols))
    middle = pl.multiple_of(SUB * (1 - core), SUB)
    halo = pl.multiple_of(span * core, SUB)

    def left(own, other):
        return jnp.where(low, own, other)

    seam_span = left(keep_ref[base + 2 * span : base + 3 * span], other_ref[base + 2 * span : base + 3 * span])
    seam_halo = left(one_ref[base_z + 2 * SUB : base_z + 3 * SUB], two_ref[base_z + 2 * SUB : base_z + 3 * SUB])
    top_row = row == jnp.where(low, 0, -1)
    end_row = row == jnp.where(low, -1, 0)
    zeros = jnp.zeros((SUB, cols), jnp.float32)
    for tile, main_ref, halo_ref, seam_core in ((core, keep_ref, one_ref, 1), (1 - core, other_ref, two_ref, 0)):
        seam_lane = jnp.where(core == seam_core, 0, -1)
        seam = lanes_of((span, cols)) == seam_lane
        seam_sub = lane == seam_lane
        for z in range(layers):
            at = 2 * span * z
            at_z = 2 * SUB * z
            p_buf[tile, z, :SUB] = zeros
            p_two[tile, z, :SUB] = zeros
            p_two[tile, z, SUB + wide :] = zeros
            p_buf[tile, z, pl.ds(middle + SUB, span)] = main_ref[at : at + span]
            p_buf[tile, z, pl.ds(halo + SUB, SUB)] = halo_ref[at_z : at_z + SUB]
            p_buf[tile, z, SUB + wide :] = zeros
            turn = (cols - z) % cols
            w = main_ref[at + span : at + 2 * span]
            w = w - jnp.where(seam, pltpu.roll(seam_span, turn, 1) if turn else seam_span, 0.0)
            w_halo = halo_ref[at_z + SUB : at_z + 2 * SUB]
            slot = jnp.broadcast_to(w_halo[0:1], (SUB, cols))
            final = jnp.broadcast_to(main_ref[base + 3 * span + z : base + 3 * span + z + 1], (SUB, cols))
            w_halo = w_halo - jnp.where(seam_sub, pltpu.roll(seam_halo, turn, 1) if turn else seam_halo, 0.0)
            w_halo = w_halo - jnp.where(end_row, final, 0.0)
            w_top = w[:SUB] - jnp.where(top_row, slot, 0.0)
            w_buf[tile, z, pl.ds(middle, SUB)] = w_top
            w_buf[tile, z, pl.ds(middle + SUB, span - SUB)] = w[SUB:]
            w_buf[tile, z, pl.ds(halo, SUB)] = w_halo
        d_buf[tile, :SUB] = zeros
        for buf, i, shift in ((d_buf, 0, SUB), (s_buf, 1, 0)):
            buf[tile, pl.ds(middle + shift, span)] = main_ref[base + i * span : base + (i + 1) * span]
            buf[tile, pl.ds(halo + shift, SUB)] = halo_ref[base_z + i * SUB : base_z + (i + 1) * SUB]

    zs = range(layers)
    for i in range(2):
        for z in zs:
            wet = d_buf[i, SUB:] > float(z)
            if True:
                wet_buf[i, z, :SUB] = zeros
                wet_buf[i, z, SUB:] = jnp.where(wet, 1.0, 0.0)
            if True:
                scale_buf[i, z] = jnp.where(wet, s_buf[i], 0.0)
            if True and z > 0:
                half_buf[i, z - 1] = jnp.where(wet, 0.5, 0.0)
    ZB = 4
    groups = layers // ZB
    lane = lanes_of((ZB, wide, cols))
    last_lane = lane == cols - 1
    first_lane = lane == 0
    here = slice(SUB, SUB + wide)
    ahead = slice(SUB + 1, SUB + 1 + wide)
    back_rows = slice(SUB - 1, SUB - 1 + wide)

    def step(t, first, p_buf, w_buf, p_out, w_out):
        def stage_a(g):
            zs = slice(g * ZB, (g + 1) * ZB)
            return [pltpu.roll(p_buf[i, zs, here], cols - 1, 2) for i in range(2)]

        def stage_b(g, turned):
            zs = slice(g * ZB, (g + 1) * ZB)
            right = [
                jnp.where(last_lane, turned[1], turned[0]),
                jnp.where(last_lane, 0.0, turned[1]),
            ]
            gy = [wet_buf[i, zs, SUB:] * (right[i] - p_buf[i, zs, here]) for i in range(2)]
            return gy, [pltpu.roll(gy[i], 1, 2) for i in range(2)]

        hz_last = [None, None]
        surface = [None, None]

        def stage_c(g, gy, back):
            zs = slice(g * ZB, (g + 1) * ZB)
            before = [
                jnp.where(first_lane, 0.0, back[0]),
                jnp.where(first_lane, back[0], back[1]),
            ]
            for i in range(2):
                p = p_buf[i, zs, here]
                w = w_buf[i, zs] - (gy[i] - before[i])
                gx = wet_buf[i, zs, SUB:] * (p_buf[i, zs, ahead] - p)
                behind = wet_buf[i, zs, SUB - 1 : SUB - 1 + wide] * (p - p_buf[i, zs, back_rows])
                w = w - (gx - behind)
                w_out[i, zs] = w
                if g + 1 < groups:
                    hz = half_buf[i, zs] * (p_buf[i, g * ZB + 1 : (g + 1) * ZB + 1, here] - p)
                elif ZB > 1:
                    hz = jnp.concatenate([half_buf[i, g * ZB :] * (p[1:] - p[:-1]), jnp.zeros((1, wide, cols), jnp.float32)], 0)
                else:
                    hz = jnp.zeros((1, wide, cols), jnp.float32)
                prev = jnp.zeros((1, wide, cols), jnp.float32) if g == 0 else hz_last[i]
                flux = w - (hz - (jnp.concatenate([prev, hz[:-1]], 0) if ZB > 1 else prev))
                hz_last[i] = hz[-1:]
                old = wet_buf[i, zs, SUB:] * p if first else p
                new = old - scale_buf[i, zs] * flux
                p_out[i, zs, here] = new
                for k in range(ZB):
                    part = new[k, SUB:span]
                    z = g * ZB + k
                    surface[i] = part if z == 0 else jnp.where(d_buf[i, 2 * SUB : SUB + span] > float(z), part, surface[i])

        turned = [stage_a(0), stage_a(1)]
        ready = stage_b(0, turned[0])
        for g in range(groups):
            if g + 2 < groups:
                turned.append(stage_a(g + 2))
            coming = stage_b(g + 1, turned[g + 1]) if g + 1 < groups else None
            stage_c(g, *ready)
            ready = coming
        for i in range(2):
            trace[t, i] = surface[i]

    def two(k, carry):
        step(2 * k, False, p_buf, w_buf, p_two, w_two)
        step(2 * k + 1, False, p_two, w_two, p_buf, w_buf)
        return carry

    step(0, True, p_buf, w_buf, p_two, w_two)
    step(1, False, p_two, w_two, p_buf, w_buf)
    lax.fori_loop(1, STEPS // 2, two, 0)
    for z in zs:
        p_keep_ref[z] = p_buf[core, z, 2 * SUB : 2 * SUB + half_rows]
        p_send_ref[z] = p_buf[1 - core, z, 2 * SUB : 2 * SUB + half_rows]

    width = cols // 2
    lane_rows = lanes_of((half_rows, cols))
    place = place_ref[...]
    count = place.shape[0] // 2
    parts = STEPS // 2
    for j in range(parts):
        pieces = []
        for i in range(2):
            one = trace[2 * j, i]
            two = trace[2 * j + 1, i]
            pieces.append(jnp.where(lane_rows < width, one, pltpu.roll(two, width, 1)))
            pieces.append(jnp.where(lane_rows < width, pltpu.roll(one, width, 1), two))
        both = jnp.concatenate(pieces, 0)
        part_a = both.astype(jnp.bfloat16)
        rest = both - part_a.astype(jnp.float32)
        part_b = rest.astype(jnp.bfloat16)
        part_c = (rest - part_b.astype(jnp.float32)).astype(jnp.bfloat16)
        total = jnp.dot(place, part_a, preferred_element_type=jnp.float32)
        total += jnp.dot(place, part_b, preferred_element_type=jnp.float32)
        total += jnp.dot(place, part_c, preferred_element_type=jnp.float32)
        panel_keep_ref[pl.ds(j, count, stride=parts)] = total[:count]
        panel_send_ref[pl.ds(j, count, stride=parts)] = total[count:]


def shards(
    pressure_start, along_start, cross_start, depth_layers, stiffness, patch_lists, owner_map
):
    sensors, layers, rows, cols = pressure_start.shape
    f32 = jnp.float32
    along_count = lax.axis_size("along")
    cross_count = lax.axis_size("cross")
    along = lax.axis_index("along")
    cross = lax.axis_index("cross")
    low = cross == 0
    swap = [(0, 1), (1, 0)]
    pair = ("along", "cross")
    steps_up = range(along_count - 1)
    route_one = [(2 * i, 2 * i + 2) for i in steps_up] + [(2 * i + 3, 2 * i + 1) for i in steps_up]
    route_two = [(2 * i + 1, 2 * i + 2) for i in steps_up] + [(2 * i + 2, 2 * i + 1) for i in steps_up]
    half_rows = rows // 2
    span = half_rows + SUB
    wide = span + SUB
    pack_rows = 2 * span * layers + 3 * span + layers
    end_rows = 2 * SUB * layers + 3 * SUB

    spec = pl.BlockSpec(memory_space=VMEM)
    keep, send, one, two = pl.pallas_call(
        edges_kernel,
        out_shape=[
            jax.ShapeDtypeStruct((pack_rows, cols), f32),
            jax.ShapeDtypeStruct((pack_rows, cols), f32),
            jax.ShapeDtypeStruct((end_rows, cols), f32),
            jax.ShapeDtypeStruct((end_rows, cols), f32),
        ],
        in_specs=[spec] * 5,
        out_specs=[spec] * 4,
        compiler_params=pltpu.CompilerParams(vmem_limit_bytes=32 * 1024 * 1024),
        name="edges",
    )(pressure_start[0], along_start[0], cross_start[0], depth_layers, stiffness)

    other_owners = lax.ppermute(owner_map, "cross", swap)
    other = lax.ppermute(send, "cross", swap)
    near = lax.ppermute(one, pair, route_one)
    far = lax.ppermute(two, pair, route_two)

    patch_count = 2 * rows
    capacity = patch_count // (along_count * cross_count) + 1
    owners = jnp.where(low, jnp.stack([owner_map[0], other_owners[0]]), jnp.stack([other_owners[0], owner_map[0]]))
    positions = jnp.arange(patch_count, dtype=jnp.int32)
    earlier = positions[None, :] < positions[:, None]
    rank = jnp.sum(((owners[:, :, None] == owners[:, None, :]) & earlier).astype(jnp.int32), axis=2)
    local_ids = patch_lists[0] - along * cross_count * patch_count
    member = jnp.any(local_ids[:, None] == jnp.arange(2 * patch_count, dtype=jnp.int32)[None, :], axis=0)
    to_chip = owners // cross_count
    rotate = along_count <= 4
    if rotate:
        to_chip = (to_chip - along) % along_count
    block = jnp.arange(2, dtype=jnp.int32)[:, None]
    count = along_count * 2 * capacity
    target = (to_chip * 2 + block) * capacity + rank + jnp.where(owners % cross_count == cross, 0, count)
    target = jnp.where(member.reshape(2, patch_count), target, -1).reshape(2, 2, half_rows, 2)
    target = jnp.where(low, target[:, 0], target[:, 1])
    target = jnp.swapaxes(target, 1, 2).reshape(patch_count)
    place = (jnp.arange(2 * count, dtype=jnp.int32)[:, None] == target[None, :]).astype(jnp.bfloat16)

    parts = STEPS // 2
    p_keep, p_send, panel_keep, panel_send = pl.pallas_call(
        steps_kernel,
        out_shape=[
            jax.ShapeDtypeStruct((layers, half_rows, cols), f32),
            jax.ShapeDtypeStruct((layers, half_rows, cols), f32),
            jax.ShapeDtypeStruct((count * parts, cols), f32),
            jax.ShapeDtypeStruct((count * parts, cols), f32),
        ],
        in_specs=[spec] * 5,
        out_specs=[spec] * 4,
        scratch_shapes=[
            VMEM((2, layers, wide + 2 * SUB, cols), f32),
            VMEM((2, layers, wide, cols), f32),
            VMEM((2, wide + SUB, cols), f32),
            VMEM((2, wide, cols), f32),
            VMEM((STEPS, 2, half_rows, cols), f32),
            VMEM((2, layers, wide + SUB, cols), f32),
            VMEM((2, layers, wide, cols), f32),
            VMEM((2, layers - 1, wide, cols), f32),
            VMEM((2, layers, wide + 2 * SUB, cols), f32),
            VMEM((2, layers, wide, cols), f32),
        ],
        compiler_params=pltpu.CompilerParams(vmem_limit_bytes=32 * 1024 * 1024),
        name="steps",
    )(keep, other, near, far, place)

    panels = panel_keep + lax.ppermute(panel_send, "cross", swap)
    panels = panels.reshape(along_count, 2 * capacity * parts, cols)
    if rotate:
        received = [panels[0]]
        for k in range(1, along_count):
            route = [(i, (i + k) % along_count) for i in range(along_count)]
            received.append(lax.ppermute(panels[k], "along", route))
        order = (along - jnp.arange(along_count, dtype=jnp.int32)) % along_count
        received = jnp.stack(received)[order]
    else:
        received = lax.all_to_all(panels, "along", split_axis=0, concat_axis=0, tiled=True)
    received = received.reshape(1, along_count * 2 * capacity, 1, parts * cols)

    p_other = lax.ppermute(p_send, "cross", swap)
    pressure = jnp.where(
        low, jnp.concatenate([p_keep, p_other], 1), jnp.concatenate([p_other, p_keep], 1)
    )
    return (pressure[None], received)


def solution(mesh):
    in_specs = (
        P("batch", None, "along", "cross"),
        P("batch", None, "along", "cross"),
        P("batch", None, "along", "cross"),
        P("along", "cross"),
        P("along", "cross"),
        P("batch", None),
        P(("along", "cross"), None),
    )
    out_specs = (P("batch", None, "along", "cross"), P(("along", "cross"), None, "batch", None))
    return jax.shard_map(shards, mesh=mesh, in_specs=in_specs, out_specs=out_specs, check_vma=False)
```

time: 95 us -> 38.8 us (0.41)
  other arithmetic: 28.7 us -> 2.76 us
  local copies, waits for them, and re-layouts: 25.8 us -> 7.99 us
  starting transfers between devices: 26.7 us -> 13.3 us
  Pallas kernels: 0 us -> 7.09 us
  waiting for transfers between devices: 11.5 us -> 6.35 us
    slice x32 -> x1, local copies, waits for them, and re-layouts: 17.3 us -> 0.02 us  [shards(): received = [panels[0]]]
    mul x17 -> x0, other arithmetic: 15.1 us -> none  [the longest x7 10.1 us: run_steps(): wet_mask * (pressure - stiffness * (flow_along - behind + (flow_cross - b...]
    all_to_all x1 -> x0, waiting for transfers between devices: 7.87 us -> none  [shards(): lax.all_to_all(outgoing, ('along', 'cross'), split_axis=0, concat_axis=0,...]
    ppermute x8 -> x9, starting transfers between devices: 21 us -> 13.3 us  [the longest x1 4.92 us: shards(): near = lax.ppermute(one, pair, route_one)]
    pallas_call x0 -> x2, Pallas kernels: none -> 7.09 us  [the longest x1 6.71 us: shards(): pl.pallas_call(steps_kernel, out_shape=[jax.ShapeDtypeStruct((layers, hal...]
    concatenate x4 -> x0, other arithmetic: 6.27 us -> none  [padded(): block = jnp.concatenate([low, block, high], axis=dim)]
    all_to_all x1 -> x0, starting transfers between devices: 5.73 us -> none  [shards(): lax.all_to_all(outgoing, ('along', 'cross'), split_axis=0, concat_axis=0,...]
    ppermute x2 -> x0, local copies, waits for them, and re-layouts: 5.6 us -> none  [the longest x1 2.82 us: padded(): lax.ppermute(lax.slice_in_dim(block, block.shape[dim] - width, None, axis...]
  transfers between devices with their start and end apart: 9 -> 9, of which waited for: 4 -> 3; matrix products, arithmetic and copies ran while one was open for 8% -> 10% of each run, Pallas kernels for 0% -> 1%
where the time goes in v2:
time: 38.8 us; the launch traced here: 38.3 us
  starting transfers between devices  13.3 us (34%)
  local copies, waits for them, and re-layouts  7.99 us (21%)
  Pallas kernels  7.09 us (18%)
  waiting for transfers between devices  6.35 us (16%)
  other arithmetic  2.76 us (7%)
  between operations  0.82 us (2%)
    pallas_call x1, Pallas kernels, shards(): pl.pallas_call(steps_kernel, out_shape=[jax.ShapeDtypeStruct((layers, hal...  6.71 us
    unnamed x15, local copies, waits for them, and re-layouts  5.96 us
    ppermute x3, waiting for transfers between devices, shards(): received.append(lax.ppermute(panels[k], 'along', route))  5.25 us
    ppermute x1, starting transfers between devices, shards(): near = lax.ppermute(one, pair, route_one)  4.92 us
    ppermute x3, starting transfers between devices, shards(): received.append(lax.ppermute(panels[k], 'along', route))  4.02 us
    ppermute x1, starting transfers between devices, shards(): panels = panel_keep + lax.ppermute(panel_send, 'cross', swap)  2.99 us
    gather x1, local copies, waits for them, and re-layouts, shards(): received = jnp.stack(received)[order]  1.27 us
    ppermute x1, waiting for transfers between devices, shards(): panels = panel_keep + lax.ppermute(panel_send, 'cross', swap)  1.08 us
  transfers between devices with their start and end apart: 9, of which 3 were waited for; matrix products, arithmetic and copies ran while one was open for 10% of the time, Pallas kernels for 1%

profile of v2, /device:TPU:0, one launch (start us, length us, event | category | flops | bytes accessed | tf_op | source)
XLA Modules:
  0.0 38.3 jit_solution(1490616958055204605)
XLA Ops:
  0.6 0.5 %collective-permute-start.3 = (s32[1,128]{1,0:T(1,128)}, s32[1,128]{1,0:T(1,128)S(1)}, u32[]{:S(2)}, u32[]{:S(2)}) collective-permute-start(s32[1,128]{1,0:T(1,128)} %param.13), channel_id=1, source_target_pairs={{0,4},{4,0},{1,5},{5,1},{2,6},{6,2},{3,7},{7,3},{8,12},{12,8},{9,1... | collective-permute-start | bytes 1544 | tf_op jit(solution)/shard_map/ppermute | solution.py:299
  1.1 0.0 copy-start
  1.2 1.0 %copy-done = f32[1,16,64,128]{3,2,1,0:T(8,128)S(1)} copy-done((f32[1,16,64,128]{3,2,1,0:T(8,128)S(1)}, f32[1,16,64,128]{3,2,1,0:T(8,128)}, u32[]{:S(2)}) %copy-start) | copy-done | bytes 524312
  2.2 0.0 copy-start.1
  2.2 1.0 %copy-done.1 = f32[1,16,64,128]{3,2,1,0:T(8,128)S(1)} copy-done((f32[1,16,64,128]{3,2,1,0:T(8,128)S(1)}, f32[1,16,64,128]{3,2,1,0:T(8,128)}, u32[]{:S(2)}) %copy-start.1) | copy-done | bytes 524312
  3.2 0.0 copy-start.2
  3.2 1.0 %copy-done.2 = f32[1,16,64,128]{3,2,1,0:T(8,128)S(1)} copy-done((f32[1,16,64,128]{3,2,1,0:T(8,128)S(1)}, f32[1,16,64,128]{3,2,1,0:T(8,128)}, u32[]{:S(2)}) %copy-start.2) | copy-done | bytes 524312
  4.3 0.0 copy-start.3
  4.3 0.8 %copy-done.3 = s32[64,128]{1,0:T(8,128)S(1)} copy-done((s32[64,128]{1,0:T(8,128)S(1)}, s32[64,128]{1,0:T(8,128)}, u32[]{:S(2)}) %copy-start.3) | copy-done | bytes 32792
  5.0 0.0 copy-start.4
  5.0 0.8 %copy-done.4 = f32[64,128]{1,0:T(8,128)S(1)} copy-done((f32[64,128]{1,0:T(8,128)S(1)}, f32[64,128]{1,0:T(8,128)}, u32[]{:S(2)}) %copy-start.4) | copy-done | bytes 32792
  5.8 0.4 %edges.1 = (f32[1416,128]{1,0:T(8,128)S(1)}, f32[1416,128]{1,0:T(8,128)S(1)}, f32[280,128]{1,0:T(8,128)S(1)}, f32[280,128]{1,0:T(8,128)S(1)}) custom-call(f32[16,64,128]{2,1,0:T(8,128)S(1)} %bitcast.17, f32[16,64,128]{2,1,0:T(8,128)S(1)} %bitcast.18, f32[16,64,128]{2,1,0:T(8,128)S(1)} %bitcast.19, s32[64,128]{1,0:T(8,128)S(1)} %copy-done.3, ...), custom_call_target="tpu_custom_call" | custom-call | tf_op jit(solution)/shard_map/edges/pallas_call | solution.py:285
  6.2 0.1 collective-permute-start
  6.3 4.9 %collective-permute-start.1 = (f32[280,128]{1,0:T(8,128)S(1)}, f32[280,128]{1,0:T(8,128)S(1)}, u32[]{:S(2)}, u32[]{:S(2)}) collective-permute-start(f32[280,128]{1,0:T(8,128)S(1)} %get-tuple-element.12), channel_id=1, source_target_pairs={{0,8},{8,16},{16,24},{12,4},{20,12},{28,20},{1,9},{9,17},{17,25},{... | collective-permute-start | bytes 430088 | tf_op jit(solution)/shard_map/ppermute | solution.py:301
  11.2 0.7 %collective-permute-start.2 = (f32[280,128]{1,0:T(8,128)S(1)}, f32[280,128]{1,0:T(8,128)S(1)}, u32[]{:S(2)}, u32[]{:S(2)}) collective-permute-start(f32[280,128]{1,0:T(8,128)S(1)} %get-tuple-element.13), channel_id=1, source_target_pairs={{4,8},{12,16},{20,24},{8,4},{16,12},{24,20},{5,9},{13,17},{21,25},... | collective-permute-start | bytes 430088 | tf_op jit(solution)/shard_map/ppermute | solution.py:302
  11.9 0.0 copy-start.5
  12.0 0.7 %copy-done.5 = s32[1,512]{1,0:T(1,128)S(1)} copy-done((s32[1,512]{1,0:T(1,128)S(1)}, s32[1,512]{1,0:T(1,128)}, u32[]{:S(2)}) %copy-start.5) | copy-done | bytes 2072
  12.6 0.2 fusion
  12.8 0.2 reshape.212
  13.0 0.0 copy-start.6
  13.0 0.5 %broadcast.145 = s32[]{:T(128)} broadcast(s32[]{:T(128)} %constant.58.clone.1), dimensions={} | broadcast | bytes 8 | tf_op args[6]
  13.5 0.1 copy-done.6
  13.6 0.7 %reduce.6 = s32[128]{0:T(128)S(1)} reduce(s32[1,128]{1,0:T(1,128)S(1)} %copy-done.6, s32[]{:T(128)} %broadcast.145), dimensions={0}, to_apply=%param.13.reduce_sub_computation.3 | reduce | bytes 1028 | tf_op args[6]
  14.3 0.1 stack.26
  14.4 0.0 collective-permute-done.3
  14.4 0.2 convert_reduce_fusion
  14.6 0.1 reduce_sum.12
  14.8 0.7 %reduce.7 = s32[128]{0:T(128)S(1)} reduce(s32[1,128]{1,0:T(1,128)S(1)} %collective-permute-done.3, s32[]{:T(128)} %broadcast.145), dimensions={0}, to_apply=%ppermute.30.reduce_sub_computation.3 | reduce | bytes 1028 | tf_op jit(solution)/shard_map/ppermute | solution.py:299
  15.4 0.1 stack.27
  15.6 0.1 fusion.9
  15.7 0.1 copy.21
  15.8 0.1 eq.66
  15.9 0.0 collective-permute-done.1.one_ref
  15.9 0.0 collective-permute-done.2.two_ref
  16.0 0.0 collective-permute-done.other_ref
  16.0 6.7 %steps.1 = (f32[16,32,128]{2,1,0:T(8,128)S(1)}, f32[16,32,128]{2,1,0:T(8,128)S(1)}, f32[544,128]{1,0:T(8,128)S(1)}, f32[544,128]{1,0:T(8,128)S(1)}) custom-call(f32[1416,128]{1,0:T(8,128)S(1)} %get-tuple-element.10.keep_ref, f32[1416,128]{1,0:T(8,128)S(1)} %collective-permute-done.other_ref, f32[280,128]{1,0:T(8,128)S(1)} %collective-permute-done.1.one_ref, ...), custom_call_target="tpu_custom_call" | custom-call | tf_op jit(solution)/shard_map/steps/pallas_call | solution.py:325
  22.7 3.0 %collective-permute-start.5 = (f32[544,128]{1,0:T(8,128)S(1)}, f32[544,128]{1,0:T(8,128)S(1)}, u32[]{:S(2)}, u32[]{:S(2)}) collective-permute-start(f32[544,128]{1,0:T(8,128)S(1)} %get-tuple-element.17), channel_id=1, source_target_pairs={{0,4},{4,0},{1,5},{5,1},{2,6},{6,2},{3,7},{7,3},{8,12},{12,8},{9,1... | collective-permute-start | bytes 835592 | tf_op jit(solution)/shard_map/ppermute | solution.py:351
  25.7 0.1 collective-permute-start.4
  25.8 1.1 %collective-permute-done.5 = f32[544,128]{1,0:T(8,128)S(1)} collective-permute-done((f32[544,128]{1,0:T(8,128)S(1)}, f32[544,128]{1,0:T(8,128)S(1)}, u32[]{:S(2)}, u32[]{:S(2)}) %collective-permute-start.5) | collective-permute-done | bytes 278560 | tf_op jit(solution)/shard_map/ppermute | solution.py:351
  26.9 1.8 %collective-permute-start.7 = (f32[136,128]{1,0:T(8,128)S(1)}, f32[136,128]{1,0:T(8,128)S(1)}, u32[]{:S(2)}, u32[]{:S(2)}) collective-permute-start(f32[136,128]{1,0:T(8,128)S(1)} %get-tuple-element.28), channel_id=1, source_target_pairs={{0,16},{8,24},{16,0},{24,8},{1,17},{9,25},{17,1},{25,9},{2,18},{10... | collective-permute-start | bytes 208904 | tf_op jit(solution)/shard_map/ppermute | solution.py:357
  28.7 2.2 %collective-permute-start.8 = (f32[136,128]{1,0:T(8,128)S(1)}, f32[136,128]{1,0:T(8,128)S(1)}, u32[]{:S(2)}, u32[]{:S(2)}) collective-permute-start(f32[136,128]{1,0:T(8,128)S(1)} %get-tuple-element.27), channel_id=1, source_target_pairs={{0,24},{8,0},{16,8},{24,16},{1,25},{9,1},{17,9},{25,17},{2,26},{10... | collective-permute-start | bytes 208904 | tf_op jit(solution)/shard_map/ppermute | solution.py:357
  30.9 0.0 collective-permute-start.6
  30.9 0.0 collective-permute-done.4
  30.9 0.8 %maximum_select_fusion = f32[1,16,64,128]{3,2,1,0:T(8,128)} fusion(f32[1,16,32,128]{3,2,1,0:T(8,128)S(1)} %bitcast.22, f32[1,16,32,128]{3,2,1,0:T(8,128)S(1)} %bitcast.20, pred[]{:T(512)S(6)} %eq.56), kind=kLoop, calls=%fused_computation.1 | loop fusion | flops 393216 | bytes 1048577 | tf_op jit(solution)/shard_map/jit(_where)/select_n | solution.py:365
  31.8 2.6 %collective-permute-done.7 = f32[136,128]{1,0:T(8,128)S(1)} collective-permute-done((f32[136,128]{1,0:T(8,128)S(1)}, f32[136,128]{1,0:T(8,128)S(1)}, u32[]{:S(2)}, u32[]{:S(2)}) %collective-permute-start.7) | collective-permute-done | bytes 69664 | tf_op jit(solution)/shard_map/ppermute | solution.py:357
  34.4 0.0 collective-permute-done.8
  34.4 2.7 %collective-permute-done.6 = f32[136,128]{1,0:T(8,128)S(1)} collective-permute-done((f32[136,128]{1,0:T(8,128)S(1)}, f32[136,128]{1,0:T(8,128)S(1)}, u32[]{:S(2)}, u32[]{:S(2)}) %collective-permute-start.6) | collective-permute-done | bytes 69664 | tf_op jit(solution)/shard_map/ppermute | solution.py:357
  37.1 1.3 %gather_fusion = f32[4,136,128]{2,1,0:T(8,128)} fusion(f32[4,136,128]{2,1,0:T(8,128)S(1)} %pad_maximum_fusion, s32[1024]{0:T(1024)S(1)} %pad_clamp_fusion), kind=kCustom, calls=%fused_computation | custom fusion | bytes 557072 | tf_op jit(solution)/shard_map/gather | solution.py:359
  (10 shorter events, 0.2 us)
Async XLA Ops:
  0.6 13.8 %collective-permute-start.3 = (s32[1,128]{1,0:T(1,128)}, s32[1,128]{1,0:T(1,128)S(1)}, u32[]{:S(2)}, u32[]{:S(2)}) collective-permute-start(s32[1,128]{1,0:T(1,128)} %param.13), channel_id=1, source_target_pairs={{0,4},{4,0},{1,5},{5,1},{2,6},{6,2},{3,7},{7,3},{8,12},{12,8},{9,1... | collective-permute-start | bytes 1544 | tf_op jit(solution)/shard_map/ppermute | solution.py:299
  1.1 1.0 %copy-start = (f32[1,16,64,128]{3,2,1,0:T(8,128)S(1)}, f32[1,16,64,128]{3,2,1,0:T(8,128)}, u32[]{:S(2)}) copy-start(f32[1,16,64,128]{3,2,1,0:T(8,128)} %param.7) | copy-start | bytes 1572868
  2.2 1.0 %copy-start.1 = (f32[1,16,64,128]{3,2,1,0:T(8,128)S(1)}, f32[1,16,64,128]{3,2,1,0:T(8,128)}, u32[]{:S(2)}) copy-start(f32[1,16,64,128]{3,2,1,0:T(8,128)} %param.8) | copy-start | bytes 1572868
  3.2 1.0 %copy-start.2 = (f32[1,16,64,128]{3,2,1,0:T(8,128)S(1)}, f32[1,16,64,128]{3,2,1,0:T(8,128)}, u32[]{:S(2)}) copy-start(f32[1,16,64,128]{3,2,1,0:T(8,128)} %param.9) | copy-start | bytes 1572868
  4.3 0.8 %copy-start.3 = (s32[64,128]{1,0:T(8,128)S(1)}, s32[64,128]{1,0:T(8,128)}, u32[]{:S(2)}) copy-start(s32[64,128]{1,0:T(8,128)} %depth_ref.1) | copy-start | bytes 98308
  5.0 0.8 %copy-start.4 = (f32[64,128]{1,0:T(8,128)S(1)}, f32[64,128]{1,0:T(8,128)}, u32[]{:S(2)}) copy-start(f32[64,128]{1,0:T(8,128)} %stiff_ref.1) | copy-start | bytes 98308
  6.2 9.8 %collective-permute-start = (f32[1416,128]{1,0:T(8,128)S(1)}, f32[1416,128]{1,0:T(8,128)S(1)}, u32[]{:S(2)}, u32[]{:S(2)}) collective-permute-start(f32[1416,128]{1,0:T(8,128)S(1)} %get-tuple-element.11), channel_id=1, source_target_pairs={{0,4},{4,0},{1,5},{5,1},{2,6},{6,2},{3,7},{7,3},{8,12},{12,8},{9,1... | collective-permute-start | bytes 2174984 | tf_op jit(solution)/shard_map/ppermute | solution.py:300
  6.3 9.6 %collective-permute-start.1 = (f32[280,128]{1,0:T(8,128)S(1)}, f32[280,128]{1,0:T(8,128)S(1)}, u32[]{:S(2)}, u32[]{:S(2)}) collective-permute-start(f32[280,128]{1,0:T(8,128)S(1)} %get-tuple-element.12), channel_id=1, source_target_pairs={{0,8},{8,16},{16,24},{12,4},{20,12},{28,20},{1,9},{9,17},{17,25},{... | collective-permute-start | bytes 430088 | tf_op jit(solution)/shard_map/ppermute | solution.py:301
  11.2 4.7 %collective-permute-start.2 = (f32[280,128]{1,0:T(8,128)S(1)}, f32[280,128]{1,0:T(8,128)S(1)}, u32[]{:S(2)}, u32[]{:S(2)}) collective-permute-start(f32[280,128]{1,0:T(8,128)S(1)} %get-tuple-element.13), channel_id=1, source_target_pairs={{4,8},{12,16},{20,24},{8,4},{16,12},{24,20},{5,9},{13,17},{21,25},... | collective-permute-start | bytes 430088 | tf_op jit(solution)/shard_map/ppermute | solution.py:302
  11.9 0.7 %copy-start.5 = (s32[1,512]{1,0:T(1,128)S(1)}, s32[1,512]{1,0:T(1,128)}, u32[]{:S(2)}) copy-start(s32[1,512]{1,0:T(1,128)} %param.12) | copy-start | bytes 6148
  13.0 0.7 %copy-start.6 = (s32[1,128]{1,0:T(1,128)S(1)}, s32[1,128]{1,0:T(1,128)}, u32[]{:S(2)}) copy-start(s32[1,128]{1,0:T(1,128)} %param.13) | copy-start | bytes 1540
  22.7 4.2 %collective-permute-start.5 = (f32[544,128]{1,0:T(8,128)S(1)}, f32[544,128]{1,0:T(8,128)S(1)}, u32[]{:S(2)}, u32[]{:S(2)}) collective-permute-start(f32[544,128]{1,0:T(8,128)S(1)} %get-tuple-element.17), channel_id=1, source_target_pairs={{0,4},{4,0},{1,5},{5,1},{2,6},{6,2},{3,7},{7,3},{8,12},{12,8},{9,1... | collective-permute-start | bytes 835592 | tf_op jit(solution)/shard_map/ppermute | solution.py:351
  25.7 5.3 %collective-permute-start.4 = (f32[16,32,128]{2,1,0:T(8,128)S(1)}, f32[16,32,128]{2,1,0:T(8,128)S(1)}, u32[]{:S(2)}, u32[]{:S(2)}) collective-permute-start(f32[16,32,128]{2,1,0:T(8,128)S(1)} %get-tuple-element.15), channel_id=1, source_target_pairs={{0,4},{4,0},{1,5},{5,1},{2,6},{6,2},{3,7},{7,3},{8,12},{12,8},{9,1... | collective-permute-start | bytes 786440 | tf_op jit(solution)/shard_map/ppermute | solution.py:364
  26.9 7.5 %collective-permute-start.7 = (f32[136,128]{1,0:T(8,128)S(1)}, f32[136,128]{1,0:T(8,128)S(1)}, u32[]{:S(2)}, u32[]{:S(2)}) collective-permute-start(f32[136,128]{1,0:T(8,128)S(1)} %get-tuple-element.28), channel_id=1, source_target_pairs={{0,16},{8,24},{16,0},{24,8},{1,17},{9,25},{17,1},{25,9},{2,18},{10... | collective-permute-start | bytes 208904 | tf_op jit(solution)/shard_map/ppermute | solution.py:357
  28.7 5.7 %collective-permute-start.8 = (f32[136,128]{1,0:T(8,128)S(1)}, f32[136,128]{1,0:T(8,128)S(1)}, u32[]{:S(2)}, u32[]{:S(2)}) collective-permute-start(f32[136,128]{1,0:T(8,128)S(1)} %get-tuple-element.27), channel_id=1, source_target_pairs={{0,24},{8,0},{16,8},{24,16},{1,25},{9,1},{17,9},{25,17},{2,26},{10... | collective-permute-start | bytes 208904 | tf_op jit(solution)/shard_map/ppermute | solution.py:357
  30.9 6.1 %collective-permute-start.6 = (f32[136,128]{1,0:T(8,128)S(1)}, f32[136,128]{1,0:T(8,128)S(1)}, u32[]{:S(2)}, u32[]{:S(2)}) collective-permute-start(f32[136,128]{1,0:T(8,128)S(1)} %get-tuple-element.29), channel_id=1, source_target_pairs={{0,8},{8,16},{16,24},{24,0},{1,9},{9,17},{17,25},{25,1},{2,10},{10... | collective-permute-start | bytes 208904 | tf_op jit(solution)/shard_map/ppermute | solution.py:357

commit v3 on v2

--- a/solution.py
+++ b/solution.py
@@ -1,3 +1,5 @@
+import functools
+
 import jax
 import jax.numpy as jnp
 from jax import lax
@@ -18,7 +20,28 @@
     return lax.broadcasted_iota(jnp.int32, shape, len(shape) - 2)
 
 
-def edges_kernel(p_ref, fa_ref, fc_ref, depth_ref, stiff_ref, keep_ref, send_ref, one_ref, two_ref):
+def edges_kernel(
+    p_hbm, fa_hbm, fc_hbm, depth_hbm, stiff_hbm, owner_hbm,
+    keep_ref, send_ref, one_ref, two_ref,
+    p_ref, fa_ref, fc_ref, depth_ref, stiff_ref, owner_ref, sems,
+):
+    copies = [
+        pltpu.make_async_copy(source, target, sems.at[i])
+        for i, (source, target) in enumerate(
+            (
+                (depth_hbm, depth_ref),
+                (stiff_hbm, stiff_ref),
+                (owner_hbm, owner_ref),
+                (fa_hbm, fa_ref),
+                (fc_hbm, fc_ref),
+                (p_hbm, p_ref),
+            )
+        )
+    ]
+    for copy in copies:
+        copy.start()
+    for copy in copies:
+        copy.wait()
     layers, rows, cols = p_ref.shape
     low = lax.axis_index("cross") == 0
     span = rows // 2 + SUB
@@ -72,13 +95,84 @@
         keep_ref[at : at + span], send_ref[at : at + span] = halves(array)
         at = base_z + SUB * i
         one_ref[at : at + SUB], two_ref[at : at + SUB] = ends(array)
+    at = base + 3 * span + layers
+    owners = owner_ref[...].astype(jnp.float32)
+    send_ref[at : at + SUB] = jnp.broadcast_to(owners, (SUB, cols))
+
+
+def place_kernel(ids_ref, own_ref, other_ref, place_ref, *, owner_count, chips, capacity):
+    along = lax.axis_index("along")
+    cross = lax.axis_index("cross")
+    low = cross == 0
+    cores = owner_count // chips
+    patches = own_ref.shape[1]
+    last = other_ref.shape[0] - SUB
+    own = own_ref[...].astype(jnp.float32)
+    other = other_ref[last : last + 1]
+    owners = [jnp.where(low, own, other), jnp.where(low, other, own)]
+    lane = lanes_of((patches, patches))
+    half = patches // 2
+    block = lane // half
+    within = lane % half
+    patch = half * cross + 2 * (within % (half // 2)) + within // (half // 2)
+    source = rows_of((patches, patches))
+    number = rows_of((owner_count, patches)).astype(jnp.float32)
+    chosen = jnp.zeros((owner_count, patches), jnp.float32)
+    counts = jnp.zeros((owner_count, patches), jnp.float32)
+    for i in range(2):
+        held = (number == owners[i]).astype(jnp.bfloat16)
+        pick = jnp.where(block == i, jnp.where(source == patch, 1.0, 0.0), 0.0).astype(jnp.bfloat16)
+        earlier = jnp.where(block == i, jnp.where(source < patch, 1.0, 0.0), 0.0).astype(jnp.bfloat16)
+        chosen += jnp.dot(held, pick, preferred_element_type=jnp.float32)
+        counts += jnp.dot(held, earlier, preferred_element_type=jnp.float32)
+    rank = jnp.sum(chosen * counts, axis=0, keepdims=True).astype(jnp.int32)
+    owner = jnp.sum(chosen * number, axis=0, keepdims=True).astype(jnp.int32)
+    wanted = (along * cores + block) * patches + patch
+    found = jnp.zeros((patches, patches), jnp.float32)
+    for j in range(ids_ref.shape[1]):
+        found = jnp.where(ids_ref[:, j : j + 1] == wanted, 1.0, found)
+    member = jnp.sum(found, axis=0, keepdims=True)
+    block = block[:1]
+    chip = owner // cores
+    owner_core = owner % cores
+    some = 2 * capacity
+    slot = block * capacity + rank
+    if chips == 4:
+        ahead = lax.rem(chip - along + chips, chips)
+        near = lax.rem(ahead, 2) == 1
+        handler = jnp.where(near, ahead // 2, owner_core)
+        slot = slot + jnp.where(
+            near, jnp.where(owner_core == handler, 0, some), jnp.where(ahead == 2, 2 * some, 3 * some)
+        )
+    else:
+        handler = owner_core
+        slot = slot + chip * some
+    slot = jnp.where(handler == cross, slot, slot + chips * some)
+    slot = jnp.where(member > 0.0, slot, -1)
+    place_ref[...] = jnp.where(rows_of(place_ref.shape) == slot, 1.0, 0.0).astype(jnp.bfloat16)
+
+
+def gather_kernel(own_ref, near_ref, far_ref, swapped_ref, out_ref, sems):
+    chips = 4
+    along = lax.axis_index("along")
+    cross = lax.axis_index("cross")
+    count = out_ref.shape[0] // chips
+    copies = []
+    for i, (ref, ahead) in enumerate(
+        ((own_ref, 0), (near_ref, 3 - 2 * cross), (far_ref, 2), (swapped_ref, 1 + 2 * cross))
+    ):
+        at = pl.multiple_of(lax.rem(along + ahead, chips) * count, SUB)
+        copies.append(pltpu.make_async_copy(ref, out_ref.at[pl.ds(at, count)], sems.at[i]))
+    for copy in copies:
+        copy.start()
+    for copy in copies:
+        copy.wait()
 
 
 def steps_kernel(
     keep_ref,
     other_ref,
-    one_ref,
-    two_ref,
+    halo_ref,
     place_ref,
     p_keep_ref,
     p_send_ref,
@@ -103,6 +197,9 @@
     blocks = wide // SUB
     base = 2 * span * layers
     base_z = 2 * SUB * layers
+    ends = halo_ref.shape[0] // 2
+    one_ref = halo_ref.at[:ends]
+    two_ref = halo_ref.at[ends:]
     lane = lanes_of((SUB, cols))
     row = rows_of((SUB, cols))
     middle = pl.multiple_of(SUB * (1 - core), SUB)
@@ -116,7 +213,7 @@
     top_row = row == jnp.where(low, 0, -1)
     end_row = row == jnp.where(low, -1, 0)
     zeros = jnp.zeros((SUB, cols), jnp.float32)
-    for tile, main_ref, halo_ref, seam_core in ((core, keep_ref, one_ref, 1), (1 - core, other_ref, two_ref, 0)):
+    for tile, main_ref, end_ref, seam_core in ((core, keep_ref, one_ref, 1), (1 - core, other_ref, two_ref, 0)):
         seam_lane = jnp.where(core == seam_core, 0, -1)
         seam = lanes_of((span, cols)) == seam_lane
         seam_sub = lane == seam_lane
@@ -127,12 +224,12 @@
             p_two[tile, z, :SUB] = zeros
             p_two[tile, z, SUB + wide :] = zeros
             p_buf[tile, z, pl.ds(middle + SUB, span)] = main_ref[at : at + span]
-            p_buf[tile, z, pl.ds(halo + SUB, SUB)] = halo_ref[at_z : at_z + SUB]
+            p_buf[tile, z, pl.ds(halo + SUB, SUB)] = end_ref[at_z : at_z + SUB]
             p_buf[tile, z, SUB + wide :] = zeros
             turn = (cols - z) % cols
             w = main_ref[at + span : at + 2 * span]
             w = w - jnp.where(seam, pltpu.roll(seam_span, turn, 1) if turn else seam_span, 0.0)
-            w_halo = halo_ref[at_z + SUB : at_z + 2 * SUB]
+            w_halo = end_ref[at_z + SUB : at_z + 2 * SUB]
             slot = jnp.broadcast_to(w_halo[0:1], (SUB, cols))
             final = jnp.broadcast_to(main_ref[base + 3 * span + z : base + 3 * span + z + 1], (SUB, cols))
             w_halo = w_halo - jnp.where(seam_sub, pltpu.roll(seam_halo, turn, 1) if turn else seam_halo, 0.0)
@@ -144,7 +241,7 @@
         d_buf[tile, :SUB] = zeros
         for buf, i, shift in ((d_buf, 0, SUB), (s_buf, 1, 0)):
             buf[tile, pl.ds(middle + shift, span)] = main_ref[base + i * span : base + (i + 1) * span]
-            buf[tile, pl.ds(halo + shift, SUB)] = halo_ref[base_z + i * SUB : base_z + (i + 1) * SUB]
+            buf[tile, pl.ds(halo + shift, SUB)] = end_ref[base_z + i * SUB : base_z + (i + 1) * SUB]
 
     zs = range(layers)
     for i in range(2):
@@ -267,14 +364,11 @@
     f32 = jnp.float32
     along_count = lax.axis_size("along")
     cross_count = lax.axis_size("cross")
-    along = lax.axis_index("along")
-    cross = lax.axis_index("cross")
-    low = cross == 0
+    low = lax.axis_index("cross") == 0
     swap = [(0, 1), (1, 0)]
     pair = ("along", "cross")
     steps_up = range(along_count - 1)
-    route_one = [(2 * i, 2 * i + 2) for i in steps_up] + [(2 * i + 3, 2 * i + 1) for i in steps_up]
-    route_two = [(2 * i + 1, 2 * i + 2) for i in steps_up] + [(2 * i + 2, 2 * i + 1) for i in steps_up]
+    route = [(2 * i, 2 * i + 2) for i in steps_up] + [(2 * i + 3, 2 * i + 1) for i in steps_up]
     half_rows = rows // 2
     span = half_rows + SUB
     wide = span + SUB
@@ -282,44 +376,49 @@
     end_rows = 2 * SUB * layers + 3 * SUB
 
     spec = pl.BlockSpec(memory_space=VMEM)
+    hbm = pl.BlockSpec(memory_space=pltpu.HBM)
+    params = pltpu.CompilerParams(vmem_limit_bytes=32 * 1024 * 1024)
     keep, send, one, two = pl.pallas_call(
         edges_kernel,
         out_shape=[
             jax.ShapeDtypeStruct((pack_rows, cols), f32),
-            jax.ShapeDtypeStruct((pack_rows, cols), f32),
+            jax.ShapeDtypeStruct((pack_rows + SUB, cols), f32),
             jax.ShapeDtypeStruct((end_rows, cols), f32),
             jax.ShapeDtypeStruct((end_rows, cols), f32),
         ],
-        in_specs=[spec] * 5,
+        in_specs=[hbm] * 6,
         out_specs=[spec] * 4,
-        compiler_params=pltpu.CompilerParams(vmem_limit_bytes=32 * 1024 * 1024),
+        scratch_shapes=[
+            VMEM((layers, rows, cols), f32),
+            VMEM((layers, rows, cols), f32),
+            VMEM((layers, rows, cols), f32),
+            VMEM((rows, cols), jnp.int32),
+            VMEM((rows, cols), f32),
+            VMEM(owner_map.shape, jnp.int32),
+            pltpu.SemaphoreType.DMA((6,)),
+        ],
+        compiler_params=params,
         name="edges",
-    )(pressure_start[0], along_start[0], cross_start[0], depth_layers, stiffness)
-
-    other_owners = lax.ppermute(owner_map, "cross", swap)
+    )(pressure_start[0], along_start[0], cross_start[0], depth_layers, stiffness, owner_map)
+
+    halo = jnp.concatenate([one, lax.ppermute(two, "cross", swap)], 0)
     other = lax.ppermute(send, "cross", swap)
-    near = lax.ppermute(one, pair, route_one)
-    far = lax.ppermute(two, pair, route_two)
+    halo = lax.ppermute(halo, pair, route)
 
     patch_count = 2 * rows
-    capacity = patch_count // (along_count * cross_count) + 1
-    owners = jnp.where(low, jnp.stack([owner_map[0], other_owners[0]]), jnp.stack([other_owners[0], owner_map[0]]))
-    positions = jnp.arange(patch_count, dtype=jnp.int32)
-    earlier = positions[None, :] < positions[:, None]
-    rank = jnp.sum(((owners[:, :, None] == owners[:, None, :]) & earlier).astype(jnp.int32), axis=2)
-    local_ids = patch_lists[0] - along * cross_count * patch_count
-    member = jnp.any(local_ids[:, None] == jnp.arange(2 * patch_count, dtype=jnp.int32)[None, :], axis=0)
-    to_chip = owners // cross_count
-    rotate = along_count <= 4
-    if rotate:
-        to_chip = (to_chip - along) % along_count
-    block = jnp.arange(2, dtype=jnp.int32)[:, None]
-    count = along_count * 2 * capacity
-    target = (to_chip * 2 + block) * capacity + rank + jnp.where(owners % cross_count == cross, 0, count)
-    target = jnp.where(member.reshape(2, patch_count), target, -1).reshape(2, 2, half_rows, 2)
-    target = jnp.where(low, target[:, 0], target[:, 1])
-    target = jnp.swapaxes(target, 1, 2).reshape(patch_count)
-    place = (jnp.arange(2 * count, dtype=jnp.int32)[:, None] == target[None, :]).astype(jnp.bfloat16)
+    owner_count = along_count * cross_count
+    capacity = patch_count // owner_count + 1
+    count = owner_count * capacity
+    place = pl.pallas_call(
+        functools.partial(
+            place_kernel, owner_count=owner_count, chips=along_count, capacity=capacity
+        ),
+        out_shape=jax.ShapeDtypeStruct((2 * count, patch_count), jnp.bfloat16),
+        in_specs=[spec] * 3,
+        out_specs=spec,
+        compiler_params=params,
+        name="place",
+    )(patch_lists.reshape(-1, patch_count).T, owner_map, other)
 
     parts = STEPS // 2
     p_keep, p_send, panel_keep, panel_send = pl.pallas_call(
@@ -330,7 +429,7 @@
             jax.ShapeDtypeStruct((count * parts, cols), f32),
             jax.ShapeDtypeStruct((count * parts, cols), f32),
         ],
-        in_specs=[spec] * 5,
+        in_specs=[spec] * 4,
         out_specs=[spec] * 4,
         scratch_shapes=[
             VMEM((2, layers, wide + 2 * SUB, cols), f32),
@@ -344,22 +443,34 @@
             VMEM((2, layers, wide + 2 * SUB, cols), f32),
             VMEM((2, layers, wide, cols), f32),
         ],
-        compiler_params=pltpu.CompilerParams(vmem_limit_bytes=32 * 1024 * 1024),
+        compiler_params=params,
         name="steps",
-    )(keep, other, near, far, place)
+    )(keep, other, halo, place)
 
     panels = panel_keep + lax.ppermute(panel_send, "cross", swap)
-    panels = panels.reshape(along_count, 2 * capacity * parts, cols)
-    if rotate:
-        received = [panels[0]]
-        for k in range(1, along_count):
-            route = [(i, (i + k) % along_count) for i in range(along_count)]
-            received.append(lax.ppermute(panels[k], "along", route))
-        order = (along - jnp.arange(along_count, dtype=jnp.int32)) % along_count
-        received = jnp.stack(received)[order]
+    if along_count == 4:
+        some = 2 * capacity * parts
+        ring = range(along_count)
+        near_route = [(2 * i, 2 * ((i + 1) % along_count)) for i in ring]
+        near_route += [(2 * ((i + 1) % along_count) + 1, 2 * i + 1) for i in ring]
+        near = lax.ppermute(panels[: 2 * some], pair, near_route)
+        far = lax.ppermute(
+            panels[2 * some : 3 * some], "along", [(i, (i + 2) % along_count) for i in ring]
+        )
+        swapped = lax.ppermute(near[some:], "cross", swap)
+        received = pl.pallas_call(
+            gather_kernel,
+            out_shape=jax.ShapeDtypeStruct((count * parts, cols), f32),
+            in_specs=[spec] * 4,
+            out_specs=hbm,
+            scratch_shapes=[pltpu.SemaphoreType.DMA((4,))],
+            compiler_params=params,
+            name="gather",
+        )(panels[3 * some :], near[:some], far, swapped)
     else:
+        panels = panels.reshape(along_count, 2 * capacity * parts, cols)
         received = lax.all_to_all(panels, "along", split_axis=0, concat_axis=0, tiled=True)
-    received = received.reshape(1, along_count * 2 * capacity, 1, parts * cols)
+    received = received.reshape(1, count, 1, parts * cols)
 
     p_other = lax.ppermute(p_send, "cross", swap)
     pressure = jnp.where(

time: 38.8 us -> 38.3 us (0.987)
  waiting for transfers between devices: 6.35 us -> 11.2 us
  local copies, waits for them, and re-layouts: 7.99 us -> 5.43 us
  starting transfers between devices: 13.3 us -> 11.3 us
  other arithmetic: 2.76 us -> 0.9 us
  Pallas kernels: 7.09 us -> 8.28 us
    ppermute x6 -> x5, waiting for transfers between devices: 5.26 us -> 10.2 us  [the longest x1 3.8 us: shards(): near = lax.ppermute(panels[:2 * some], pair, near_route)]
    ppermute x1, starting transfers between devices: 2.99 us -> 0.07 us  [shards(): panels = panel_keep + lax.ppermute(panel_send, 'cross', swap)]
    gather x1 -> x0, local copies, waits for them, and re-layouts: 1.27 us -> none  [shards(): received = jnp.stack(received)[order]]
    pallas_call x0 -> x2, Pallas kernels: none -> 0.95 us  [the longest x1 0.73 us: shards(): pl.pallas_call(gather_kernel, out_shape=jax.ShapeDtypeStruct((count * par...]
    unnamed x15 -> x14, local copies, waits for them, and re-layouts: 5.96 us -> 5.29 us
    ppermute x1 -> x0, other arithmetic: 0.67 us -> none  [shards(): other_owners = lax.ppermute(owner_map, 'cross', swap)]
    unnamed x1 -> x0, other arithmetic: 0.66 us -> none
    ppermute x1, starting transfers between devices: 0.08 us -> 0.49 us  [shards(): p_other = lax.ppermute(p_send, 'cross', swap)]
  transfers between devices with their start and end apart: 9 -> 8, of which waited for: 3 -> 5; matrix products, arithmetic and copies ran while one was open for 10% -> 3% of each run, Pallas kernels for 1% -> 1%
where the time goes in v3:
time: 38.3 us; the launch traced here: 37.8 us
  starting transfers between devices  11.3 us (30%)
  waiting for transfers between devices  11.2 us (29%)
  Pallas kernels  8.28 us (22%)
  local copies, waits for them, and re-layouts  5.43 us (14%)
  other arithmetic  0.9 us (2%)
  between operations  0.74 us (2%)
    pallas_call x1, Pallas kernels, shards(): pl.pallas_call(steps_kernel, out_shape=[jax.ShapeDtypeStruct((layers, hal...  6.71 us
    unnamed x14, local copies, waits for them, and re-layouts  5.29 us
    ppermute x1, starting transfers between devices, shards(): halo = lax.ppermute(halo, pair, route)  4.87 us
    ppermute x1, waiting for transfers between devices, shards(): near = lax.ppermute(panels[:2 * some], pair, near_route)  3.8 us
    ppermute x1, waiting for transfers between devices, shards(): halo = lax.ppermute(halo, pair, route)  3.77 us
    ppermute x1, starting transfers between devices, shards(): lax.ppermute(panels[2 * some:3 * some], 'along', [(i, (i + 2) % along_cou...  2.65 us
    ppermute x1, starting transfers between devices, shards(): near = lax.ppermute(panels[:2 * some], pair, near_route)  2.54 us
    ppermute x1, waiting for transfers between devices, shards(): halo = jnp.concatenate([one, lax.ppermute(two, 'cross', swap)], 0)  1.96 us
  transfers between devices with their start and end apart: 8, of which 5 were waited for; matrix products, arithmetic and copies ran while one was open for 3% of the time, Pallas kernels for 1%

profile of v3, /device:TPU:0, one launch (start us, length us, event | category | flops | bytes accessed | tf_op | source)
XLA Modules:
  0.0 37.8 jit_solution(18150408655897975652)
XLA Ops:
  0.6 0.0 copy-start.5
  0.6 0.6 %copy-done.5 = s32[1,128]{1,0:T(1,128)S(1)} copy-done((s32[1,128]{1,0:T(1,128)S(1)}, s32[1,128]{1,0:T(1,128)}, u32[]{:S(2)}) %copy-start.5) | copy-done | bytes 536
  1.3 0.0 copy-start
  1.3 1.0 %copy-done = f32[1,16,64,128]{3,2,1,0:T(8,128)S(1)} copy-done((f32[1,16,64,128]{3,2,1,0:T(8,128)S(1)}, f32[1,16,64,128]{3,2,1,0:T(8,128)}, u32[]{:S(2)}) %copy-start) | copy-done | bytes 524312
  2.3 0.0 copy-start.1
  2.3 1.0 %copy-done.1 = f32[1,16,64,128]{3,2,1,0:T(8,128)S(1)} copy-done((f32[1,16,64,128]{3,2,1,0:T(8,128)S(1)}, f32[1,16,64,128]{3,2,1,0:T(8,128)}, u32[]{:S(2)}) %copy-start.1) | copy-done | bytes 524312
  3.4 0.0 copy-start.2
  3.4 1.0 %copy-done.2 = f32[1,16,64,128]{3,2,1,0:T(8,128)S(1)} copy-done((f32[1,16,64,128]{3,2,1,0:T(8,128)S(1)}, f32[1,16,64,128]{3,2,1,0:T(8,128)}, u32[]{:S(2)}) %copy-start.2) | copy-done | bytes 524312
  4.4 0.0 copy-start.3
  4.4 0.8 %copy-done.3 = s32[64,128]{1,0:T(8,128)S(1)} copy-done((s32[64,128]{1,0:T(8,128)S(1)}, s32[64,128]{1,0:T(8,128)}, u32[]{:S(2)}) %copy-start.3) | copy-done | bytes 32792
  5.2 0.0 copy-start.4
  5.2 0.8 %copy-done.4 = f32[64,128]{1,0:T(8,128)S(1)} copy-done((f32[64,128]{1,0:T(8,128)S(1)}, f32[64,128]{1,0:T(8,128)}, u32[]{:S(2)}) %copy-start.4) | copy-done | bytes 32792
  5.9 0.6 %edges.1 = (f32[1416,128]{1,0:T(8,128)S(1)}, f32[1424,128]{1,0:T(8,128)S(1)}, f32[280,128]{1,0:T(8,128)S(1)}, f32[280,128]{1,0:T(8,128)S(1)}) custom-call(f32[16,64,128]{2,1,0:T(8,128)S(1)} %bitcast.8, f32[16,64,128]{2,1,0:T(8,128)S(1)} %bitcast.9, f32[16,64,128]{2,1,0:T(8,128)S(1)} %bitcast.10, s32[64,128]{1,0:T(8,128)S(1)} %copy-done.3, ...), custom_call_target="tpu_custom_call" | custom-call | tf_op jit(solution)/shard_map/edges/pallas_call | solution.py:381
  6.6 0.5 %collective-permute-start = (f32[1424,128]{1,0:T(8,128)S(1)}, f32[1424,128]{1,0:T(8,128)S(1)}, u32[]{:S(2)}, u32[]{:S(2)}) collective-permute-start(f32[1424,128]{1,0:T(8,128)S(1)} %get-tuple-element.11), channel_id=1, source_target_pairs={{0,4},{4,0},{1,5},{5,1},{2,6},{6,2},{3,7},{7,3},{8,12},{12,8},{9,1... | collective-permute-start | bytes 2187272 | tf_op jit(solution)/shard_map/ppermute | solution.py:405
  7.1 0.1 collective-permute-start.1
  7.2 2.0 %collective-permute-done.1 = f32[280,128]{1,0:T(8,128)S(1)} collective-permute-done((f32[280,128]{1,0:T(8,128)S(1)}, f32[280,128]{1,0:T(8,128)S(1)}, u32[]{:S(2)}, u32[]{:S(2)}) %collective-permute-start.1) | collective-permute-done | bytes 143392 | tf_op jit(solution)/shard_map/ppermute | solution.py:404
  9.1 0.0 copy-start.6
  9.1 4.9 %collective-permute-start.2 = (f32[560,128]{1,0:T(8,128)S(1)}, f32[560,128]{1,0:T(8,128)S(1)}, u32[]{:S(2)}, u32[]{:S(2)}) collective-permute-start(f32[560,128]{1,0:T(8,128)S(1)} %pad_maximum_fusion), channel_id=1, source_target_pairs={{0,8},{8,16},{16,24},{12,4},{20,12},{28,20},{1,9},{9,17},{17,25},{... | collective-permute-start | bytes 860168 | tf_op jit(solution)/shard_map/ppermute | solution.py:406
  14.0 0.0 copy-done.6
  14.0 0.1 copy.10
  14.1 0.0 collective-permute-done.other_ref
  14.1 0.2 place.1.place_ref
  14.4 3.8 %collective-permute-done.2.halo_ref = f32[560,128]{1,0:T(8,128)S(1)} collective-permute-done((f32[560,128]{1,0:T(8,128)S(1)}, f32[560,128]{1,0:T(8,128)S(1)}, u32[]{:S(2)}, u32[]{:S(2)}) %collective-permute-start.2) | collective-permute-done | bytes 286752 | tf_op jit(solution)/shard_map/ppermute | solution.py:406
  18.1 6.7 %steps.1 = (f32[16,32,128]{2,1,0:T(8,128)S(1)}, f32[16,32,128]{2,1,0:T(8,128)S(1)}, f32[544,128]{1,0:T(8,128)S(1)}, f32[544,128]{1,0:T(8,128)S(1)}) custom-call(f32[1416,128]{1,0:T(8,128)S(1)} %get-tuple-element.10.keep_ref, f32[1424,128]{1,0:T(8,128)S(1)} %collective-permute-done.other_ref, f32[560,128]{1,0:T(8,128)S(1)} %collective-permute-done.2.halo_ref, ...), custom_call_target="tpu_custom_call" | custom-call | tf_op jit(solution)/shard_map/steps/pallas_call | solution.py:424
  24.9 0.1 collective-permute-start.4
  24.9 0.5 %collective-permute-start.3 = (f32[16,32,128]{2,1,0:T(8,128)S(1)}, f32[16,32,128]{2,1,0:T(8,128)S(1)}, u32[]{:S(2)}, u32[]{:S(2)}) collective-permute-start(f32[16,32,128]{2,1,0:T(8,128)S(1)} %get-tuple-element.15), channel_id=1, source_target_pairs={{0,4},{4,0},{1,5},{5,1},{2,6},{6,2},{3,7},{7,3},{8,12},{12,8},{9,1... | collective-permute-start | bytes 786440 | tf_op jit(solution)/shard_map/ppermute | solution.py:475
  25.4 1.0 %collective-permute-done.4 = f32[544,128]{1,0:T(8,128)S(1)} collective-permute-done((f32[544,128]{1,0:T(8,128)S(1)}, f32[544,128]{1,0:T(8,128)S(1)}, u32[]{:S(2)}, u32[]{:S(2)}) %collective-permute-start.4) | collective-permute-done | bytes 278560 | tf_op jit(solution)/shard_map/ppermute | solution.py:450
  26.5 2.5 %collective-permute-start.5 = (f32[272,128]{1,0:T(8,128)S(1)}, f32[272,128]{1,0:T(8,128)S(1)}, u32[]{:S(2)}, u32[]{:S(2)}) collective-permute-start(f32[272,128]{1,0:T(8,128)S(1)} %slice.21), channel_id=1, source_target_pairs={{0,8},{8,16},{16,24},{24,0},{12,4},{20,12},{28,20},{4,28},{1,9},{9... | collective-permute-start | bytes 417800 | tf_op jit(solution)/shard_map/ppermute | solution.py:456
  29.1 2.7 %collective-permute-start.6 = (f32[136,128]{1,0:T(8,128)S(1)}, f32[136,128]{1,0:T(8,128)S(1)}, u32[]{:S(2)}, u32[]{:S(2)}) collective-permute-start(f32[136,128]{1,0:T(8,128)S(1)} %get-tuple-element.22), channel_id=1, source_target_pairs={{0,16},{8,24},{16,0},{24,8},{1,17},{9,25},{17,1},{25,9},{2,18},{10... | collective-permute-start | bytes 208904 | tf_op jit(solution)/shard_map/ppermute | solution.py:457
  31.7 3.8 %collective-permute-done.5 = f32[272,128]{1,0:T(8,128)S(1)} collective-permute-done((f32[272,128]{1,0:T(8,128)S(1)}, f32[272,128]{1,0:T(8,128)S(1)}, u32[]{:S(2)}, u32[]{:S(2)}) %collective-permute-start.5) | collective-permute-done | bytes 139296 | tf_op jit(solution)/shard_map/ppermute | solution.py:456
  35.5 0.1 collective-permute-start.7
  35.6 0.0 collective-permute-done.3
  35.6 0.9 %maximum_select_fusion = f32[1,16,64,128]{3,2,1,0:T(8,128)} fusion(f32[1,16,32,128]{3,2,1,0:T(8,128)S(1)} %bitcast.14, f32[1,16,32,128]{3,2,1,0:T(8,128)S(1)} %bitcast.12, pred[]{:T(512)S(6)} %eq.3), kind=kLoop, calls=%fused_computation | loop fusion | flops 393216 | bytes 1048577 | tf_op jit(solution)/shard_map/jit(_where)/select_n | solution.py:476
  36.5 0.6 %collective-permute-done.6.far_ref = f32[136,128]{1,0:T(8,128)S(1)} collective-permute-done((f32[136,128]{1,0:T(8,128)S(1)}, f32[136,128]{1,0:T(8,128)S(1)}, u32[]{:S(2)}, u32[]{:S(2)}) %collective-permute-start.6) | collective-permute-done | bytes 69664 | tf_op jit(solution)/shard_map/ppermute | solution.py:457
  37.1 0.0 collective-permute-done.7.swapped_ref
  37.1 0.7 %gather.1 = f32[544,128]{1,0:T(8,128)} custom-call(f32[136,128]{1,0:T(8,128)S(1)} %get-tuple-element.23.own_ref, f32[136,128]{1,0:T(8,128)S(1)} %get-tuple-element.25.near_ref, f32[136,128]{1,0:T(8,128)S(1)} %collective-permute-done.6.far_ref, f32[136,128]{1,0:T(8,128)S(1)} %collective-permute-done.7.swapped_ref), custom_call_target="tpu_custom_call" | custom-call | tf_op jit(solution)/shard_map/gather/pallas_call | solution.py:461
  (5 shorter events, 0.1 us)
Async XLA Ops:
  0.6 0.7 %copy-start.5 = (s32[1,128]{1,0:T(1,128)S(1)}, s32[1,128]{1,0:T(1,128)}, u32[]{:S(2)}) copy-start(s32[1,128]{1,0:T(1,128)} %own_ref.1) | copy-start | bytes 1540
  1.3 1.0 %copy-start = (f32[1,16,64,128]{3,2,1,0:T(8,128)S(1)}, f32[1,16,64,128]{3,2,1,0:T(8,128)}, u32[]{:S(2)}) copy-start(f32[1,16,64,128]{3,2,1,0:T(8,128)} %param.7) | copy-start | bytes 1572868
  2.3 1.0 %copy-start.1 = (f32[1,16,64,128]{3,2,1,0:T(8,128)S(1)}, f32[1,16,64,128]{3,2,1,0:T(8,128)}, u32[]{:S(2)}) copy-start(f32[1,16,64,128]{3,2,1,0:T(8,128)} %param.8) | copy-start | bytes 1572868
  3.4 1.0 %copy-start.2 = (f32[1,16,64,128]{3,2,1,0:T(8,128)S(1)}, f32[1,16,64,128]{3,2,1,0:T(8,128)}, u32[]{:S(2)}) copy-start(f32[1,16,64,128]{3,2,1,0:T(8,128)} %param.9) | copy-start | bytes 1572868
  4.4 0.8 %copy-start.3 = (s32[64,128]{1,0:T(8,128)S(1)}, s32[64,128]{1,0:T(8,128)}, u32[]{:S(2)}) copy-start(s32[64,128]{1,0:T(8,128)} %depth_hbm.1) | copy-start | bytes 98308
  5.2 0.8 %copy-start.4 = (f32[64,128]{1,0:T(8,128)S(1)}, f32[64,128]{1,0:T(8,128)}, u32[]{:S(2)}) copy-start(f32[64,128]{1,0:T(8,128)} %stiff_hbm.1) | copy-start | bytes 98308
  6.6 7.6 %collective-permute-start = (f32[1424,128]{1,0:T(8,128)S(1)}, f32[1424,128]{1,0:T(8,128)S(1)}, u32[]{:S(2)}, u32[]{:S(2)}) collective-permute-start(f32[1424,128]{1,0:T(8,128)S(1)} %get-tuple-element.11), channel_id=1, source_target_pairs={{0,4},{4,0},{1,5},{5,1},{2,6},{6,2},{3,7},{7,3},{8,12},{12,8},{9,1... | collective-permute-start | bytes 2187272 | tf_op jit(solution)/shard_map/ppermute | solution.py:405
  7.1 2.0 %collective-permute-start.1 = (f32[280,128]{1,0:T(8,128)S(1)}, f32[280,128]{1,0:T(8,128)S(1)}, u32[]{:S(2)}, u32[]{:S(2)}) collective-permute-start(f32[280,128]{1,0:T(8,128)S(1)} %get-tuple-element.13), channel_id=1, source_target_pairs={{0,4},{4,0},{1,5},{5,1},{2,6},{6,2},{3,7},{7,3},{8,12},{12,8},{9,1... | collective-permute-start | bytes 430088 | tf_op jit(solution)/shard_map/ppermute | solution.py:404
  9.1 4.9 %copy-start.6 = (s32[1,512]{1,0:T(1,128)S(1)}, s32[1,512]{1,0:T(1,128)}, u32[]{:S(2)}) copy-start(s32[1,512]{1,0:T(1,128)} %param.12) | copy-start | bytes 6148
  9.1 9.0 %collective-permute-start.2 = (f32[560,128]{1,0:T(8,128)S(1)}, f32[560,128]{1,0:T(8,128)S(1)}, u32[]{:S(2)}, u32[]{:S(2)}) collective-permute-start(f32[560,128]{1,0:T(8,128)S(1)} %pad_maximum_fusion), channel_id=1, source_target_pairs={{0,8},{8,16},{16,24},{12,4},{20,12},{28,20},{1,9},{9,17},{17,25},{... | collective-permute-start | bytes 860168 | tf_op jit(solution)/shard_map/ppermute | solution.py:406
  24.9 1.6 %collective-permute-start.4 = (f32[544,128]{1,0:T(8,128)S(1)}, f32[544,128]{1,0:T(8,128)S(1)}, u32[]{:S(2)}, u32[]{:S(2)}) collective-permute-start(f32[544,128]{1,0:T(8,128)S(1)} %get-tuple-element.17), channel_id=1, source_target_pairs={{0,4},{4,0},{1,5},{5,1},{2,6},{6,2},{3,7},{7,3},{8,12},{12,8},{9,1... | collective-permute-start | bytes 835592 | tf_op jit(solution)/shard_map/ppermute | solution.py:450
  24.9 10.7 %collective-permute-start.3 = (f32[16,32,128]{2,1,0:T(8,128)S(1)}, f32[16,32,128]{2,1,0:T(8,128)S(1)}, u32[]{:S(2)}, u32[]{:S(2)}) collective-permute-start(f32[16,32,128]{2,1,0:T(8,128)S(1)} %get-tuple-element.15), channel_id=1, source_target_pairs={{0,4},{4,0},{1,5},{5,1},{2,6},{6,2},{3,7},{7,3},{8,12},{12,8},{9,1... | collective-permute-start | bytes 786440 | tf_op jit(solution)/shard_map/ppermute | solution.py:475
  26.5 9.0 %collective-permute-start.5 = (f32[272,128]{1,0:T(8,128)S(1)}, f32[272,128]{1,0:T(8,128)S(1)}, u32[]{:S(2)}, u32[]{:S(2)}) collective-permute-start(f32[272,128]{1,0:T(8,128)S(1)} %slice.21), channel_id=1, source_target_pairs={{0,8},{8,16},{16,24},{24,0},{12,4},{20,12},{28,20},{4,28},{1,9},{9... | collective-permute-start | bytes 417800 | tf_op jit(solution)/shard_map/ppermute | solution.py:456
  29.1 8.0 %collective-permute-start.6 = (f32[136,128]{1,0:T(8,128)S(1)}, f32[136,128]{1,0:T(8,128)S(1)}, u32[]{:S(2)}, u32[]{:S(2)}) collective-permute-start(f32[136,128]{1,0:T(8,128)S(1)} %get-tuple-element.22), channel_id=1, source_target_pairs={{0,16},{8,24},{16,0},{24,8},{1,17},{9,25},{17,1},{25,9},{2,18},{10... | collective-permute-start | bytes 208904 | tf_op jit(solution)/shard_map/ppermute | solution.py:457
  35.5 1.6 %collective-permute-start.7 = (f32[136,128]{1,0:T(8,128)S(1)}, f32[136,128]{1,0:T(8,128)S(1)}, u32[]{:S(2)}, u32[]{:S(2)}) collective-permute-start(f32[136,128]{1,0:T(8,128)S(1)} %get-tuple-element.24), channel_id=1, source_target_pairs={{0,4},{4,0},{1,5},{5,1},{2,6},{6,2},{3,7},{7,3},{8,12},{12,8},{9,1... | collective-permute-start | bytes 208904 | tf_op jit(solution)/shard_map/ppermute | solution.py:460

commit v4 on v3

--- a/solution.py
+++ b/solution.py
@@ -169,91 +169,98 @@
         copy.wait()
 
 
+def prepare_kernel(
+    keep_ref, other_ref, two_in_ref,
+    two_ref, p_buf, w_buf, d_buf, wet_buf, scale_buf, half_buf,
+):
+    layers = p_buf.shape[1]
+    cols = p_buf.shape[3]
+    core = lax.axis_index("cross")
+    low = core == 0
+    wide = w_buf.shape[2]
+    span = wide - SUB
+    base = 2 * span * layers
+    lane = lanes_of((span, cols))
+    middle = pl.multiple_of(SUB * (1 - core), SUB)
+    zeros = jnp.zeros((SUB, cols), jnp.float32)
+    two_ref[...] = two_in_ref[...]
+    at = base + 2 * span
+    seam = jnp.where(low, keep_ref[at : at + span], other_ref[at : at + span])
+    for tile, main_ref, seam_core in ((core, keep_ref, 1), (1 - core, other_ref, 0)):
+        seam_lane = lane == jnp.where(core == seam_core, 0, -1)
+        depth = main_ref[base : base + span]
+        stiff = main_ref[base + span : base + 2 * span]
+        d_buf[tile, :SUB] = zeros
+        d_buf[tile, pl.ds(middle + SUB, span)] = depth
+        for z in range(layers):
+            at = 2 * span * z
+            p_buf[tile, z, :SUB] = zeros
+            p_buf[tile, z, SUB + wide :] = zeros
+            p_buf[tile, z, pl.ds(middle + SUB, span)] = main_ref[at : at + span]
+            turned = pltpu.roll(seam, cols - z, 1) if z else seam
+            w_buf[tile, z, pl.ds(middle, span)] = main_ref[at + span : at + 2 * span] - jnp.where(
+                seam_lane, turned, 0.0
+            )
+            wet = depth > float(z)
+            wet_buf[tile, z, :SUB] = zeros
+            wet_buf[tile, z, pl.ds(middle + SUB, span)] = jnp.where(wet, 1.0, 0.0)
+            scale_buf[tile, z, pl.ds(middle, span)] = jnp.where(wet, stiff, 0.0)
+            if z > 0:
+                half_buf[tile, z - 1, pl.ds(middle, span)] = jnp.where(wet, 0.5, 0.0)
+
+
 def steps_kernel(
-    keep_ref,
-    other_ref,
-    halo_ref,
-    place_ref,
-    p_keep_ref,
-    p_send_ref,
-    panel_keep_ref,
-    panel_send_ref,
-    p_buf,
-    w_buf,
-    d_buf,
-    s_buf,
-    trace,
-    wet_buf,
-    scale_buf,
-    half_buf,
-    p_two,
-    w_two,
+    keep_ref, other_ref, one_ref, two_ref, place_ref,
+    p_in, w_in, d_in, wet_in, scale_in, half_in,
+    p_keep_ref, p_send_ref, panel_keep_ref, panel_send_ref,
+    p_buf, w_buf, d_buf, wet_buf, scale_buf, half_buf,
+    trace, p_two, w_two,
 ):
     layers, half_rows, cols = p_keep_ref.shape
     core = lax.axis_index("cross")
     low = core == 0
     span = half_rows + SUB
     wide = span + SUB
-    blocks = wide // SUB
     base = 2 * span * layers
     base_z = 2 * SUB * layers
-    ends = halo_ref.shape[0] // 2
-    one_ref = halo_ref.at[:ends]
-    two_ref = halo_ref.at[ends:]
     lane = lanes_of((SUB, cols))
     row = rows_of((SUB, cols))
     middle = pl.multiple_of(SUB * (1 - core), SUB)
     halo = pl.multiple_of(span * core, SUB)
-
-    def left(own, other):
-        return jnp.where(low, own, other)
-
-    seam_span = left(keep_ref[base + 2 * span : base + 3 * span], other_ref[base + 2 * span : base + 3 * span])
-    seam_halo = left(one_ref[base_z + 2 * SUB : base_z + 3 * SUB], two_ref[base_z + 2 * SUB : base_z + 3 * SUB])
+    at = base_z + 2 * SUB
+    seam = jnp.where(low, one_ref[at : at + SUB], two_ref[at : at + SUB])
     top_row = row == jnp.where(low, 0, -1)
     end_row = row == jnp.where(low, -1, 0)
     zeros = jnp.zeros((SUB, cols), jnp.float32)
-    for tile, main_ref, end_ref, seam_core in ((core, keep_ref, one_ref, 1), (1 - core, other_ref, two_ref, 0)):
-        seam_lane = jnp.where(core == seam_core, 0, -1)
-        seam = lanes_of((span, cols)) == seam_lane
-        seam_sub = lane == seam_lane
+    for tile, main_ref, end_ref, seam_core in (
+        (core, keep_ref, one_ref, 1), (1 - core, other_ref, two_ref, 0)
+    ):
+        seam_lane = lane == jnp.where(core == seam_core, 0, -1)
+        depth = end_ref[base_z : base_z + SUB]
+        stiff = end_ref[base_z + SUB : base_z + 2 * SUB]
+        d_buf[tile, pl.ds(halo + SUB, SUB)] = depth
         for z in range(layers):
-            at = 2 * span * z
-            at_z = 2 * SUB * z
-            p_buf[tile, z, :SUB] = zeros
+            at = 2 * SUB * z
             p_two[tile, z, :SUB] = zeros
             p_two[tile, z, SUB + wide :] = zeros
-            p_buf[tile, z, pl.ds(middle + SUB, span)] = main_ref[at : at + span]
-            p_buf[tile, z, pl.ds(halo + SUB, SUB)] = end_ref[at_z : at_z + SUB]
-            p_buf[tile, z, SUB + wide :] = zeros
-            turn = (cols - z) % cols
-            w = main_ref[at + span : at + 2 * span]
-            w = w - jnp.where(seam, pltpu.roll(seam_span, turn, 1) if turn else seam_span, 0.0)
-            w_halo = end_ref[at_z + SUB : at_z + 2 * SUB]
-            slot = jnp.broadcast_to(w_halo[0:1], (SUB, cols))
-            final = jnp.broadcast_to(main_ref[base + 3 * span + z : base + 3 * span + z + 1], (SUB, cols))
-            w_halo = w_halo - jnp.where(seam_sub, pltpu.roll(seam_halo, turn, 1) if turn else seam_halo, 0.0)
-            w_halo = w_halo - jnp.where(end_row, final, 0.0)
-            w_top = w[:SUB] - jnp.where(top_row, slot, 0.0)
-            w_buf[tile, z, pl.ds(middle, SUB)] = w_top
-            w_buf[tile, z, pl.ds(middle + SUB, span - SUB)] = w[SUB:]
-            w_buf[tile, z, pl.ds(halo, SUB)] = w_halo
-        d_buf[tile, :SUB] = zeros
-        for buf, i, shift in ((d_buf, 0, SUB), (s_buf, 1, 0)):
-            buf[tile, pl.ds(middle + shift, span)] = main_ref[base + i * span : base + (i + 1) * span]
-            buf[tile, pl.ds(halo + shift, SUB)] = end_ref[base_z + i * SUB : base_z + (i + 1) * SUB]
+            p_buf[tile, z, pl.ds(halo + SUB, SUB)] = end_ref[at : at + SUB]
+            w = end_ref[at + SUB : at + 2 * SUB]
+            slot = jnp.broadcast_to(w[0:1], (SUB, cols))
+            final = base + 3 * span + z
+            final = jnp.broadcast_to(main_ref[final : final + 1], (SUB, cols))
+            turned = pltpu.roll(seam, cols - z, 1) if z else seam
+            w = w - jnp.where(seam_lane, turned, 0.0) - jnp.where(end_row, final, 0.0)
+            w_buf[tile, z, pl.ds(halo, SUB)] = w
+            w_buf[tile, z, pl.ds(middle, SUB)] = w_buf[tile, z, pl.ds(middle, SUB)] - jnp.where(
+                top_row, slot, 0.0
+            )
+            wet = depth > float(z)
+            wet_buf[tile, z, pl.ds(halo + SUB, SUB)] = jnp.where(wet, 1.0, 0.0)
+            scale_buf[tile, z, pl.ds(halo, SUB)] = jnp.where(wet, stiff, 0.0)
+            if z > 0:
+                half_buf[tile, z - 1, pl.ds(halo, SUB)] = jnp.where(wet, 0.5, 0.0)
 
     zs = range(layers)
-    for i in range(2):
-        for z in zs:
-            wet = d_buf[i, SUB:] > float(z)
-            if True:
-                wet_buf[i, z, :SUB] = zeros
-                wet_buf[i, z, SUB:] = jnp.where(wet, 1.0, 0.0)
-            if True:
-                scale_buf[i, z] = jnp.where(wet, s_buf[i], 0.0)
-            if True and z > 0:
-                half_buf[i, z - 1] = jnp.where(wet, 0.5, 0.0)
     ZB = 4
     groups = layers // ZB
     lane = lanes_of((ZB, wide, cols))
@@ -368,7 +375,9 @@
     swap = [(0, 1), (1, 0)]
     pair = ("along", "cross")
     steps_up = range(along_count - 1)
-    route = [(2 * i, 2 * i + 2) for i in steps_up] + [(2 * i + 3, 2 * i + 1) for i in steps_up]
+    route_one = [(2 * i, 2 * i + 2) for i in steps_up] + [(2 * i + 3, 2 * i + 1) for i in steps_up]
+    route_two = [(2 * i + 1, 2 * i + 2) for i in steps_up]
+    route_two += [(2 * i + 2, 2 * i + 1) for i in steps_up]
     half_rows = rows // 2
     span = half_rows + SUB
     wide = span + SUB
@@ -399,11 +408,42 @@
         ],
         compiler_params=params,
         name="edges",
-    )(pressure_start[0], along_start[0], cross_start[0], depth_layers, stiffness, owner_map)
-
-    halo = jnp.concatenate([one, lax.ppermute(two, "cross", swap)], 0)
+    )(
+        *(
+            pltpu.with_memory_space_constraint(x, pltpu.HBM)
+            for x in (
+                pressure_start[0],
+                along_start[0],
+                cross_start[0],
+                depth_layers,
+                stiffness,
+                owner_map,
+            )
+        )
+    )
+
     other = lax.ppermute(send, "cross", swap)
-    halo = lax.ppermute(halo, pair, route)
+    one = lax.ppermute(one, pair, route_one)
+    state_shapes = [
+        jax.ShapeDtypeStruct(shape, f32)
+        for shape in (
+            (2, layers, wide + 2 * SUB, cols),
+            (2, layers, wide, cols),
+            (2, wide + SUB, cols),
+            (2, layers, wide + SUB, cols),
+            (2, layers, wide, cols),
+            (2, layers - 1, wide, cols),
+        )
+    ]
+    two, *state = pl.pallas_call(
+        prepare_kernel,
+        out_shape=[jax.ShapeDtypeStruct((end_rows, cols), f32)] + state_shapes,
+        in_specs=[spec] * 3,
+        out_specs=[spec] * 7,
+        compiler_params=params,
+        name="prepare",
+    )(keep, other, two)
+    two = lax.ppermute(two, pair, route_two)
 
     patch_count = 2 * rows
     owner_count = along_count * cross_count
@@ -421,31 +461,26 @@
     )(patch_lists.reshape(-1, patch_count).T, owner_map, other)
 
     parts = STEPS // 2
-    p_keep, p_send, panel_keep, panel_send = pl.pallas_call(
+    p_keep, p_send, panel_keep, panel_send, *state = pl.pallas_call(
         steps_kernel,
         out_shape=[
             jax.ShapeDtypeStruct((layers, half_rows, cols), f32),
             jax.ShapeDtypeStruct((layers, half_rows, cols), f32),
             jax.ShapeDtypeStruct((count * parts, cols), f32),
             jax.ShapeDtypeStruct((count * parts, cols), f32),
-        ],
-        in_specs=[spec] * 4,
-        out_specs=[spec] * 4,
+        ]
+        + state_shapes,
+        in_specs=[spec] * 11,
+        out_specs=[spec] * 10,
         scratch_shapes=[
-            VMEM((2, layers, wide + 2 * SUB, cols), f32),
-            VMEM((2, layers, wide, cols), f32),
-            VMEM((2, wide + SUB, cols), f32),
-            VMEM((2, wide, cols), f32),
             VMEM((STEPS, 2, half_rows, cols), f32),
-            VMEM((2, layers, wide + SUB, cols), f32),
-            VMEM((2, layers, wide, cols), f32),
-            VMEM((2, layers - 1, wide, cols), f32),
             VMEM((2, layers, wide + 2 * SUB, cols), f32),
             VMEM((2, layers, wide, cols), f32),
         ],
+        input_output_aliases={5 + i: 4 + i for i in range(6)},
         compiler_params=params,
         name="steps",
-    )(keep, other, halo, place)
+    )(keep, other, one, two, place, *state)
 
     panels = panel_keep + lax.ppermute(panel_send, "cross", swap)
     if along_count == 4:

time: 38.3 us -> 46.4 us (1.21)
  Pallas kernels: 8.28 us -> 14 us
  waiting for transfers between devices: 11.2 us -> 7.32 us
  starting transfers between devices: 11.3 us -> 14.1 us
  local copies, waits for them, and re-layouts: 5.43 us -> 8.07 us
  other arithmetic: 0.9 us -> 1.83 us
    ppermute x2, waiting for transfers between devices: 5.72 us -> 0.01 us  [the longest x1 0.01 us: shards(): one = lax.ppermute(one, pair, route_one)]
    ppermute x1, starting transfers between devices: 0.07 us -> 3.48 us  [shards(): panels = panel_keep + lax.ppermute(panel_send, 'cross', swap)]
    pallas_call x1, Pallas kernels: 6.71 us -> 9.71 us  [shards(): pl.pallas_call(steps_kernel, out_shape=[jax.ShapeDtypeStruct((layers, hal...]
    unnamed x14 -> x24, local copies, waits for them, and re-layouts: 5.29 us -> 7.93 us
    pallas_call x1, Pallas kernels: 0.62 us -> 2.49 us  [shards(): pl.pallas_call(edges_kernel, out_shape=[jax.ShapeDtypeStruct((pack_rows,...]
    ppermute x2, starting transfers between devices: 4.94 us -> 6.6 us  [the longest x1 5.16 us: shards(): one = lax.ppermute(one, pair, route_one)]
    ppermute x1, starting transfers between devices: 2.65 us -> 1.33 us  [shards(): lax.ppermute(panels[2 * some:3 * some], 'along', [(i, (i + 2) % along_cou...]
    ppermute x1, waiting for transfers between devices: 3.8 us -> 5.1 us  [shards(): near = lax.ppermute(panels[:2 * some], pair, near_route)]
  transfers between devices with their start and end apart: 8 -> 8, of which waited for: 5 -> 3; matrix products, arithmetic and copies ran while one was open for 3% -> 4% of each run, Pallas kernels for 1% -> 2%
where the time goes in v4:
time: 46.4 us; the launch traced here: 46 us
  starting transfers between devices  14.1 us (30%)
  Pallas kernels  14 us (30%)
  local copies, waits for them, and re-layouts  8.07 us (17%)
  waiting for transfers between devices  7.32 us (16%)
  other arithmetic  1.83 us (4%)
  between operations  0.73 us (2%)
    pallas_call x1, Pallas kernels, shards(): pl.pallas_call(steps_kernel, out_shape=[jax.ShapeDtypeStruct((layers, hal...  9.71 us
    unnamed x24, local copies, waits for them, and re-layouts  7.93 us
    ppermute x1, starting transfers between devices, shards(): one = lax.ppermute(one, pair, route_one)  5.16 us
    ppermute x1, waiting for transfers between devices, shards(): near = lax.ppermute(panels[:2 * some], pair, near_route)  5.1 us
    ppermute x1, starting transfers between devices, shards(): panels = panel_keep + lax.ppermute(panel_send, 'cross', swap)  3.48 us
    pallas_call x1, Pallas kernels, shards(): pl.pallas_call(edges_kernel, out_shape=[jax.ShapeDtypeStruct((pack_rows,...  2.49 us
    ppermute x1, starting transfers between devices, shards(): near = lax.ppermute(panels[:2 * some], pair, near_route)  2.04 us
    ppermute x1, starting transfers between devices, shards(): two = lax.ppermute(two, pair, route_two)  1.43 us
  transfers between devices with their start and end apart: 8, of which 3 were waited for; matrix products, arithmetic and copies ran while one was open for 4% of the time, Pallas kernels for 2%

profile of v4, /device:TPU:0, one launch (start us, length us, event | category | flops | bytes accessed | tf_op | source)
XLA Modules:
  0.0 46.0 jit_solution(10739376526124017439)
XLA Ops:
  0.6 2.5 %edges.1 = (f32[1416,128]{1,0:T(8,128)S(1)}, f32[1424,128]{1,0:T(8,128)S(1)}, f32[280,128]{1,0:T(8,128)}, f32[280,128]{1,0:T(8,128)S(1)}) custom-call(f32[16,64,128]{2,1,0:T(8,128)} %bitcast.10, f32[16,64,128]{2,1,0:T(8,128)} %bitcast.11, f32[16,64,128]{2,1,0:T(8,128)} %bitcast.12, s32[64,128]{1,0:T(8,128)} %depth_hbm.1, f32[64,128]{1,0:T(8,128)} %stiff_hbm.1, ...), custom_call_target="tpu_custom_call" | custom-call | tf_op jit(solution)/shard_map/edges/pallas_call | solution.py:390
  3.1 0.5 %collective-permute-start = (f32[1424,128]{1,0:T(8,128)S(1)}, f32[1424,128]{1,0:T(8,128)S(1)}, u32[]{:S(2)}, u32[]{:S(2)}) collective-permute-start(f32[1424,128]{1,0:T(8,128)S(1)} %get-tuple-element.18), channel_id=1, source_target_pairs={{0,4},{4,0},{1,5},{5,1},{2,6},{6,2},{3,7},{7,3},{8,12},{12,8},{9,1... | collective-permute-start | bytes 2187272 | tf_op jit(solution)/shard_map/ppermute | solution.py:425
  3.6 5.2 %collective-permute-start.1 = (f32[280,128]{1,0:T(8,128)}, f32[280,128]{1,0:T(8,128)}, u32[]{:S(2)}, u32[]{:S(2)}) collective-permute-start(f32[280,128]{1,0:T(8,128)} %get-tuple-element.19), channel_id=1, source_target_pairs={{0,8},{8,16},{16,24},{12,4},{20,12},{28,20},{1,9},{9,17},{17,25},{... | collective-permute-start | bytes 430088 | tf_op jit(solution)/shard_map/ppermute | solution.py:426
  8.8 0.0 collective-permute-done.other_ref
  8.8 0.9 %prepare.1 = (f32[280,128]{1,0:T(8,128)}, f32[2,16,64,128]{3,2,1,0:T(8,128)S(1)}, f32[2,16,48,128]{3,2,1,0:T(8,128)S(1)}, f32[2,56,128]{2,1,0:T(8,128)S(1)}, f32...) custom-call(f32[1416,128]{1,0:T(8,128)S(1)} %get-tuple-element.17.keep_ref, ...), custom_call_target="tpu_custom_call" | custom-call | tf_op jit(solution)/shard_map/prepare/pallas_call | solution.py:438
  9.7 0.0 copy-start
  9.7 0.9 %copy-done = f32[2,16,48,128]{3,2,1,0:T(8,128)} copy-done((f32[2,16,48,128]{3,2,1,0:T(8,128)}, f32[2,16,48,128]{3,2,1,0:T(8,128)S(1)}, u32[]{:S(2)}) %copy-start) | copy-done | bytes 786456
  10.5 0.0 copy-start.2
  10.5 0.9 %copy-done.2 = f32[2,16,48,128]{3,2,1,0:T(8,128)} copy-done((f32[2,16,48,128]{3,2,1,0:T(8,128)}, f32[2,16,48,128]{3,2,1,0:T(8,128)S(1)}, u32[]{:S(2)}) %copy-start.2) | copy-done | bytes 786456
  11.5 0.0 copy-start.4
  11.5 0.9 %copy-done.4 = f32[2,15,48,128]{3,2,1,0:T(8,128)} copy-done((f32[2,15,48,128]{3,2,1,0:T(8,128)}, f32[2,15,48,128]{3,2,1,0:T(8,128)S(1)}, u32[]{:S(2)}) %copy-start.4) | copy-done | bytes 737304
  12.3 0.0 copy-start.11
  12.3 1.4 %collective-permute-start.2 = (f32[280,128]{1,0:T(8,128)}, f32[280,128]{1,0:T(8,128)}, u32[]{:S(2)}, u32[]{:S(2)}) collective-permute-start(f32[280,128]{1,0:T(8,128)} %get-tuple-element.21), channel_id=1, source_target_pairs={{4,8},{12,16},{20,24},{8,4},{16,12},{24,20},{5,9},{13,17},{21,25},... | collective-permute-start | bytes 430088 | tf_op jit(solution)/shard_map/ppermute | solution.py:446
  13.8 0.0 copy-done.11
  13.8 0.0 copy-start.9
  13.8 0.1 copy.16
  13.9 0.0 copy-start.1
  13.9 0.5 %copy-done.9 = s32[1,128]{1,0:T(1,128)S(1)} copy-done((s32[1,128]{1,0:T(1,128)S(1)}, s32[1,128]{1,0:T(1,128)}, u32[]{:S(2)}) %copy-start.9) | copy-done | bytes 536
  14.4 0.2 place.1.place_ref
  14.6 0.0 collective-permute-done.1.one_ref
  14.6 0.0 collective-permute-done.2.two_ref
  14.7 0.3 copy-done.1
  15.0 0.0 copy-start.3
  15.0 1.1 %copy-done.3 = f32[2,16,48,128]{3,2,1,0:T(8,128)S(1)} copy-done((f32[2,16,48,128]{3,2,1,0:T(8,128)S(1)}, f32[2,16,48,128]{3,2,1,0:T(8,128)}, u32[]{:S(2)}) %copy-start.3) | copy-done | bytes 786456
  16.1 0.0 copy-start.5
  16.1 1.1 %copy-done.5 = f32[2,15,48,128]{3,2,1,0:T(8,128)S(1)} copy-done((f32[2,15,48,128]{3,2,1,0:T(8,128)S(1)}, f32[2,15,48,128]{3,2,1,0:T(8,128)}, u32[]{:S(2)}) %copy-start.5) | copy-done | bytes 737304
  17.3 9.7 %steps.1 = (f32[16,32,128]{2,1,0:T(8,128)S(1)}, f32[16,32,128]{2,1,0:T(8,128)S(1)}, f32[544,128]{1,0:T(8,128)S(1)}, f32[544,128]{1,0:T(8,128)}, f32[2,16,64,128]...) custom-call(f32[1416,128]{1,0:T(8,128)S(1)} %get-tuple-element.17.ke, ...), custom_call_target="tpu_custom_call", output_to_operand_aliasing={{4}: (5, {}), {5}: (6, {}), {6}: (7, {}), {7}: (8, {}), {8}... | custom-call | tf_op jit(solution)/shard_map/steps/pallas_call | solution.py:464
  27.0 0.0 copy-start.6
  27.0 0.7 %copy-done.6 = f32[544,128]{1,0:T(8,128)} copy-done((f32[544,128]{1,0:T(8,128)}, f32[544,128]{1,0:T(8,128)S(1)}, u32[]{:S(2)}) %copy-start.6) | copy-done | bytes 278552
  27.7 0.0 copy-start.7
  27.7 0.7 %copy-done.7 = f32[16,32,128]{2,1,0:T(8,128)} copy-done((f32[16,32,128]{2,1,0:T(8,128)}, f32[16,32,128]{2,1,0:T(8,128)S(1)}, u32[]{:S(2)}) %copy-start.7) | copy-done | bytes 262168
  28.4 0.0 copy-start.10
  28.4 0.7 %copy-done.10 = f32[16,32,128]{2,1,0:T(8,128)} copy-done((f32[16,32,128]{2,1,0:T(8,128)}, f32[16,32,128]{2,1,0:T(8,128)S(1)}, u32[]{:S(2)}) %copy-start.10) | copy-done | bytes 262168
  29.1 3.5 %collective-permute-start.4 = (f32[544,128]{1,0:T(8,128)}, f32[544,128]{1,0:T(8,128)S(1)}, u32[]{:S(2)}, u32[]{:S(2)}) collective-permute-start(f32[544,128]{1,0:T(8,128)} %get-tuple-element.31), channel_id=1, source_target_pairs={{0,4},{4,0},{1,5},{5,1},{2,6},{6,2},{3,7},{7,3},{8,12},{12,8},{9,1... | collective-permute-start | bytes 835592 | tf_op jit(solution)/shard_map/ppermute | solution.py:485
  32.6 0.0 collective-permute-start.3
  32.6 1.4 %collective-permute-done.4 = f32[544,128]{1,0:T(8,128)S(1)} collective-permute-done((f32[544,128]{1,0:T(8,128)}, f32[544,128]{1,0:T(8,128)S(1)}, u32[]{:S(2)}, u32[]{:S(2)}) %collective-permute-start.4) | collective-permute-done | bytes 278560 | tf_op jit(solution)/shard_map/ppermute | solution.py:485
  34.0 1.0 %add.3 = f32[544,128]{1,0:T(8,128)S(1)} add(f32[544,128]{1,0:T(8,128)} %copy-done.6, f32[544,128]{1,0:T(8,128)S(1)} %collective-permute-done.4) | non-fusion elementwise | flops 69632 | bytes 835584 | tf_op jit(solution)/shard_map/add | solution.py:485
  35.0 0.0 copy-start.8
  35.0 2.0 %collective-permute-start.5 = (f32[272,128]{1,0:T(8,128)S(1)}, f32[272,128]{1,0:T(8,128)S(1)}, u32[]{:S(2)}, u32[]{:S(2)}) collective-permute-start(f32[272,128]{1,0:T(8,128)S(1)} %slice.21), channel_id=1, source_target_pairs={{0,8},{8,16},{16,24},{24,0},{12,4},{20,12},{28,20},{4,28},{1,9},{9... | collective-permute-start | bytes 417800 | tf_op jit(solution)/shard_map/ppermute | solution.py:491
  37.0 1.3 %collective-permute-start.6 = (f32[136,128]{1,0:T(8,128)S(1)}, f32[136,128]{1,0:T(8,128)S(1)}, u32[]{:S(2)}, u32[]{:S(2)}) collective-permute-start(f32[136,128]{1,0:T(8,128)S(1)} %get-tuple-element.36), channel_id=1, source_target_pairs={{0,16},{8,24},{16,0},{24,8},{1,17},{9,25},{17,1},{25,9},{2,18},{10... | collective-permute-start | bytes 208904 | tf_op jit(solution)/shard_map/ppermute | solution.py:492
  38.4 5.1 %collective-permute-done.5 = f32[272,128]{1,0:T(8,128)S(1)} collective-permute-done((f32[272,128]{1,0:T(8,128)S(1)}, f32[272,128]{1,0:T(8,128)S(1)}, u32[]{:S(2)}, u32[]{:S(2)}) %collective-permute-start.5) | collective-permute-done | bytes 139296 | tf_op jit(solution)/shard_map/ppermute | solution.py:491
  43.5 0.1 collective-permute-start.7
  43.6 0.0 collective-permute-done.3
  43.6 0.0 copy-done.8
  43.6 0.8 %maximum_select_fusion = f32[1,16,64,128]{3,2,1,0:T(8,128)} fusion(f32[1,16,32,128]{3,2,1,0:T(8,128)S(1)} %bitcast.14, f32[1,16,32,128]{3,2,1,0:T(8,128)S(1)} %bitcast.9, pred[]{:T(512)S(6)} %eq.3), kind=kLoop, calls=%fused_computation | loop fusion | flops 393216 | bytes 1048577 | tf_op jit(solution)/shard_map/jit(_where)/select_n | solution.py:511
  44.4 0.8 %collective-permute-done.6.far_ref = f32[136,128]{1,0:T(8,128)S(1)} collective-permute-done((f32[136,128]{1,0:T(8,128)S(1)}, f32[136,128]{1,0:T(8,128)S(1)}, u32[]{:S(2)}, u32[]{:S(2)}) %collective-permute-start.6) | collective-permute-done | bytes 69664 | tf_op jit(solution)/shard_map/ppermute | solution.py:492
  45.3 0.0 collective-permute-done.7.swapped_ref
  45.3 0.7 %gather.1 = f32[544,128]{1,0:T(8,128)} custom-call(f32[136,128]{1,0:T(8,128)S(1)} %get-tuple-element.37.own_ref, f32[136,128]{1,0:T(8,128)S(1)} %get-tuple-element.39.near_ref, f32[136,128]{1,0:T(8,128)S(1)} %collective-permute-done.6.far_ref, f32[136,128]{1,0:T(8,128)S(1)} %collective-permute-done.7.swapped_ref), custom_call_target="tpu_custom_call" | custom-call | tf_op jit(solution)/shard_map/gather/pallas_call | solution.py:496
  (3 shorter events, 0.0 us)
Async XLA Ops:
  3.1 5.7 %collective-permute-start = (f32[1424,128]{1,0:T(8,128)S(1)}, f32[1424,128]{1,0:T(8,128)S(1)}, u32[]{:S(2)}, u32[]{:S(2)}) collective-permute-start(f32[1424,128]{1,0:T(8,128)S(1)} %get-tuple-element.18), channel_id=1, source_target_pairs={{0,4},{4,0},{1,5},{5,1},{2,6},{6,2},{3,7},{7,3},{8,12},{12,8},{9,1... | collective-permute-start | bytes 2187272 | tf_op jit(solution)/shard_map/ppermute | solution.py:425
  3.6 11.0 %collective-permute-start.1 = (f32[280,128]{1,0:T(8,128)}, f32[280,128]{1,0:T(8,128)}, u32[]{:S(2)}, u32[]{:S(2)}) collective-permute-start(f32[280,128]{1,0:T(8,128)} %get-tuple-element.19), channel_id=1, source_target_pairs={{0,8},{8,16},{16,24},{12,4},{20,12},{28,20},{1,9},{9,17},{17,25},{... | collective-permute-start | bytes 430088 | tf_op jit(solution)/shard_map/ppermute | solution.py:426
  9.7 0.9 %copy-start = (f32[2,16,48,128]{3,2,1,0:T(8,128)}, f32[2,16,48,128]{3,2,1,0:T(8,128)S(1)}, u32[]{:S(2)}) copy-start(f32[2,16,48,128]{3,2,1,0:T(8,128)S(1)} %get-tuple-element.23.w_in) | copy-start | bytes 2359300
  10.5 0.9 %copy-start.2 = (f32[2,16,48,128]{3,2,1,0:T(8,128)}, f32[2,16,48,128]{3,2,1,0:T(8,128)S(1)}, u32[]{:S(2)}) copy-start(f32[2,16,48,128]{3,2,1,0:T(8,128)S(1)} %get-tuple-element.26.scale_in) | copy-start | bytes 2359300
  11.5 0.9 %copy-start.4 = (f32[2,15,48,128]{3,2,1,0:T(8,128)}, f32[2,15,48,128]{3,2,1,0:T(8,128)S(1)}, u32[]{:S(2)}) copy-start(f32[2,15,48,128]{3,2,1,0:T(8,128)S(1)} %get-tuple-element.27.half_in) | copy-start | bytes 2211844
  12.3 1.4 %copy-start.11 = (s32[1,512]{1,0:T(1,128)S(1)}, s32[1,512]{1,0:T(1,128)}, u32[]{:S(2)}) copy-start(s32[1,512]{1,0:T(1,128)} %param.12) | copy-start | bytes 6148
  12.3 2.3 %collective-permute-start.2 = (f32[280,128]{1,0:T(8,128)}, f32[280,128]{1,0:T(8,128)}, u32[]{:S(2)}, u32[]{:S(2)}) collective-permute-start(f32[280,128]{1,0:T(8,128)} %get-tuple-element.21), channel_id=1, source_target_pairs={{4,8},{12,16},{20,24},{8,4},{16,12},{24,20},{5,9},{13,17},{21,25},... | collective-permute-start | bytes 430088 | tf_op jit(solution)/shard_map/ppermute | solution.py:446
  13.8 0.7 %copy-start.9 = (s32[1,128]{1,0:T(1,128)S(1)}, s32[1,128]{1,0:T(1,128)}, u32[]{:S(2)}) copy-start(s32[1,128]{1,0:T(1,128)} %own_ref.1) | copy-start | bytes 1540
  13.9 1.1 %copy-start.1 = (f32[2,16,48,128]{3,2,1,0:T(8,128)S(1)}, f32[2,16,48,128]{3,2,1,0:T(8,128)}, u32[]{:S(2)}) copy-start(f32[2,16,48,128]{3,2,1,0:T(8,128)} %copy-done) | copy-start | bytes 2359300
  15.0 1.1 %copy-start.3 = (f32[2,16,48,128]{3,2,1,0:T(8,128)S(1)}, f32[2,16,48,128]{3,2,1,0:T(8,128)}, u32[]{:S(2)}) copy-start(f32[2,16,48,128]{3,2,1,0:T(8,128)} %copy-done.2) | copy-start | bytes 2359300
  16.1 1.1 %copy-start.5 = (f32[2,15,48,128]{3,2,1,0:T(8,128)S(1)}, f32[2,15,48,128]{3,2,1,0:T(8,128)}, u32[]{:S(2)}) copy-start(f32[2,15,48,128]{3,2,1,0:T(8,128)} %copy-done.4) | copy-start | bytes 2211844
  27.0 0.7 %copy-start.6 = (f32[544,128]{1,0:T(8,128)}, f32[544,128]{1,0:T(8,128)S(1)}, u32[]{:S(2)}) copy-start(f32[544,128]{1,0:T(8,128)S(1)} %get-tuple-element.30) | copy-start | bytes 835588
  27.7 0.7 %copy-start.7 = (f32[16,32,128]{2,1,0:T(8,128)}, f32[16,32,128]{2,1,0:T(8,128)S(1)}, u32[]{:S(2)}) copy-start(f32[16,32,128]{2,1,0:T(8,128)S(1)} %get-tuple-element.28) | copy-start | bytes 786436
  28.4 0.7 %copy-start.10 = (f32[16,32,128]{2,1,0:T(8,128)}, f32[16,32,128]{2,1,0:T(8,128)S(1)}, u32[]{:S(2)}) copy-start(f32[16,32,128]{2,1,0:T(8,128)S(1)} %get-tuple-element.29) | copy-start | bytes 786436
  29.1 4.9 %collective-permute-start.4 = (f32[544,128]{1,0:T(8,128)}, f32[544,128]{1,0:T(8,128)S(1)}, u32[]{:S(2)}, u32[]{:S(2)}) collective-permute-start(f32[544,128]{1,0:T(8,128)} %get-tuple-element.31), channel_id=1, source_target_pairs={{0,4},{4,0},{1,5},{5,1},{2,6},{6,2},{3,7},{7,3},{8,12},{12,8},{9,1... | collective-permute-start | bytes 835592 | tf_op jit(solution)/shard_map/ppermute | solution.py:485
  32.6 11.0 %collective-permute-start.3 = (f32[16,32,128]{2,1,0:T(8,128)}, f32[16,32,128]{2,1,0:T(8,128)S(1)}, u32[]{:S(2)}, u32[]{:S(2)}) collective-permute-start(f32[16,32,128]{2,1,0:T(8,128)} %copy-done.10), channel_id=1, source_target_pairs={{0,4},{4,0},{1,5},{5,1},{2,6},{6,2},{3,7},{7,3},{8,12},{12,8},{9,1... | collective-permute-start | bytes 786440 | tf_op jit(solution)/shard_map/ppermute | solution.py:510
  35.0 8.6 %copy-start.8 = (f32[16,32,128]{2,1,0:T(8,128)S(1)}, f32[16,32,128]{2,1,0:T(8,128)}, u32[]{:S(2)}) copy-start(f32[16,32,128]{2,1,0:T(8,128)} %copy-done.7) | copy-start | bytes 786436
  35.0 8.5 %collective-permute-start.5 = (f32[272,128]{1,0:T(8,128)S(1)}, f32[272,128]{1,0:T(8,128)S(1)}, u32[]{:S(2)}, u32[]{:S(2)}) collective-permute-start(f32[272,128]{1,0:T(8,128)S(1)} %slice.21), channel_id=1, source_target_pairs={{0,8},{8,16},{16,24},{24,0},{12,4},{20,12},{28,20},{4,28},{1,9},{9... | collective-permute-start | bytes 417800 | tf_op jit(solution)/shard_map/ppermute | solution.py:491
  37.0 8.2 %collective-permute-start.6 = (f32[136,128]{1,0:T(8,128)S(1)}, f32[136,128]{1,0:T(8,128)S(1)}, u32[]{:S(2)}, u32[]{:S(2)}) collective-permute-start(f32[136,128]{1,0:T(8,128)S(1)} %get-tuple-element.36), channel_id=1, source_target_pairs={{0,16},{8,24},{16,0},{24,8},{1,17},{9,25},{17,1},{25,9},{2,18},{10... | collective-permute-start | bytes 208904 | tf_op jit(solution)/shard_map/ppermute | solution.py:492
  43.5 1.8 %collective-permute-start.7 = (f32[136,128]{1,0:T(8,128)S(1)}, f32[136,128]{1,0:T(8,128)S(1)}, u32[]{:S(2)}, u32[]{:S(2)}) collective-permute-start(f32[136,128]{1,0:T(8,128)S(1)} %get-tuple-element.38), channel_id=1, source_target_pairs={{0,4},{4,0},{1,5},{5,1},{2,6},{6,2},{3,7},{7,3},{8,12},{12,8},{9,1... | collective-permute-start | bytes 208904 | tf_op jit(solution)/shard_map/ppermute | solution.py:495

commit v5 on v3

--- a/solution.py
+++ b/solution.py
@@ -172,7 +172,8 @@
 def steps_kernel(
     keep_ref,
     other_ref,
-    halo_ref,
+    one_ref,
+    two_ref,
     place_ref,
     p_keep_ref,
     p_send_ref,
@@ -197,9 +198,6 @@
     blocks = wide // SUB
     base = 2 * span * layers
     base_z = 2 * SUB * layers
-    ends = halo_ref.shape[0] // 2
-    one_ref = halo_ref.at[:ends]
-    two_ref = halo_ref.at[ends:]
     lane = lanes_of((SUB, cols))
     row = rows_of((SUB, cols))
     middle = pl.multiple_of(SUB * (1 - core), SUB)
@@ -368,7 +366,9 @@
     swap = [(0, 1), (1, 0)]
     pair = ("along", "cross")
     steps_up = range(along_count - 1)
-    route = [(2 * i, 2 * i + 2) for i in steps_up] + [(2 * i + 3, 2 * i + 1) for i in steps_up]
+    route_one = [(2 * i, 2 * i + 2) for i in steps_up] + [(2 * i + 3, 2 * i + 1) for i in steps_up]
+    route_two = [(2 * i + 1, 2 * i + 2) for i in steps_up]
+    route_two += [(2 * i + 2, 2 * i + 1) for i in steps_up]
     half_rows = rows // 2
     span = half_rows + SUB
     wide = span + SUB
@@ -399,11 +399,23 @@
         ],
         compiler_params=params,
         name="edges",
-    )(pressure_start[0], along_start[0], cross_start[0], depth_layers, stiffness, owner_map)
-
-    halo = jnp.concatenate([one, lax.ppermute(two, "cross", swap)], 0)
+    )(
+        *(
+            pltpu.with_memory_space_constraint(x, pltpu.HBM)
+            for x in (
+                pressure_start[0],
+                along_start[0],
+                cross_start[0],
+                depth_layers,
+                stiffness,
+                owner_map,
+            )
+        )
+    )
+
     other = lax.ppermute(send, "cross", swap)
-    halo = lax.ppermute(halo, pair, route)
+    one = lax.ppermute(one, pair, route_one)
+    two = lax.ppermute(two, pair, route_two)
 
     patch_count = 2 * rows
     owner_count = along_count * cross_count
@@ -429,7 +441,7 @@
             jax.ShapeDtypeStruct((count * parts, cols), f32),
             jax.ShapeDtypeStruct((count * parts, cols), f32),
         ],
-        in_specs=[spec] * 4,
+        in_specs=[spec] * 5,
         out_specs=[spec] * 4,
         scratch_shapes=[
             VMEM((2, layers, wide + 2 * SUB, cols), f32),
@@ -445,7 +457,7 @@
         ],
         compiler_params=params,
         name="steps",
-    )(keep, other, halo, place)
+    )(keep, other, one, two, place)
 
     panels = panel_keep + lax.ppermute(panel_send, "cross", swap)
     if along_count == 4:

time: 38.3 us -> 33.1 us (0.86)
  local copies, waits for them, and re-layouts: 5.43 us -> 0.79 us
  waiting for transfers between devices: 11.2 us -> 7.99 us
  starting transfers between devices: 11.3 us -> 13 us
  Pallas kernels: 8.28 us -> 9.52 us
    ppermute x2, waiting for transfers between devices: 5.72 us -> 0.93 us  [the longest x1 0.93 us: shards(): one = lax.ppermute(one, pair, route_one)]
    unnamed x14 -> x4, local copies, waits for them, and re-layouts: 5.29 us -> 0.64 us
    ppermute x1, starting transfers between devices: 0.07 us -> 3.82 us  [shards(): panels = panel_keep + lax.ppermute(panel_send, 'cross', swap)]
    ppermute x1, starting transfers between devices: 2.65 us -> 1.27 us  [shards(): lax.ppermute(panels[2 * some:3 * some], 'along', [(i, (i + 2) % along_cou...]
    ppermute x1, waiting for transfers between devices: 3.8 us -> 5.17 us  [shards(): near = lax.ppermute(panels[:2 * some], pair, near_route)]
    pallas_call x1, Pallas kernels: 0.62 us -> 1.87 us  [shards(): pl.pallas_call(edges_kernel, out_shape=[jax.ShapeDtypeStruct((pack_rows,...]
    ppermute x1, starting transfers between devices: 2.54 us -> 2.05 us  [shards(): near = lax.ppermute(panels[:2 * some], pair, near_route)]
    ppermute x1, starting transfers between devices: 0.49 us -> 0.08 us  [shards(): p_other = lax.ppermute(p_send, 'cross', swap)]
  transfers between devices with their start and end apart: 8 -> 8, of which waited for: 5 -> 4; matrix products, arithmetic and copies ran while one was open for 3% -> 3% of each run, Pallas kernels for 1% -> 1%
where the time goes in v5:
time: 33.1 us; the launch traced here: 32.9 us
  starting transfers between devices  13 us (39%)
  Pallas kernels  9.52 us (29%)
  waiting for transfers between devices  7.99 us (24%)
  other arithmetic  0.9 us (3%)
  local copies, waits for them, and re-layouts  0.79 us (2%)
  between operations  0.73 us (2%)
    pallas_call x1, Pallas kernels, shards(): pl.pallas_call(steps_kernel, out_shape=[jax.ShapeDtypeStruct((layers, hal...  6.71 us
    ppermute x1, waiting for transfers between devices, shards(): near = lax.ppermute(panels[:2 * some], pair, near_route)  5.17 us
    ppermute x1, starting transfers between devices, shards(): one = lax.ppermute(one, pair, route_one)  4.51 us
    ppermute x1, starting transfers between devices, shards(): panels = panel_keep + lax.ppermute(panel_send, 'cross', swap)  3.82 us
    ppermute x1, starting transfers between devices, shards(): near = lax.ppermute(panels[:2 * some], pair, near_route)  2.05 us
    pallas_call x1, Pallas kernels, shards(): pl.pallas_call(edges_kernel, out_shape=[jax.ShapeDtypeStruct((pack_rows,...  1.87 us
    ppermute x1, starting transfers between devices, shards(): lax.ppermute(panels[2 * some:3 * some], 'along', [(i, (i + 2) % along_cou...  1.27 us
    ppermute x1, waiting for transfers between devices, shards(): panels = panel_keep + lax.ppermute(panel_send, 'cross', swap)  1.1 us
  transfers between devices with their start and end apart: 8, of which 4 were waited for; matrix products, arithmetic and copies ran while one was open for 3% of the time, Pallas kernels for 1%

profile of v5, /device:TPU:0, one launch (start us, length us, event | category | flops | bytes accessed | tf_op | source)
XLA Modules:
  0.0 32.9 jit_solution(726846581876757762)
XLA Ops:
  0.6 1.9 %edges.1 = (f32[1416,128]{1,0:T(8,128)S(1)}, f32[1424,128]{1,0:T(8,128)S(1)}, f32[280,128]{1,0:T(8,128)S(1)}, f32[280,128]{1,0:T(8,128)S(1)}) custom-call(f32[16,64,128]{2,1,0:T(8,128)} %bitcast.10, f32[16,64,128]{2,1,0:T(8,128)} %bitcast.11, f32[16,64,128]{2,1,0:T(8,128)} %bitcast.12, s32[64,128]{1,0:T(8,128)} %depth_hbm.1, f32[64,128]{1,0:T(8,128)} %stiff_hbm.1, ...), custom_call_target="tpu_custom_call" | custom-call | tf_op jit(solution)/shard_map/edges/pallas_call | solution.py:381
  2.5 0.5 %collective-permute-start = (f32[1424,128]{1,0:T(8,128)S(1)}, f32[1424,128]{1,0:T(8,128)S(1)}, u32[]{:S(2)}, u32[]{:S(2)}) collective-permute-start(f32[1424,128]{1,0:T(8,128)S(1)} %get-tuple-element.11), channel_id=1, source_target_pairs={{0,4},{4,0},{1,5},{5,1},{2,6},{6,2},{3,7},{7,3},{8,12},{12,8},{9,1... | collective-permute-start | bytes 2187272 | tf_op jit(solution)/shard_map/ppermute | solution.py:416
  3.0 0.0 copy-start.1
  3.0 4.5 %collective-permute-start.1 = (f32[280,128]{1,0:T(8,128)S(1)}, f32[280,128]{1,0:T(8,128)S(1)}, u32[]{:S(2)}, u32[]{:S(2)}) collective-permute-start(f32[280,128]{1,0:T(8,128)S(1)} %get-tuple-element.12), channel_id=1, source_target_pairs={{0,8},{8,16},{16,24},{12,4},{20,12},{28,20},{1,9},{9,17},{17,25},{... | collective-permute-start | bytes 430088 | tf_op jit(solution)/shard_map/ppermute | solution.py:417
  7.5 0.7 %collective-permute-start.2 = (f32[280,128]{1,0:T(8,128)S(1)}, f32[280,128]{1,0:T(8,128)S(1)}, u32[]{:S(2)}, u32[]{:S(2)}) collective-permute-start(f32[280,128]{1,0:T(8,128)S(1)} %get-tuple-element.13), channel_id=1, source_target_pairs={{4,8},{12,16},{20,24},{8,4},{16,12},{24,20},{5,9},{13,17},{21,25},... | collective-permute-start | bytes 430088 | tf_op jit(solution)/shard_map/ppermute | solution.py:418
  8.2 0.0 copy-done.1
  8.2 0.1 copy.10
  8.3 0.0 copy-start
  8.3 0.0 collective-permute-done.other_ref
  8.4 0.6 %copy-done = s32[1,128]{1,0:T(1,128)S(1)} copy-done((s32[1,128]{1,0:T(1,128)S(1)}, s32[1,128]{1,0:T(1,128)}, u32[]{:S(2)}) %copy-start) | copy-done | bytes 536
  9.0 0.2 place.1.place_ref
  9.2 0.9 %collective-permute-done.1.one_ref = f32[280,128]{1,0:T(8,128)S(1)} collective-permute-done((f32[280,128]{1,0:T(8,128)S(1)}, f32[280,128]{1,0:T(8,128)S(1)}, u32[]{:S(2)}, u32[]{:S(2)}) %collective-permute-start.1) | collective-permute-done | bytes 143392 | tf_op jit(solution)/shard_map/ppermute | solution.py:417
  10.2 0.0 collective-permute-done.2.two_ref
  10.2 6.7 %steps.1 = (f32[16,32,128]{2,1,0:T(8,128)S(1)}, f32[16,32,128]{2,1,0:T(8,128)S(1)}, f32[544,128]{1,0:T(8,128)S(1)}, f32[544,128]{1,0:T(8,128)S(1)}) custom-call(f32[1416,128]{1,0:T(8,128)S(1)} %get-tuple-element.10.keep_ref, f32[1424,128]{1,0:T(8,128)S(1)} %collective-permute-done.other_ref, f32[280,128]{1,0:T(8,128)S(1)} %collective-permute-done.1.one_ref, ...), custom_call_target="tpu_custom_call" | custom-call | tf_op jit(solution)/shard_map/steps/pallas_call | solution.py:436
  16.9 3.8 %collective-permute-start.4 = (f32[544,128]{1,0:T(8,128)S(1)}, f32[544,128]{1,0:T(8,128)S(1)}, u32[]{:S(2)}, u32[]{:S(2)}) collective-permute-start(f32[544,128]{1,0:T(8,128)S(1)} %get-tuple-element.17), channel_id=1, source_target_pairs={{0,4},{4,0},{1,5},{5,1},{2,6},{6,2},{3,7},{7,3},{8,12},{12,8},{9,1... | collective-permute-start | bytes 835592 | tf_op jit(solution)/shard_map/ppermute | solution.py:462
  20.7 0.1 collective-permute-start.3
  20.8 1.1 %collective-permute-done.4 = f32[544,128]{1,0:T(8,128)S(1)} collective-permute-done((f32[544,128]{1,0:T(8,128)S(1)}, f32[544,128]{1,0:T(8,128)S(1)}, u32[]{:S(2)}, u32[]{:S(2)}) %collective-permute-start.4) | collective-permute-done | bytes 278560 | tf_op jit(solution)/shard_map/ppermute | solution.py:462
  21.9 2.0 %collective-permute-start.5 = (f32[272,128]{1,0:T(8,128)S(1)}, f32[272,128]{1,0:T(8,128)S(1)}, u32[]{:S(2)}, u32[]{:S(2)}) collective-permute-start(f32[272,128]{1,0:T(8,128)S(1)} %slice.21), channel_id=1, source_target_pairs={{0,8},{8,16},{16,24},{24,0},{12,4},{20,12},{28,20},{4,28},{1,9},{9... | collective-permute-start | bytes 417800 | tf_op jit(solution)/shard_map/ppermute | solution.py:468
  24.0 1.3 %collective-permute-start.6 = (f32[136,128]{1,0:T(8,128)S(1)}, f32[136,128]{1,0:T(8,128)S(1)}, u32[]{:S(2)}, u32[]{:S(2)}) collective-permute-start(f32[136,128]{1,0:T(8,128)S(1)} %get-tuple-element.22), channel_id=1, source_target_pairs={{0,16},{8,24},{16,0},{24,8},{1,17},{9,25},{17,1},{25,9},{2,18},{10... | collective-permute-start | bytes 208904 | tf_op jit(solution)/shard_map/ppermute | solution.py:469
  25.3 5.2 %collective-permute-done.5 = f32[272,128]{1,0:T(8,128)S(1)} collective-permute-done((f32[272,128]{1,0:T(8,128)S(1)}, f32[272,128]{1,0:T(8,128)S(1)}, u32[]{:S(2)}, u32[]{:S(2)}) %collective-permute-start.5) | collective-permute-done | bytes 139296 | tf_op jit(solution)/shard_map/ppermute | solution.py:468
  30.4 0.1 collective-permute-start.7
  30.5 0.0 collective-permute-done.3
  30.5 0.9 %maximum_select_fusion = f32[1,16,64,128]{3,2,1,0:T(8,128)} fusion(f32[1,16,32,128]{3,2,1,0:T(8,128)S(1)} %bitcast.14, f32[1,16,32,128]{3,2,1,0:T(8,128)S(1)} %bitcast.9, pred[]{:T(512)S(6)} %eq.3), kind=kLoop, calls=%fused_computation | loop fusion | flops 393216 | bytes 1048577 | tf_op jit(solution)/shard_map/jit(_where)/select_n | solution.py:488
  31.4 0.8 %collective-permute-done.6.far_ref = f32[136,128]{1,0:T(8,128)S(1)} collective-permute-done((f32[136,128]{1,0:T(8,128)S(1)}, f32[136,128]{1,0:T(8,128)S(1)}, u32[]{:S(2)}, u32[]{:S(2)}) %collective-permute-start.6) | collective-permute-done | bytes 69664 | tf_op jit(solution)/shard_map/ppermute | solution.py:469
  32.2 0.0 collective-permute-done.7.swapped_ref
  32.2 0.7 %gather.1 = f32[544,128]{1,0:T(8,128)} custom-call(f32[136,128]{1,0:T(8,128)S(1)} %get-tuple-element.23.own_ref, f32[136,128]{1,0:T(8,128)S(1)} %get-tuple-element.25.near_ref, f32[136,128]{1,0:T(8,128)S(1)} %collective-permute-done.6.far_ref, f32[136,128]{1,0:T(8,128)S(1)} %collective-permute-done.7.swapped_ref), custom_call_target="tpu_custom_call" | custom-call | tf_op jit(solution)/shard_map/gather/pallas_call | solution.py:473
  (4 shorter events, 0.1 us)
Async XLA Ops:
  2.5 5.8 %collective-permute-start = (f32[1424,128]{1,0:T(8,128)S(1)}, f32[1424,128]{1,0:T(8,128)S(1)}, u32[]{:S(2)}, u32[]{:S(2)}) collective-permute-start(f32[1424,128]{1,0:T(8,128)S(1)} %get-tuple-element.11), channel_id=1, source_target_pairs={{0,4},{4,0},{1,5},{5,1},{2,6},{6,2},{3,7},{7,3},{8,12},{12,8},{9,1... | collective-permute-start | bytes 2187272 | tf_op jit(solution)/shard_map/ppermute | solution.py:416
  3.0 5.2 %copy-start.1 = (s32[1,512]{1,0:T(1,128)S(1)}, s32[1,512]{1,0:T(1,128)}, u32[]{:S(2)}) copy-start(s32[1,512]{1,0:T(1,128)} %param.12) | copy-start | bytes 6148
  3.0 7.1 %collective-permute-start.1 = (f32[280,128]{1,0:T(8,128)S(1)}, f32[280,128]{1,0:T(8,128)S(1)}, u32[]{:S(2)}, u32[]{:S(2)}) collective-permute-start(f32[280,128]{1,0:T(8,128)S(1)} %get-tuple-element.12), channel_id=1, source_target_pairs={{0,8},{8,16},{16,24},{12,4},{20,12},{28,20},{1,9},{9,17},{17,25},{... | collective-permute-start | bytes 430088 | tf_op jit(solution)/shard_map/ppermute | solution.py:417
  7.5 2.6 %collective-permute-start.2 = (f32[280,128]{1,0:T(8,128)S(1)}, f32[280,128]{1,0:T(8,128)S(1)}, u32[]{:S(2)}, u32[]{:S(2)}) collective-permute-start(f32[280,128]{1,0:T(8,128)S(1)} %get-tuple-element.13), channel_id=1, source_target_pairs={{4,8},{12,16},{20,24},{8,4},{16,12},{24,20},{5,9},{13,17},{21,25},... | collective-permute-start | bytes 430088 | tf_op jit(solution)/shard_map/ppermute | solution.py:418
  8.3 0.7 %copy-start = (s32[1,128]{1,0:T(1,128)S(1)}, s32[1,128]{1,0:T(1,128)}, u32[]{:S(2)}) copy-start(s32[1,128]{1,0:T(1,128)} %own_ref.1) | copy-start | bytes 1540
  16.9 5.0 %collective-permute-start.4 = (f32[544,128]{1,0:T(8,128)S(1)}, f32[544,128]{1,0:T(8,128)S(1)}, u32[]{:S(2)}, u32[]{:S(2)}) collective-permute-start(f32[544,128]{1,0:T(8,128)S(1)} %get-tuple-element.17), channel_id=1, source_target_pairs={{0,4},{4,0},{1,5},{5,1},{2,6},{6,2},{3,7},{7,3},{8,12},{12,8},{9,1... | collective-permute-start | bytes 835592 | tf_op jit(solution)/shard_map/ppermute | solution.py:462
  20.7 9.8 %collective-permute-start.3 = (f32[16,32,128]{2,1,0:T(8,128)S(1)}, f32[16,32,128]{2,1,0:T(8,128)S(1)}, u32[]{:S(2)}, u32[]{:S(2)}) collective-permute-start(f32[16,32,128]{2,1,0:T(8,128)S(1)} %get-tuple-element.15), channel_id=1, source_target_pairs={{0,4},{4,0},{1,5},{5,1},{2,6},{6,2},{3,7},{7,3},{8,12},{12,8},{9,1... | collective-permute-start | bytes 786440 | tf_op jit(solution)/shard_map/ppermute | solution.py:487
  21.9 8.5 %collective-permute-start.5 = (f32[272,128]{1,0:T(8,128)S(1)}, f32[272,128]{1,0:T(8,128)S(1)}, u32[]{:S(2)}, u32[]{:S(2)}) collective-permute-start(f32[272,128]{1,0:T(8,128)S(1)} %slice.21), channel_id=1, source_target_pairs={{0,8},{8,16},{16,24},{24,0},{12,4},{20,12},{28,20},{4,28},{1,9},{9... | collective-permute-start | bytes 417800 | tf_op jit(solution)/shard_map/ppermute | solution.py:468
  24.0 8.2 %collective-permute-start.6 = (f32[136,128]{1,0:T(8,128)S(1)}, f32[136,128]{1,0:T(8,128)S(1)}, u32[]{:S(2)}, u32[]{:S(2)}) collective-permute-start(f32[136,128]{1,0:T(8,128)S(1)} %get-tuple-element.22), channel_id=1, source_target_pairs={{0,16},{8,24},{16,0},{24,8},{1,17},{9,25},{17,1},{25,9},{2,18},{10... | collective-permute-start | bytes 208904 | tf_op jit(solution)/shard_map/ppermute | solution.py:469
  30.4 1.7 %collective-permute-start.7 = (f32[136,128]{1,0:T(8,128)S(1)}, f32[136,128]{1,0:T(8,128)S(1)}, u32[]{:S(2)}, u32[]{:S(2)}) collective-permute-start(f32[136,128]{1,0:T(8,128)S(1)} %get-tuple-element.24), channel_id=1, source_target_pairs={{0,4},{4,0},{1,5},{5,1},{2,6},{6,2},{3,7},{7,3},{8,12},{12,8},{9,1... | collective-permute-start | bytes 208904 | tf_op jit(solution)/shard_map/ppermute | solution.py:472

commit v6 on v5

v6 whole, which is shorter than its diff:
```python
import functools

import jax
import jax.numpy as jnp
from jax import lax
from jax.experimental import pallas as pl
from jax.experimental.pallas import tpu as pltpu
from jax.sharding import PartitionSpec as P

STEPS = 8
SUB = 8
VMEM = pltpu.VMEM


def lanes_of(shape):
    return lax.broadcasted_iota(jnp.int32, shape, len(shape) - 1)


def rows_of(shape):
    return lax.broadcasted_iota(jnp.int32, shape, len(shape) - 2)


def edges_kernel(
    p_hbm, fa_hbm, fc_hbm, depth_hbm, stiff_hbm, owner_hbm, ids_hbm,
    keep_ref, send_ref, one_ref, two_ref, ids_ref, owners_ref,
    p_ref, fa_ref, fc_ref, depth_ref, stiff_ref, owner_ref, sems,
):
    copies = [
        pltpu.make_async_copy(source, target, sems.at[i])
        for i, (source, target) in enumerate(
            (
                (depth_hbm, depth_ref),
                (stiff_hbm, stiff_ref),
                (owner_hbm, owner_ref),
                (ids_hbm, ids_ref),
                (fa_hbm, fa_ref),
                (fc_hbm, fc_ref),
                (p_hbm, p_ref),
            )
        )
    ]
    for copy in copies:
        copy.start()
    for copy in copies:
        copy.wait()
    layers, rows, cols = p_ref.shape
    low = lax.axis_index("cross") == 0
    span = rows // 2 + SUB
    last = rows - SUB
    lane = lanes_of((rows, cols))
    row = rows_of((rows, cols))
    row_sub = rows_of((SUB, cols))
    depth = depth_ref[...]
    stiff = stiff_ref[...]
    first_lane = lane == 0
    slot_one = row_sub == jnp.where(low, 0, -1)
    slot_two = row_sub == jnp.where(low, -1, 0)
    base = 2 * span * layers
    base_z = 2 * SUB * layers
    velocity = jnp.zeros((rows, cols), jnp.float32)

    def halves(array):
        first, second = array[:span], array[rows - span :]
        return jnp.where(low, first, second), jnp.where(low, second, first)

    def ends(array):
        first, second = array[:SUB], array[last:]
        return jnp.where(low, second, first), jnp.where(low, first, second)

    for z in range(layers):
        wet = depth > z
        p = p_ref[z]
        va = jnp.where(wet, fa_ref[z], 0.0)
        vc = jnp.where(wet, fc_ref[z], 0.0)
        behind = jnp.where(row == 0, 0.0, pltpu.roll(va, 1, 0))
        before = jnp.where(first_lane, 0.0, pltpu.roll(vc, 1, 1))
        w = (va - behind) + (vc - before)
        velocity = jnp.where(lane == z, pltpu.roll(vc, z + 1, 1), velocity)
        at = 2 * span * z
        keep_ref[at : at + span], send_ref[at : at + span] = halves(p)
        at += span
        keep_ref[at : at + span], send_ref[at : at + span] = halves(w)
        final = va[rows - 1 : rows]
        at = base + 3 * span + z
        keep_ref[at : at + 1] = final
        send_ref[at : at + 1] = final
        at = 2 * SUB * z
        one_ref[at : at + SUB], two_ref[at : at + SUB] = ends(p)
        at += SUB
        one, two = ends(w)
        final = jnp.broadcast_to(final, (SUB, cols))
        one_ref[at : at + SUB] = jnp.where(slot_one, final, one)
        two_ref[at : at + SUB] = jnp.where(slot_two, final, two)
    for i, array in enumerate((depth.astype(jnp.float32), stiff, velocity)):
        at = base + span * i
        keep_ref[at : at + span], send_ref[at : at + span] = halves(array)
        at = base_z + SUB * i
        one_ref[at : at + SUB], two_ref[at : at + SUB] = ends(array)
    at = base + 3 * span + layers
    owners = jnp.broadcast_to(owner_ref[...].astype(jnp.float32), (SUB, cols))
    owners_ref[...] = owners
    send_ref[at : at + SUB] = owners


def place_kernel(ids_ref, own_ref, other_ref, place_ref, *, owner_count, chips, capacity):
    along = lax.axis_index("along")
    cross = lax.axis_index("cross")
    low = cross == 0
    cores = owner_count // chips
    patches = own_ref.shape[1]
    last = other_ref.shape[0] - SUB
    own = own_ref[0:1]
    other = other_ref[last : last + 1]
    owners = [jnp.where(low, own, other), jnp.where(low, other, own)]
    lane = lanes_of((patches, patches))
    half = patches // 2
    block = lane // half
    within = lane % half
    held = half // 2
    turn = (held - SUB) * cross
    patch = half * cross + 2 * lax.rem(within % held + turn, held) + within // held
    source = rows_of((patches, patches))
    number = rows_of((owner_count, patches)).astype(jnp.float32)
    chosen = jnp.zeros((owner_count, patches), jnp.float32)
    counts = jnp.zeros((owner_count, patches), jnp.float32)
    for i in range(2):
        owned = (number == owners[i]).astype(jnp.bfloat16)
        pick = jnp.where(block == i, jnp.where(source == patch, 1.0, 0.0), 0.0).astype(jnp.bfloat16)
        earlier = jnp.where(block == i, jnp.where(source < patch, 1.0, 0.0), 0.0).astype(jnp.bfloat16)
        chosen += jnp.dot(owned, pick, preferred_element_type=jnp.float32)
        counts += jnp.dot(owned, earlier, preferred_element_type=jnp.float32)
    rank = jnp.sum(chosen * counts, axis=0, keepdims=True).astype(jnp.int32)
    owner = jnp.sum(chosen * number, axis=0, keepdims=True).astype(jnp.int32)
    wanted = (along * cores + block) * patches + patch
    found = jnp.zeros((patches, patches), jnp.float32)
    for j in range(ids_ref.shape[1]):
        found = jnp.where(ids_ref[:, j : j + 1] == wanted, 1.0, found)
    member = jnp.sum(found, axis=0, keepdims=True)
    block = block[:1]
    chip = owner // cores
    owner_core = owner % cores
    some = 2 * capacity
    slot = block * capacity + rank
    if chips == 4:
        ahead = lax.rem(chip - along + chips, chips)
        slot = slot + ahead * some
    else:
        slot = slot + chip * some
    handler = owner_core
    slot = jnp.where(handler == cross, slot, slot + chips * some)
    slot = jnp.where(member > 0.0, slot, -1)
    place_ref[...] = jnp.where(rows_of(place_ref.shape) == slot, 1.0, 0.0).astype(jnp.bfloat16)


def gather_kernel(own_ref, one_ref, two_ref, three_ref, out_ref, sems):
    chips = 4
    along = lax.axis_index("along")
    count = out_ref.shape[0] // chips
    copies = []
    for i, (ref, ahead) in enumerate(
        ((own_ref, 0), (one_ref, 3), (two_ref, 2), (three_ref, 1))
    ):
        at = pl.multiple_of(lax.rem(along + ahead, chips) * count, SUB)
        copies.append(pltpu.make_async_copy(ref, out_ref.at[pl.ds(at, count)], sems.at[i]))
    for copy in copies:
        copy.start()
    for copy in copies:
        copy.wait()


ZB = 4


def masks(depth, stiff, d_buf, wet_buf, scale_buf, half_buf, tile):
    layers = wet_buf.shape[1]
    zeros = jnp.zeros((SUB, depth.shape[1]), jnp.float32)
    d_buf[tile] = depth
    for z in range(layers):
        wet = depth > float(z)
        wet_buf[tile, z, :SUB] = zeros
        wet_buf[tile, z, SUB:] = jnp.where(wet, 1.0, 0.0)
        scale_buf[tile, z] = jnp.where(wet, stiff, 0.0)
        if z > 0:
            half_buf[tile, z - 1] = jnp.where(wet, 0.5, 0.0)


def advance(p_buf, w_buf, d_buf, wet_buf, scale_buf, half_buf, p_two, w_two, trace, kept):
    layers = p_buf.shape[1]
    wide, cols = w_buf.shape[2:]
    groups = layers // ZB
    lane = lanes_of((ZB, wide, cols))
    last_lane = lane == cols - 1
    first_lane = lane == 0
    zeros = jnp.zeros((SUB, cols), jnp.float32)
    for tile in range(2):
        for z in range(layers):
            for buf in (p_buf, p_two):
                buf[tile, z, :SUB] = zeros
                buf[tile, z, SUB + wide :] = zeros
    here = slice(SUB, SUB + wide)
    ahead = slice(SUB + 1, SUB + 1 + wide)
    back_rows = slice(SUB - 1, SUB - 1 + wide)

    def step(t, first, p_buf, w_buf, p_out, w_out):
        def stage_a(g):
            zs = slice(g * ZB, (g + 1) * ZB)
            return [pltpu.roll(p_buf[i, zs, here], cols - 1, 2) for i in range(2)]

        def stage_b(g, turned):
            zs = slice(g * ZB, (g + 1) * ZB)
            right = [
                jnp.where(last_lane, turned[1], turned[0]),
                jnp.where(last_lane, 0.0, turned[1]),
            ]
            gy = [wet_buf[i, zs, SUB:] * (right[i] - p_buf[i, zs, here]) for i in range(2)]
            return gy, [pltpu.roll(gy[i], 1, 2) for i in range(2)]

        hz_last = [None, None]
        surface = [None, None]

        def stage_c(g, gy, back):
            zs = slice(g * ZB, (g + 1) * ZB)
            before = [
                jnp.where(first_lane, 0.0, back[0]),
                jnp.where(first_lane, back[0], back[1]),
            ]
            for i in range(2):
                p = p_buf[i, zs, here]
                w = w_buf[i, zs] - (gy[i] - before[i])
                gx = wet_buf[i, zs, SUB:] * (p_buf[i, zs, ahead] - p)
                behind = wet_buf[i, zs, SUB - 1 : SUB - 1 + wide] * (p - p_buf[i, zs, back_rows])
                w = w - (gx - behind)
                w_out[i, zs] = w
                if g + 1 < groups:
                    hz = half_buf[i, zs] * (p_buf[i, g * ZB + 1 : (g + 1) * ZB + 1, here] - p)
                elif ZB > 1:
                    hz = jnp.concatenate([half_buf[i, g * ZB :] * (p[1:] - p[:-1]), jnp.zeros((1, wide, cols), jnp.float32)], 0)
                else:
                    hz = jnp.zeros((1, wide, cols), jnp.float32)
                prev = jnp.zeros((1, wide, cols), jnp.float32) if g == 0 else hz_last[i]
                flux = w - (hz - (jnp.concatenate([prev, hz[:-1]], 0) if ZB > 1 else prev))
                hz_last[i] = hz[-1:]
                old = wet_buf[i, zs, SUB:] * p if first else p
                new = old - scale_buf[i, zs] * flux
                p_out[i, zs, here] = new
                for k in range(ZB):
                    part = new[k, kept]
                    z = g * ZB + k
                    surface[i] = part if z == 0 else jnp.where(d_buf[i, kept] > float(z), part, surface[i])

        turned = [stage_a(0), stage_a(1)]
        ready = stage_b(0, turned[0])
        for g in range(groups):
            if g + 2 < groups:
                turned.append(stage_a(g + 2))
            coming = stage_b(g + 1, turned[g + 1]) if g + 1 < groups else None
            stage_c(g, *ready)
            ready = coming
        for i in range(2):
            trace[t, i] = surface[i]

    def two(k, carry):
        step(2 * k, False, p_buf, w_buf, p_two, w_two)
        step(2 * k + 1, False, p_two, w_two, p_buf, w_buf)
        return carry

    step(0, True, p_buf, w_buf, p_two, w_two)
    step(1, False, p_two, w_two, p_buf, w_buf)
    lax.fori_loop(1, STEPS // 2, two, 0)


def state_buffers(layers, wide, cols):
    return [
        VMEM(shape, jnp.float32)
        for shape in (
            (2, layers, wide + 2 * SUB, cols),
            (2, layers, wide, cols),
            (2, wide, cols),
            (2, layers, wide + SUB, cols),
            (2, layers, wide, cols),
            (2, layers - 1, wide, cols),
            (2, layers, wide + 2 * SUB, cols),
            (2, layers, wide, cols),
        )
    ]


def inner_kernel(keep_ref, other_ref, p_keep_ref, p_send_ref, trace_ref, *state):
    layers, inner_rows, cols = p_keep_ref.shape
    core = lax.axis_index("cross")
    low = core == 0
    span = inner_rows + 2 * SUB
    base = 2 * span * layers
    p_buf, w_buf, d_buf, wet_buf, scale_buf, half_buf, p_two, w_two = state
    lane = lanes_of((span, cols))
    at = base + 2 * span
    seam = jnp.where(low, keep_ref[at : at + span], other_ref[at : at + span])
    for tile, main_ref, seam_core in ((core, keep_ref, 1), (1 - core, other_ref, 0)):
        seam_lane = lane == jnp.where(core == seam_core, 0, -1)
        masks(
            main_ref[base : base + span],
            main_ref[base + span : base + 2 * span],
            d_buf, wet_buf, scale_buf, half_buf, tile,
        )
        for z in range(layers):
            at = 2 * span * z
            p_buf[tile, z, SUB : SUB + span] = main_ref[at : at + span]
            turned = pltpu.roll(seam, cols - z, 1) if z else seam
            w_buf[tile, z] = main_ref[at + span : at + 2 * span] - jnp.where(seam_lane, turned, 0.0)
    kept = slice(SUB, SUB + inner_rows)
    advance(p_buf, w_buf, d_buf, wet_buf, scale_buf, half_buf, p_two, w_two, trace_ref, kept)
    for z in range(layers):
        p_keep_ref[z] = p_buf[core, z, 2 * SUB : 2 * SUB + inner_rows]
        p_send_ref[z] = p_buf[1 - core, z, 2 * SUB : 2 * SUB + inner_rows]


def outer_kernel(
    keep_ref, other_ref, halo_ref, place_ref, inner_ref,
    p_keep_ref, p_send_ref, panel_keep_ref, panel_send_ref, trace, *state,
):
    layers, cols = p_keep_ref.shape[0], p_keep_ref.shape[2]
    inner_rows = inner_ref.shape[2]
    core = lax.axis_index("cross")
    low = core == 0
    span = inner_rows + 2 * SUB
    near = 2 * SUB
    base = 2 * span * layers
    base_z = 2 * SUB * layers
    ends = halo_ref.shape[0] // 2
    p_buf, w_buf, d_buf, wet_buf, scale_buf, half_buf, p_two, w_two = state
    lane = lanes_of((SUB, cols))
    row = rows_of((SUB, cols))
    offset = (span - near) * core

    def main_rows(ref, at):
        return ref[pl.ds(pl.multiple_of(at + offset, SUB), near)]

    def joined(main, halo):
        return jnp.where(
            low, jnp.concatenate([halo, main], 0), jnp.concatenate([main, halo], 0)
        )

    seam_at = base_z + 2 * SUB
    seam_halo = jnp.where(
        low, halo_ref[seam_at : seam_at + SUB], halo_ref[ends + seam_at : ends + seam_at + SUB]
    )
    seam_main = jnp.where(
        low, main_rows(keep_ref, base + 2 * span), main_rows(other_ref, base + 2 * span)
    )
    seam = joined(seam_main, seam_halo)
    top_row = row == jnp.where(low, 0, -1)
    end_row = row == jnp.where(low, -1, 0)
    wide_lane = lanes_of((near + SUB, cols))
    for tile, main_ref, end, seam_core in ((core, keep_ref, 0, 1), (1 - core, other_ref, ends, 0)):
        seam_lane = wide_lane == jnp.where(core == seam_core, 0, -1)

        def end_rows(at):
            return halo_ref[end + at : end + at + SUB]

        masks(
            joined(main_rows(main_ref, base), end_rows(base_z)),
            joined(main_rows(main_ref, base + span), end_rows(base_z + SUB)),
            d_buf, wet_buf, scale_buf, half_buf, tile,
        )
        for z in range(layers):
            at = 2 * span * z
            at_z = 2 * SUB * z
            p_buf[tile, z, SUB : 2 * SUB + near] = joined(main_rows(main_ref, at), end_rows(at_z))
            w = main_rows(main_ref, at + span)
            w_end = end_rows(at_z + SUB)
            slot = jnp.broadcast_to(w_end[0:1], (SUB, cols))
            final = base + 3 * span + z
            final = jnp.broadcast_to(main_ref[final : final + 1], (SUB, cols))
            w = jnp.concatenate([w[:SUB] - jnp.where(top_row, slot, 0.0), w[SUB:]], 0)
            w = joined(w, w_end - jnp.where(end_row, final, 0.0))
            turned = pltpu.roll(seam, cols - z, 1) if z else seam
            w_buf[tile, z] = w - jnp.where(seam_lane, turned, 0.0)
    kept = slice(SUB, 2 * SUB)
    advance(p_buf, w_buf, d_buf, wet_buf, scale_buf, half_buf, p_two, w_two, trace, kept)
    for z in range(layers):
        p_keep_ref[z] = p_buf[core, z, 2 * SUB : 3 * SUB]
        p_send_ref[z] = p_buf[1 - core, z, 2 * SUB : 3 * SUB]

    width = cols // 2
    lane_rows = lanes_of((inner_rows + SUB, cols))
    place = place_ref[...]
    count = place.shape[0] // 2
    parts = STEPS // 2
    for j in range(parts):
        pieces = []
        for i in range(2):
            one = jnp.concatenate([trace[2 * j, i], inner_ref[2 * j, i]], 0)
            two = jnp.concatenate([trace[2 * j + 1, i], inner_ref[2 * j + 1, i]], 0)
            pieces.append(jnp.where(lane_rows < width, one, pltpu.roll(two, width, 1)))
            pieces.append(jnp.where(lane_rows < width, pltpu.roll(one, width, 1), two))
        both = jnp.concatenate(pieces, 0)
        part_a = both.astype(jnp.bfloat16)
        rest = both - part_a.astype(jnp.float32)
        part_b = rest.astype(jnp.bfloat16)
        part_c = (rest - part_b.astype(jnp.float32)).astype(jnp.bfloat16)
        total = jnp.dot(place, part_a, preferred_element_type=jnp.float32)
        total += jnp.dot(place, part_b, preferred_element_type=jnp.float32)
        total += jnp.dot(place, part_c, preferred_element_type=jnp.float32)
        panel_keep_ref[pl.ds(j, count, stride=parts)] = total[:count]
        panel_send_ref[pl.ds(j, count, stride=parts)] = total[count:]


def shards(
    pressure_start, along_start, cross_start, depth_layers, stiffness, patch_lists, owner_map
):
    sensors, layers, rows, cols = pressure_start.shape
    f32 = jnp.float32
    along_count = lax.axis_size("along")
    cross_count = lax.axis_size("cross")
    low = lax.axis_index("cross") == 0
    swap = [(0, 1), (1, 0)]
    pair = ("along", "cross")
    steps_up = range(along_count - 1)
    route = [(2 * i, 2 * i + 2) for i in steps_up] + [(2 * i + 3, 2 * i + 1) for i in steps_up]
    half_rows = rows // 2
    span = half_rows + SUB
    pack_rows = 2 * span * layers + 3 * span + layers
    end_rows = 2 * SUB * layers + 3 * SUB

    spec = pl.BlockSpec(memory_space=VMEM)
    hbm = pl.BlockSpec(memory_space=pltpu.HBM)
    params = pltpu.CompilerParams(vmem_limit_bytes=32 * 1024 * 1024)
    keep, send, one, two, ids, owners = pl.pallas_call(
        edges_kernel,
        out_shape=[
            jax.ShapeDtypeStruct((pack_rows, cols), f32),
            jax.ShapeDtypeStruct((pack_rows + SUB, cols), f32),
            jax.ShapeDtypeStruct((end_rows, cols), f32),
            jax.ShapeDtypeStruct((end_rows, cols), f32),
            jax.ShapeDtypeStruct(patch_lists.shape, jnp.int32),
            jax.ShapeDtypeStruct((SUB, cols), f32),
        ],
        in_specs=[hbm] * 7,
        out_specs=[spec] * 6,
        scratch_shapes=[
            VMEM((layers, rows, cols), f32),
            VMEM((layers, rows, cols), f32),
            VMEM((layers, rows, cols), f32),
            VMEM((rows, cols), jnp.int32),
            VMEM((rows, cols), f32),
            VMEM(owner_map.shape, jnp.int32),
            pltpu.SemaphoreType.DMA((7,)),
        ],
        compiler_params=params,
        name="edges",
    )(
        *(
            pltpu.with_memory_space_constraint(x, pltpu.HBM)
            for x in (
                pressure_start[0],
                along_start[0],
                cross_start[0],
                depth_layers,
                stiffness,
                owner_map,
                patch_lists,
            )
        )
    )

    two = lax.ppermute(two, "cross", swap)
    halo = jnp.concatenate([one, two], 0)
    send = lax.optimization_barrier((send, two))[0]
    other = lax.ppermute(send, "cross", swap)
    halo = lax.ppermute(halo, pair, route)

    patch_count = 2 * rows
    owner_count = along_count * cross_count
    capacity = patch_count // owner_count + 1
    count = owner_count * capacity
    place = pl.pallas_call(
        functools.partial(
            place_kernel, owner_count=owner_count, chips=along_count, capacity=capacity
        ),
        out_shape=jax.ShapeDtypeStruct((2 * count, patch_count), jnp.bfloat16),
        in_specs=[spec] * 3,
        out_specs=spec,
        compiler_params=params,
        name="place",
    )(ids.reshape(-1, patch_count).T, owners, other)

    parts = STEPS // 2
    inner_rows = half_rows - SUB
    inner_shape = jax.ShapeDtypeStruct((layers, inner_rows, cols), f32)
    inner_keep, inner_send, inner_trace = pl.pallas_call(
        inner_kernel,
        out_shape=[
            inner_shape,
            inner_shape,
            jax.ShapeDtypeStruct((STEPS, 2, inner_rows, cols), f32),
        ],
        in_specs=[spec] * 2,
        out_specs=[spec] * 3,
        scratch_shapes=state_buffers(layers, span, cols),
        compiler_params=params,
        cost_estimate=pl.CostEstimate(
            flops=400 * layers * span * cols,
            bytes_accessed=200 * layers * span * cols,
            transcendentals=0,
        ),
        name="inner",
    )(keep, other)
    outer_shape = jax.ShapeDtypeStruct((layers, SUB, cols), f32)
    panel_shape = jax.ShapeDtypeStruct((count * parts, cols), f32)
    outer_keep, outer_send, panel_keep, panel_send = pl.pallas_call(
        outer_kernel,
        out_shape=[outer_shape, outer_shape, panel_shape, panel_shape],
        in_specs=[spec] * 5,
        out_specs=[spec] * 4,
        scratch_shapes=[VMEM((STEPS, 2, SUB, cols), f32)] + state_buffers(layers, 3 * SUB, cols),
        compiler_params=params,
        name="outer",
    )(keep, other, halo, place, inner_trace)

    panels = panel_keep + lax.ppermute(panel_send, "cross", swap)
    if along_count == 4:
        some = 2 * capacity * parts
        ring = range(along_count)
        pieces = [panels[:some]]
        for k in range(1, along_count):
            pieces.append(
                lax.ppermute(
                    panels[k * some : (k + 1) * some],
                    "along",
                    [(i, (i + k) % along_count) for i in ring],
                )
            )
        received = pl.pallas_call(
            gather_kernel,
            out_shape=jax.ShapeDtypeStruct((count * parts, cols), f32),
            in_specs=[spec] * 4,
            out_specs=hbm,
            scratch_shapes=[pltpu.SemaphoreType.DMA((4,))],
            compiler_params=params,
            name="gather",
        )(*pieces)
    else:
        panels = panels.reshape(along_count, 2 * capacity * parts, cols)
        received = lax.all_to_all(panels, "along", split_axis=0, concat_axis=0, tiled=True)
    received = received.reshape(1, count, 1, parts * cols)

    inner_other = lax.ppermute(inner_send, "cross", swap)
    outer_other = lax.ppermute(outer_send, "cross", swap)
    pressure = jnp.where(
        low,
        jnp.concatenate([outer_keep, inner_keep, inner_other, outer_other], 1),
        jnp.concatenate([outer_other, inner_other, inner_keep, outer_keep], 1),
    )
    return (pressure[None], received)


def solution(mesh):
    in_specs = (
        P("batch", None, "along", "cross"),
        P("batch", None, "along", "cross"),
        P("batch", None, "along", "cross"),
        P("along", "cross"),
        P("along", "cross"),
        P("batch", None),
        P(("along", "cross"), None),
    )
    out_specs = (P("batch", None, "along", "cross"), P(("along", "cross"), None, "batch", None))
    return jax.shard_map(shards, mesh=mesh, in_specs=in_specs, out_specs=out_specs, check_vma=False)
```

time: 33.1 us -> 30.1 us (0.909)
  waiting for transfers between devices: 7.99 us -> 4.82 us
  Pallas kernels: 9.52 us -> 11.6 us
  starting transfers between devices: 13 us -> 11.7 us
  local copies, waits for them, and re-layouts: 0.79 us -> 0.13 us
    ppermute x1, starting transfers between devices: 3.82 us -> 0.07 us  [shards(): panels = panel_keep + lax.ppermute(panel_send, 'cross', swap)]
    ppermute x6 -> x7, waiting for transfers between devices: 6.89 us -> 3.86 us  [the longest x3 2.85 us: shards(): lax.ppermute(panels[k * some:(k + 1) * some], 'along', [(i, (i + k) % alo...]
    ppermute x6 -> x7, starting transfers between devices: 8.65 us -> 11.3 us  [the longest x3 5.55 us: shards(): lax.ppermute(panels[k * some:(k + 1) * some], 'along', [(i, (i + k) % alo...]
    pallas_call x1 -> x2, Pallas kernels: 6.71 us -> 8.8 us  [the longest x1 4.95 us: shards(): pl.pallas_call(inner_kernel, out_shape=[inner_shape, inner_shape, jax.Sha...]
    unnamed x4 -> x0, local copies, waits for them, and re-layouts: 0.64 us -> none
  transfers between devices with their start and end apart: 8 -> 9, of which waited for: 4 -> 4; matrix products, arithmetic and copies ran while one was open for 3% -> 3% of each run, Pallas kernels for 1% -> 17%
where the time goes in v6:
time: 30.1 us; the launch traced here: 29.9 us
  starting transfers between devices  11.7 us (39%)
  Pallas kernels  11.6 us (39%)
  waiting for transfers between devices  4.82 us (16%)
  other arithmetic  0.89 us (3%)
  between operations  0.72 us (2%)
    ppermute x3, starting transfers between devices, shards(): lax.ppermute(panels[k * some:(k + 1) * some], 'along', [(i, (i + k) % alo...  5.55 us
    pallas_call x1, Pallas kernels, shards(): pl.pallas_call(inner_kernel, out_shape=[inner_shape, inner_shape, jax.Sha...  4.95 us
    ppermute x1, starting transfers between devices, shards(): halo = lax.ppermute(halo, pair, route)  4.64 us
    pallas_call x1, Pallas kernels, shards(): pl.pallas_call(outer_kernel, out_shape=[outer_shape, outer_shape, panel_s...  3.85 us
    ppermute x3, waiting for transfers between devices, shards(): lax.ppermute(panels[k * some:(k + 1) * some], 'along', [(i, (i + k) % alo...  2.85 us
    pallas_call x1, Pallas kernels, shards(): pl.pallas_call(edges_kernel, out_shape=[jax.ShapeDtypeStruct((pack_rows,...  1.89 us
    ppermute x1, waiting for transfers between devices, shards(): two = lax.ppermute(two, 'cross', swap)  1 us
    ppermute x1, waiting for transfers between devices, shards(): panels = panel_keep + lax.ppermute(panel_send, 'cross', swap)  0.96 us
  transfers between devices with their start and end apart: 9, of which 4 were waited for; matrix products, arithmetic and copies ran while one was open for 3% of the time, Pallas kernels for 17%

profile of v6, /device:TPU:0, one launch (start us, length us, event | category | flops | bytes accessed | tf_op | source)
XLA Modules:
  0.0 29.9 jit_solution(7839816957687390494)
XLA Ops:
  0.6 1.9 %edges.1 = (f32[1416,128]{1,0:T(8,128)S(1)}, f32[1424,128]{1,0:T(8,128)S(1)}, f32[280,128]{1,0:T(8,128)S(1)}, f32[280,128]{1,0:T(8,128)S(1)}, s32[1,512]{1,0:T(1,128)S(1)}, /*index=5*/f32[8,128]{1,0:T(8,128)S(1)}) custom-call(f32[16,64,128]{2,1,0:T(8,128)} %bitcast.14, f32[16,64,128]{2,1,0:T(8,128)} %bitcast.15, f32[16,64,128]{2,1,0:T(8,128)} %bitcast.16, ...), custom_call_target="tpu_custom_call" | custom-call | tf_op jit(solution)/shard_map/edges/pallas_call | solution.py:428
  2.5 0.5 %collective-permute-start = (f32[280,128]{1,0:T(8,128)S(1)}, f32[280,128]{1,0:T(8,128)S(1)}, u32[]{:S(2)}, u32[]{:S(2)}) collective-permute-start(f32[280,128]{1,0:T(8,128)S(1)} %get-tuple-element.18), channel_id=1, source_target_pairs={{0,4},{4,0},{1,5},{5,1},{2,6},{6,2},{3,7},{7,3},{8,12},{12,8},{9,1... | collective-permute-start | bytes 430088 | tf_op jit(solution)/shard_map/ppermute | solution.py:466
  3.0 1.0 %collective-permute-done = f32[280,128]{1,0:T(8,128)S(1)} collective-permute-done((f32[280,128]{1,0:T(8,128)S(1)}, f32[280,128]{1,0:T(8,128)S(1)}, u32[]{:S(2)}, u32[]{:S(2)}) %collective-permute-start) | collective-permute-done | bytes 143392 | tf_op jit(solution)/shard_map/ppermute | solution.py:466
  4.1 0.4 %collective-permute-start.1 = (f32[1424,128]{1,0:T(8,128)S(1)}, f32[1424,128]{1,0:T(8,128)S(1)}, u32[]{:S(2)}, u32[]{:S(2)}) collective-permute-start(f32[1424,128]{1,0:T(8,128)S(1)} %get-tuple-element.19), channel_id=1, source_target_pairs={{0,4},{4,0},{1,5},{5,1},{2,6},{6,2},{3,7},{7,3},{8,12},{12,8},{9,1... | collective-permute-start | bytes 2187272 | tf_op jit(solution)/shard_map/ppermute | solution.py:469
  4.4 4.6 %collective-permute-start.2 = (f32[560,128]{1,0:T(8,128)S(1)}, f32[560,128]{1,0:T(8,128)S(1)}, u32[]{:S(2)}, u32[]{:S(2)}) collective-permute-start(f32[560,128]{1,0:T(8,128)S(1)} %pad_maximum_fusion), channel_id=1, source_target_pairs={{0,8},{8,16},{16,24},{12,4},{20,12},{28,20},{1,9},{9,17},{17,25},{... | collective-permute-start | bytes 860168 | tf_op jit(solution)/shard_map/ppermute | solution.py:470
  9.1 0.1 copy.10
  9.2 0.0 collective-permute-done.1.other_ref
  9.2 0.2 place.1.place_ref
  9.4 4.9 %inner.1 = (f32[16,24,128]{2,1,0:T(8,128)S(1)}, f32[16,24,128]{2,1,0:T(8,128)S(1)}, f32[8,2,24,128]{3,2,1,0:T(8,128)S(1)}) custom-call(f32[1416,128]{1,0:T(8,128)S(1)} %get-tuple-element.16.keep_ref, f32[1424,128]{1,0:T(8,128)S(1)} %collective-permute-done.1.other_ref), custom_call_target="tpu_custom_call" | custom-call | flops 32768000 | bytes 16384000 | tf_op jit(solution)/shard_map/inner/pallas_call | solution.py:490
  14.4 0.0 collective-permute-done.2.halo_ref
  14.4 3.8 %outer.1 = (f32[16,8,128]{2,1,0:T(8,128)S(1)}, f32[16,8,128]{2,1,0:T(8,128)S(1)}, f32[544,128]{1,0:T(8,128)S(1)}, f32[544,128]{1,0:T(8,128)S(1)}) custom-call(f32[1416,128]{1,0:T(8,128)S(1)} %get-tuple-element.16.keep_ref, f32[1424,128]{1,0:T(8,128)S(1)} %collective-permute-done.1.other_ref, f32[560,128]{1,0:T(8,128)S(1)} %collective-permute-done.2.halo_ref, ...), custom_call_target="tpu_custom_call" | custom-call | tf_op jit(solution)/shard_map/outer/pallas_call | solution.py:510
  18.2 0.1 collective-permute-start.5
  18.3 0.5 %collective-permute-start.4 = (f32[16,8,128]{2,1,0:T(8,128)S(1)}, f32[16,8,128]{2,1,0:T(8,128)S(1)}, u32[]{:S(2)}, u32[]{:S(2)}) collective-permute-start(f32[16,8,128]{2,1,0:T(8,128)S(1)} %get-tuple-element.27), channel_id=1, source_target_pairs={{0,4},{4,0},{1,5},{5,1},{2,6},{6,2},{3,7},{7,3},{8,12},{12,8},{9,1... | collective-permute-start | bytes 196616 | tf_op jit(solution)/shard_map/ppermute | solution.py:548
  18.8 0.1 collective-permute-start.3
  18.9 1.0 %collective-permute-done.5 = f32[544,128]{1,0:T(8,128)S(1)} collective-permute-done((f32[544,128]{1,0:T(8,128)S(1)}, f32[544,128]{1,0:T(8,128)S(1)}, u32[]{:S(2)}, u32[]{:S(2)}) %collective-permute-start.5) | collective-permute-done | bytes 278560 | tf_op jit(solution)/shard_map/ppermute | solution.py:520
  19.9 1.6 %collective-permute-start.6 = (f32[136,128]{1,0:T(8,128)S(1)}, f32[136,128]{1,0:T(8,128)S(1)}, u32[]{:S(2)}, u32[]{:S(2)}) collective-permute-start(f32[136,128]{1,0:T(8,128)S(1)} %get-tuple-element.36), channel_id=1, source_target_pairs={{0,8},{8,16},{16,24},{24,0},{1,9},{9,17},{17,25},{25,1},{2,10},{10... | collective-permute-start | bytes 208904 | tf_op jit(solution)/shard_map/ppermute | solution.py:527
  21.5 2.3 %collective-permute-start.7 = (f32[136,128]{1,0:T(8,128)S(1)}, f32[136,128]{1,0:T(8,128)S(1)}, u32[]{:S(2)}, u32[]{:S(2)}) collective-permute-start(f32[136,128]{1,0:T(8,128)S(1)} %get-tuple-element.35), channel_id=1, source_target_pairs={{0,16},{8,24},{16,0},{24,8},{1,17},{9,25},{17,1},{25,9},{2,18},{10... | collective-permute-start | bytes 208904 | tf_op jit(solution)/shard_map/ppermute | solution.py:527
  23.9 1.6 %collective-permute-start.8 = (f32[136,128]{1,0:T(8,128)S(1)}, f32[136,128]{1,0:T(8,128)S(1)}, u32[]{:S(2)}, u32[]{:S(2)}) collective-permute-start(f32[136,128]{1,0:T(8,128)S(1)} %get-tuple-element.34), channel_id=1, source_target_pairs={{0,24},{8,0},{16,8},{24,16},{1,25},{9,1},{17,9},{25,17},{2,26},{10... | collective-permute-start | bytes 208904 | tf_op jit(solution)/shard_map/ppermute | solution.py:527
  25.5 0.0 collective-permute-done.4
  25.5 0.0 collective-permute-done.3
  25.5 0.8 %maximum_select_fusion = f32[1,16,64,128]{3,2,1,0:T(8,128)} fusion(f32[1,16,8,128]{3,2,1,0:T(8,128)S(1)} %bitcast.19, f32[1,16,24,128]{3,2,1,0:T(8,128)S(1)} %bitcast.18, f32[1,16,24,128]{3,2,1,0:T(8,128)S(1)} %bitcast.11, f32[1,16,8,128]{3,2,1,0:T(8,128)S(1)} %bitcast.12, pred[]{:T(512)S(6)} %eq.3), kind=kLoop, calls=%fused_computation | loop fusion | flops 917504 | bytes 1048577 | tf_op jit(solution)/shard_map/jit(_where)/select_n | solution.py:549
  26.3 0.0 collective-permute-done.6.one_ref
  26.4 2.7 %collective-permute-done.7.two_ref = f32[136,128]{1,0:T(8,128)S(1)} collective-permute-done((f32[136,128]{1,0:T(8,128)S(1)}, f32[136,128]{1,0:T(8,128)S(1)}, u32[]{:S(2)}, u32[]{:S(2)}) %collective-permute-start.7) | collective-permute-done | bytes 69664 | tf_op jit(solution)/shard_map/ppermute | solution.py:527
  29.1 0.1 collective-permute-done.8.three_ref
  29.2 0.7 %gather.1 = f32[544,128]{1,0:T(8,128)} custom-call(f32[136,128]{1,0:T(8,128)S(1)} %get-tuple-element.37.own_ref, f32[136,128]{1,0:T(8,128)S(1)} %collective-permute-done.6.one_ref, f32[136,128]{1,0:T(8,128)S(1)} %collective-permute-done.7.two_ref, f32[136,128]{1,0:T(8,128)S(1)} %collective-permute-done.8.three_ref), custom_call_target="tpu_custom_call" | custom-call | tf_op jit(solution)/shard_map/gather/pallas_call | solution.py:533
  (3 shorter events, 0.1 us)
Async XLA Ops:
  2.5 1.5 %collective-permute-start = (f32[280,128]{1,0:T(8,128)S(1)}, f32[280,128]{1,0:T(8,128)S(1)}, u32[]{:S(2)}, u32[]{:S(2)}) collective-permute-start(f32[280,128]{1,0:T(8,128)S(1)} %get-tuple-element.18), channel_id=1, source_target_pairs={{0,4},{4,0},{1,5},{5,1},{2,6},{6,2},{3,7},{7,3},{8,12},{12,8},{9,1... | collective-permute-start | bytes 430088 | tf_op jit(solution)/shard_map/ppermute | solution.py:466
  4.1 5.2 %collective-permute-start.1 = (f32[1424,128]{1,0:T(8,128)S(1)}, f32[1424,128]{1,0:T(8,128)S(1)}, u32[]{:S(2)}, u32[]{:S(2)}) collective-permute-start(f32[1424,128]{1,0:T(8,128)S(1)} %get-tuple-element.19), channel_id=1, source_target_pairs={{0,4},{4,0},{1,5},{5,1},{2,6},{6,2},{3,7},{7,3},{8,12},{12,8},{9,1... | collective-permute-start | bytes 2187272 | tf_op jit(solution)/shard_map/ppermute | solution.py:469
  4.4 9.9 %collective-permute-start.2 = (f32[560,128]{1,0:T(8,128)S(1)}, f32[560,128]{1,0:T(8,128)S(1)}, u32[]{:S(2)}, u32[]{:S(2)}) collective-permute-start(f32[560,128]{1,0:T(8,128)S(1)} %pad_maximum_fusion), channel_id=1, source_target_pairs={{0,8},{8,16},{16,24},{12,4},{20,12},{28,20},{1,9},{9,17},{17,25},{... | collective-permute-start | bytes 860168 | tf_op jit(solution)/shard_map/ppermute | solution.py:470
  18.2 1.6 %collective-permute-start.5 = (f32[544,128]{1,0:T(8,128)S(1)}, f32[544,128]{1,0:T(8,128)S(1)}, u32[]{:S(2)}, u32[]{:S(2)}) collective-permute-start(f32[544,128]{1,0:T(8,128)S(1)} %get-tuple-element.29), channel_id=1, source_target_pairs={{0,4},{4,0},{1,5},{5,1},{2,6},{6,2},{3,7},{7,3},{8,12},{12,8},{9,1... | collective-permute-start | bytes 835592 | tf_op jit(solution)/shard_map/ppermute | solution.py:520
  18.3 7.2 %collective-permute-start.4 = (f32[16,8,128]{2,1,0:T(8,128)S(1)}, f32[16,8,128]{2,1,0:T(8,128)S(1)}, u32[]{:S(2)}, u32[]{:S(2)}) collective-permute-start(f32[16,8,128]{2,1,0:T(8,128)S(1)} %get-tuple-element.27), channel_id=1, source_target_pairs={{0,4},{4,0},{1,5},{5,1},{2,6},{6,2},{3,7},{7,3},{8,12},{12,8},{9,1... | collective-permute-start | bytes 196616 | tf_op jit(solution)/shard_map/ppermute | solution.py:548
  18.8 6.7 %collective-permute-start.3 = (f32[16,24,128]{2,1,0:T(8,128)S(1)}, f32[16,24,128]{2,1,0:T(8,128)S(1)}, u32[]{:S(2)}, u32[]{:S(2)}) collective-permute-start(f32[16,24,128]{2,1,0:T(8,128)S(1)} %get-tuple-element.26), channel_id=1, source_target_pairs={{0,4},{4,0},{1,5},{5,1},{2,6},{6,2},{3,7},{7,3},{8,12},{12,8},{9,1... | collective-permute-start | bytes 589832 | tf_op jit(solution)/shard_map/ppermute | solution.py:547
  19.9 6.4 %collective-permute-start.6 = (f32[136,128]{1,0:T(8,128)S(1)}, f32[136,128]{1,0:T(8,128)S(1)}, u32[]{:S(2)}, u32[]{:S(2)}) collective-permute-start(f32[136,128]{1,0:T(8,128)S(1)} %get-tuple-element.36), channel_id=1, source_target_pairs={{0,8},{8,16},{16,24},{24,0},{1,9},{9,17},{17,25},{25,1},{2,10},{10... | collective-permute-start | bytes 208904 | tf_op jit(solution)/shard_map/ppermute | solution.py:527
  21.5 7.5 %collective-permute-start.7 = (f32[136,128]{1,0:T(8,128)S(1)}, f32[136,128]{1,0:T(8,128)S(1)}, u32[]{:S(2)}, u32[]{:S(2)}) collective-permute-start(f32[136,128]{1,0:T(8,128)S(1)} %get-tuple-element.35), channel_id=1, source_target_pairs={{0,16},{8,24},{16,0},{24,8},{1,17},{9,25},{17,1},{25,9},{2,18},{10... | collective-permute-start | bytes 208904 | tf_op jit(solution)/shard_map/ppermute | solution.py:527
  23.9 5.3 %collective-permute-start.8 = (f32[136,128]{1,0:T(8,128)S(1)}, f32[136,128]{1,0:T(8,128)S(1)}, u32[]{:S(2)}, u32[]{:S(2)}) collective-permute-start(f32[136,128]{1,0:T(8,128)S(1)} %get-tuple-element.34), channel_id=1, source_target_pairs={{0,24},{8,0},{16,8},{24,16},{1,25},{9,1},{17,9},{25,17},{2,26},{10... | collective-permute-start | bytes 208904 | tf_op jit(solution)/shard_map/ppermute | solution.py:527

commit v7 on v6

--- a/solution.py
+++ b/solution.py
@@ -168,9 +168,6 @@
         copy.wait()
 
 
-ZB = 4
-
-
 def masks(depth, stiff, d_buf, wet_buf, scale_buf, half_buf, tile):
     layers = wet_buf.shape[1]
     zeros = jnp.zeros((SUB, depth.shape[1]), jnp.float32)
@@ -184,7 +181,8 @@
             half_buf[tile, z - 1] = jnp.where(wet, 0.5, 0.0)
 
 
-def advance(p_buf, w_buf, d_buf, wet_buf, scale_buf, half_buf, p_two, w_two, trace, kept):
+def advance(state, before_step, after_step, ZB):
+    p_buf, w_buf, d_buf, wet_buf, scale_buf, half_buf, p_two, w_two = state
     layers = p_buf.shape[1]
     wide, cols = w_buf.shape[2:]
     groups = layers // ZB
@@ -202,6 +200,8 @@
     back_rows = slice(SUB - 1, SUB - 1 + wide)
 
     def step(t, first, p_buf, w_buf, p_out, w_out):
+        before_step(t, p_buf)
+
         def stage_a(g):
             zs = slice(g * ZB, (g + 1) * ZB)
             return [pltpu.roll(p_buf[i, zs, here], cols - 1, 2) for i in range(2)]
@@ -244,9 +244,9 @@
                 new = old - scale_buf[i, zs] * flux
                 p_out[i, zs, here] = new
                 for k in range(ZB):
-                    part = new[k, kept]
+                    part = new[k]
                     z = g * ZB + k
-                    surface[i] = part if z == 0 else jnp.where(d_buf[i, kept] > float(z), part, surface[i])
+                    surface[i] = part if z == 0 else jnp.where(d_buf[i] > float(z), part, surface[i])
 
         turned = [stage_a(0), stage_a(1)]
         ready = stage_b(0, turned[0])
@@ -257,7 +257,7 @@
             stage_c(g, *ready)
             ready = coming
         for i in range(2):
-            trace[t, i] = surface[i]
+            after_step(t, i, surface[i])
 
     def two(k, carry):
         step(2 * k, False, p_buf, w_buf, p_two, w_two)
@@ -285,7 +285,7 @@
     ]
 
 
-def inner_kernel(keep_ref, other_ref, p_keep_ref, p_send_ref, trace_ref, *state):
+def inner_kernel(keep_ref, other_ref, p_keep_ref, p_send_ref, trace_ref, border_ref, *state):
     layers, inner_rows, cols = p_keep_ref.shape
     core = lax.axis_index("cross")
     low = core == 0
@@ -307,15 +307,26 @@
             p_buf[tile, z, SUB : SUB + span] = main_ref[at : at + span]
             turned = pltpu.roll(seam, cols - z, 1) if z else seam
             w_buf[tile, z] = main_ref[at + span : at + 2 * span] - jnp.where(seam_lane, turned, 0.0)
-    kept = slice(SUB, SUB + inner_rows)
-    advance(p_buf, w_buf, d_buf, wet_buf, scale_buf, half_buf, p_two, w_two, trace_ref, kept)
+
+    def before_step(t, p_now):
+        for i in range(2):
+            for z in range(layers):
+                first, second = 2 * SUB, span - 1
+                border_ref[t, i, z : z + 1] = jnp.where(
+                    low, p_now[i, z, first : first + 1], p_now[i, z, second : second + 1]
+                )
+
+    def after_step(t, i, surface):
+        trace_ref[t, i] = surface[SUB : SUB + inner_rows]
+
+    advance(state, before_step, after_step, 4)
     for z in range(layers):
         p_keep_ref[z] = p_buf[core, z, 2 * SUB : 2 * SUB + inner_rows]
         p_send_ref[z] = p_buf[1 - core, z, 2 * SUB : 2 * SUB + inner_rows]
 
 
 def outer_kernel(
-    keep_ref, other_ref, halo_ref, place_ref, inner_ref,
+    keep_ref, other_ref, halo_ref, place_ref, inner_ref, border_ref,
     p_keep_ref, p_send_ref, panel_keep_ref, panel_send_ref, trace, *state,
 ):
     layers, cols = p_keep_ref.shape[0], p_keep_ref.shape[2]
@@ -323,7 +334,7 @@
     core = lax.axis_index("cross")
     low = core == 0
     span = inner_rows + 2 * SUB
-    near = 2 * SUB
+    near = SUB
     base = 2 * span * layers
     base_z = 2 * SUB * layers
     ends = halo_ref.shape[0] // 2
@@ -371,15 +382,31 @@
             slot = jnp.broadcast_to(w_end[0:1], (SUB, cols))
             final = base + 3 * span + z
             final = jnp.broadcast_to(main_ref[final : final + 1], (SUB, cols))
-            w = jnp.concatenate([w[:SUB] - jnp.where(top_row, slot, 0.0), w[SUB:]], 0)
-            w = joined(w, w_end - jnp.where(end_row, final, 0.0))
+            w = joined(w - jnp.where(top_row, slot, 0.0), w_end - jnp.where(end_row, final, 0.0))
             turned = pltpu.roll(seam, cols - z, 1) if z else seam
             w_buf[tile, z] = w - jnp.where(seam_lane, turned, 0.0)
-    kept = slice(SUB, 2 * SUB)
-    advance(p_buf, w_buf, d_buf, wet_buf, scale_buf, half_buf, p_two, w_two, trace, kept)
+        for z in range(layers):
+            first, second = base + SUB, base + span - SUB - 1
+            depth = jnp.where(
+                low, main_ref[first : first + 1], main_ref[second : second + 1]
+            )
+            wet_buf[tile, z, SUB - 1 : SUB] = jnp.where(depth > float(z), 1.0, 0.0)
+
+    def before_step(t, p_now):
+        for i in range(2):
+            for z in range(layers):
+                value = border_ref[t, i, z : z + 1]
+                p_now[i, z, SUB - 1 : SUB] = value
+                p_now[i, z, 2 * SUB + near : 2 * SUB + near + 1] = value
+
+    def after_step(t, i, surface):
+        trace[t, i] = jnp.where(low, surface[SUB:], surface[:SUB])
+
+    advance(state, before_step, after_step, 8)
+    own = pl.multiple_of(SUB + SUB * (1 - core), SUB)
     for z in range(layers):
-        p_keep_ref[z] = p_buf[core, z, 2 * SUB : 3 * SUB]
-        p_send_ref[z] = p_buf[1 - core, z, 2 * SUB : 3 * SUB]
+        p_keep_ref[z] = p_buf[core, z, pl.ds(own, SUB)]
+        p_send_ref[z] = p_buf[1 - core, z, pl.ds(own, SUB)]
 
     width = cols // 2
     lane_rows = lanes_of((inner_rows + SUB, cols))
@@ -487,15 +514,16 @@
     parts = STEPS // 2
     inner_rows = half_rows - SUB
     inner_shape = jax.ShapeDtypeStruct((layers, inner_rows, cols), f32)
-    inner_keep, inner_send, inner_trace = pl.pallas_call(
+    inner_keep, inner_send, inner_trace, border = pl.pallas_call(
         inner_kernel,
         out_shape=[
             inner_shape,
             inner_shape,
             jax.ShapeDtypeStruct((STEPS, 2, inner_rows, cols), f32),
+            jax.ShapeDtypeStruct((STEPS, 2, layers, cols), f32),
         ],
         in_specs=[spec] * 2,
-        out_specs=[spec] * 3,
+        out_specs=[spec] * 4,
         scratch_shapes=state_buffers(layers, span, cols),
         compiler_params=params,
         cost_estimate=pl.CostEstimate(
@@ -510,12 +538,12 @@
     outer_keep, outer_send, panel_keep, panel_send = pl.pallas_call(
         outer_kernel,
         out_shape=[outer_shape, outer_shape, panel_shape, panel_shape],
-        in_specs=[spec] * 5,
+        in_specs=[spec] * 6,
         out_specs=[spec] * 4,
-        scratch_shapes=[VMEM((STEPS, 2, SUB, cols), f32)] + state_buffers(layers, 3 * SUB, cols),
+        scratch_shapes=[VMEM((STEPS, 2, SUB, cols), f32)] + state_buffers(layers, 2 * SUB, cols),
         compiler_params=params,
         name="outer",
-    )(keep, other, halo, place, inner_trace)
+    )(keep, other, halo, place, inner_trace, border)
 
     panels = panel_keep + lax.ppermute(panel_send, "cross", swap)
     if along_count == 4:

time: 30.1 us -> 29.2 us (0.970)
  Pallas kernels: 11.6 us -> 10.7 us
    pallas_call x1, Pallas kernels: 3.85 us -> 2.94 us  [shards(): pl.pallas_call(outer_kernel, out_shape=[outer_shape, outer_shape, panel_s...]
  transfers between devices with their start and end apart: 9 -> 9, of which waited for: 4 -> 4; matrix products, arithmetic and copies ran while one was open for 3% -> 4% of each run, Pallas kernels for 17% -> 18%
where the time goes in v7:
time: 29.2 us; the launch traced here: 29 us
  starting transfers between devices  11.7 us (40%)
  Pallas kernels  10.7 us (37%)
  waiting for transfers between devices  4.85 us (17%)
  other arithmetic  0.89 us (3%)
  between operations  0.72 us (2%)
    ppermute x3, starting transfers between devices, shards(): lax.ppermute(panels[k * some:(k + 1) * some], 'along', [(i, (i + k) % alo...  5.55 us
    pallas_call x1, Pallas kernels, shards(): pl.pallas_call(inner_kernel, out_shape=[inner_shape, inner_shape, jax.Sha...  4.9 us
    ppermute x1, starting transfers between devices, shards(): halo = lax.ppermute(halo, pair, route)  4.64 us
    pallas_call x1, Pallas kernels, shards(): pl.pallas_call(outer_kernel, out_shape=[outer_shape, outer_shape, panel_s...  2.94 us
    ppermute x3, waiting for transfers between devices, shards(): lax.ppermute(panels[k * some:(k + 1) * some], 'along', [(i, (i + k) % alo...  2.87 us
    pallas_call x1, Pallas kernels, shards(): pl.pallas_call(edges_kernel, out_shape=[jax.ShapeDtypeStruct((pack_rows,...  1.89 us
    ppermute x1, waiting for transfers between devices, shards(): two = lax.ppermute(two, 'cross', swap)  1 us
    ppermute x1, waiting for transfers between devices, shards(): panels = panel_keep + lax.ppermute(panel_send, 'cross', swap)  0.96 us
  transfers between devices with their start and end apart: 9, of which 4 were waited for; matrix products, arithmetic and copies ran while one was open for 4% of the time, Pallas kernels for 18%

profile of v7, /device:TPU:0, one launch (start us, length us, event | category | flops | bytes accessed | tf_op | source)
XLA Modules:
  0.0 29.0 jit_solution(1824243580704297558)
XLA Ops:
  0.6 1.9 %edges.1 = (f32[1416,128]{1,0:T(8,128)S(1)}, f32[1424,128]{1,0:T(8,128)S(1)}, f32[280,128]{1,0:T(8,128)S(1)}, f32[280,128]{1,0:T(8,128)S(1)}, s32[1,512]{1,0:T(1,128)S(1)}, /*index=5*/f32[8,128]{1,0:T(8,128)S(1)}) custom-call(f32[16,64,128]{2,1,0:T(8,128)} %bitcast.14, f32[16,64,128]{2,1,0:T(8,128)} %bitcast.15, f32[16,64,128]{2,1,0:T(8,128)} %bitcast.16, ...), custom_call_target="tpu_custom_call" | custom-call | tf_op jit(solution)/shard_map/edges/pallas_call | solution.py:455
  2.5 0.5 %collective-permute-start = (f32[280,128]{1,0:T(8,128)S(1)}, f32[280,128]{1,0:T(8,128)S(1)}, u32[]{:S(2)}, u32[]{:S(2)}) collective-permute-start(f32[280,128]{1,0:T(8,128)S(1)} %get-tuple-element.19), channel_id=1, source_target_pairs={{0,4},{4,0},{1,5},{5,1},{2,6},{6,2},{3,7},{7,3},{8,12},{12,8},{9,1... | collective-permute-start | bytes 430088 | tf_op jit(solution)/shard_map/ppermute | solution.py:493
  3.0 1.0 %collective-permute-done = f32[280,128]{1,0:T(8,128)S(1)} collective-permute-done((f32[280,128]{1,0:T(8,128)S(1)}, f32[280,128]{1,0:T(8,128)S(1)}, u32[]{:S(2)}, u32[]{:S(2)}) %collective-permute-start) | collective-permute-done | bytes 143392 | tf_op jit(solution)/shard_map/ppermute | solution.py:493
  4.1 0.4 %collective-permute-start.1 = (f32[1424,128]{1,0:T(8,128)S(1)}, f32[1424,128]{1,0:T(8,128)S(1)}, u32[]{:S(2)}, u32[]{:S(2)}) collective-permute-start(f32[1424,128]{1,0:T(8,128)S(1)} %get-tuple-element.20), channel_id=1, source_target_pairs={{0,4},{4,0},{1,5},{5,1},{2,6},{6,2},{3,7},{7,3},{8,12},{12,8},{9,1... | collective-permute-start | bytes 2187272 | tf_op jit(solution)/shard_map/ppermute | solution.py:496
  4.4 4.6 %collective-permute-start.2 = (f32[560,128]{1,0:T(8,128)S(1)}, f32[560,128]{1,0:T(8,128)S(1)}, u32[]{:S(2)}, u32[]{:S(2)}) collective-permute-start(f32[560,128]{1,0:T(8,128)S(1)} %pad_maximum_fusion), channel_id=1, source_target_pairs={{0,8},{8,16},{16,24},{12,4},{20,12},{28,20},{1,9},{9,17},{17,25},{... | collective-permute-start | bytes 860168 | tf_op jit(solution)/shard_map/ppermute | solution.py:497
  9.1 0.1 copy.10
  9.2 0.0 collective-permute-done.1.other_ref
  9.2 0.2 place.1.place_ref
  9.4 4.9 %inner.1 = (f32[16,24,128]{2,1,0:T(8,128)S(1)}, f32[16,24,128]{2,1,0:T(8,128)S(1)}, f32[8,2,24,128]{3,2,1,0:T(8,128)S(1)}, f32[8,2,16,128]{3,2,1,0:T(8,128)S(1)}) custom-call(f32[1416,128]{1,0:T(8,128)S(1)} %get-tuple-element.17.keep_ref, f32[1424,128]{1,0:T(8,128)S(1)} %collective-permute-done.1.other_ref), custom_call_target="tpu_custom_call" | custom-call | flops 32768000 | bytes 16384000 | tf_op jit(solution)/shard_map/inner/pallas_call | solution.py:517
  14.3 0.0 collective-permute-done.2.halo_ref
  14.3 2.9 %outer.1 = (f32[16,8,128]{2,1,0:T(8,128)S(1)}, f32[16,8,128]{2,1,0:T(8,128)S(1)}, f32[544,128]{1,0:T(8,128)S(1)}, f32[544,128]{1,0:T(8,128)S(1)}) custom-call(f32[1416,128]{1,0:T(8,128)S(1)} %get-tuple-element.17.keep_ref, f32[1424,128]{1,0:T(8,128)S(1)} %collective-permute-done.1.other_ref, f32[560,128]{1,0:T(8,128)S(1)} %collective-permute-done.2.halo_ref, ...), custom_call_target="tpu_custom_call" | custom-call | tf_op jit(solution)/shard_map/outer/pallas_call | solution.py:538
  17.3 0.1 collective-permute-start.5
  17.4 0.5 %collective-permute-start.4 = (f32[16,8,128]{2,1,0:T(8,128)S(1)}, f32[16,8,128]{2,1,0:T(8,128)S(1)}, u32[]{:S(2)}, u32[]{:S(2)}) collective-permute-start(f32[16,8,128]{2,1,0:T(8,128)S(1)} %get-tuple-element.29), channel_id=1, source_target_pairs={{0,4},{4,0},{1,5},{5,1},{2,6},{6,2},{3,7},{7,3},{8,12},{12,8},{9,1... | collective-permute-start | bytes 196616 | tf_op jit(solution)/shard_map/ppermute | solution.py:576
  17.9 0.1 collective-permute-start.3
  18.0 1.0 %collective-permute-done.5 = f32[544,128]{1,0:T(8,128)S(1)} collective-permute-done((f32[544,128]{1,0:T(8,128)S(1)}, f32[544,128]{1,0:T(8,128)S(1)}, u32[]{:S(2)}, u32[]{:S(2)}) %collective-permute-start.5) | collective-permute-done | bytes 278560 | tf_op jit(solution)/shard_map/ppermute | solution.py:548
  19.0 1.6 %collective-permute-start.6 = (f32[136,128]{1,0:T(8,128)S(1)}, f32[136,128]{1,0:T(8,128)S(1)}, u32[]{:S(2)}, u32[]{:S(2)}) collective-permute-start(f32[136,128]{1,0:T(8,128)S(1)} %get-tuple-element.38), channel_id=1, source_target_pairs={{0,8},{8,16},{16,24},{24,0},{1,9},{9,17},{17,25},{25,1},{2,10},{10... | collective-permute-start | bytes 208904 | tf_op jit(solution)/shard_map/ppermute | solution.py:555
  20.6 2.4 %collective-permute-start.7 = (f32[136,128]{1,0:T(8,128)S(1)}, f32[136,128]{1,0:T(8,128)S(1)}, u32[]{:S(2)}, u32[]{:S(2)}) collective-permute-start(f32[136,128]{1,0:T(8,128)S(1)} %get-tuple-element.37), channel_id=1, source_target_pairs={{0,16},{8,24},{16,0},{24,8},{1,17},{9,25},{17,1},{25,9},{2,18},{10... | collective-permute-start | bytes 208904 | tf_op jit(solution)/shard_map/ppermute | solution.py:555
  23.0 1.6 %collective-permute-start.8 = (f32[136,128]{1,0:T(8,128)S(1)}, f32[136,128]{1,0:T(8,128)S(1)}, u32[]{:S(2)}, u32[]{:S(2)}) collective-permute-start(f32[136,128]{1,0:T(8,128)S(1)} %get-tuple-element.36), channel_id=1, source_target_pairs={{0,24},{8,0},{16,8},{24,16},{1,25},{9,1},{17,9},{25,17},{2,26},{10... | collective-permute-start | bytes 208904 | tf_op jit(solution)/shard_map/ppermute | solution.py:555
  24.5 0.0 collective-permute-done.4
  24.5 0.0 collective-permute-done.3
  24.5 0.8 %maximum_select_fusion = f32[1,16,64,128]{3,2,1,0:T(8,128)} fusion(f32[1,16,8,128]{3,2,1,0:T(8,128)S(1)} %bitcast.19, f32[1,16,24,128]{3,2,1,0:T(8,128)S(1)} %bitcast.18, f32[1,16,24,128]{3,2,1,0:T(8,128)S(1)} %bitcast.11, f32[1,16,8,128]{3,2,1,0:T(8,128)S(1)} %bitcast.12, pred[]{:T(512)S(6)} %eq.3), kind=kLoop, calls=%fused_computation | loop fusion | flops 917504 | bytes 1048577 | tf_op jit(solution)/shard_map/jit(_where)/select_n | solution.py:577
  25.4 0.0 collective-permute-done.6.one_ref
  25.4 2.7 %collective-permute-done.7.two_ref = f32[136,128]{1,0:T(8,128)S(1)} collective-permute-done((f32[136,128]{1,0:T(8,128)S(1)}, f32[136,128]{1,0:T(8,128)S(1)}, u32[]{:S(2)}, u32[]{:S(2)}) %collective-permute-start.7) | collective-permute-done | bytes 69664 | tf_op jit(solution)/shard_map/ppermute | solution.py:555
  28.1 0.1 collective-permute-done.8.three_ref
  28.3 0.7 %gather.1 = f32[544,128]{1,0:T(8,128)} custom-call(f32[136,128]{1,0:T(8,128)S(1)} %get-tuple-element.39.own_ref, f32[136,128]{1,0:T(8,128)S(1)} %collective-permute-done.6.one_ref, f32[136,128]{1,0:T(8,128)S(1)} %collective-permute-done.7.two_ref, f32[136,128]{1,0:T(8,128)S(1)} %collective-permute-done.8.three_ref), custom_call_target="tpu_custom_call" | custom-call | tf_op jit(solution)/shard_map/gather/pallas_call | solution.py:561
  (3 shorter events, 0.1 us)
Async XLA Ops:
  2.5 1.5 %collective-permute-start = (f32[280,128]{1,0:T(8,128)S(1)}, f32[280,128]{1,0:T(8,128)S(1)}, u32[]{:S(2)}, u32[]{:S(2)}) collective-permute-start(f32[280,128]{1,0:T(8,128)S(1)} %get-tuple-element.19), channel_id=1, source_target_pairs={{0,4},{4,0},{1,5},{5,1},{2,6},{6,2},{3,7},{7,3},{8,12},{12,8},{9,1... | collective-permute-start | bytes 430088 | tf_op jit(solution)/shard_map/ppermute | solution.py:493
  4.1 5.2 %collective-permute-start.1 = (f32[1424,128]{1,0:T(8,128)S(1)}, f32[1424,128]{1,0:T(8,128)S(1)}, u32[]{:S(2)}, u32[]{:S(2)}) collective-permute-start(f32[1424,128]{1,0:T(8,128)S(1)} %get-tuple-element.20), channel_id=1, source_target_pairs={{0,4},{4,0},{1,5},{5,1},{2,6},{6,2},{3,7},{7,3},{8,12},{12,8},{9,1... | collective-permute-start | bytes 2187272 | tf_op jit(solution)/shard_map/ppermute | solution.py:496
  4.4 9.9 %collective-permute-start.2 = (f32[560,128]{1,0:T(8,128)S(1)}, f32[560,128]{1,0:T(8,128)S(1)}, u32[]{:S(2)}, u32[]{:S(2)}) collective-permute-start(f32[560,128]{1,0:T(8,128)S(1)} %pad_maximum_fusion), channel_id=1, source_target_pairs={{0,8},{8,16},{16,24},{12,4},{20,12},{28,20},{1,9},{9,17},{17,25},{... | collective-permute-start | bytes 860168 | tf_op jit(solution)/shard_map/ppermute | solution.py:497
  17.3 1.6 %collective-permute-start.5 = (f32[544,128]{1,0:T(8,128)S(1)}, f32[544,128]{1,0:T(8,128)S(1)}, u32[]{:S(2)}, u32[]{:S(2)}) collective-permute-start(f32[544,128]{1,0:T(8,128)S(1)} %get-tuple-element.31), channel_id=1, source_target_pairs={{0,4},{4,0},{1,5},{5,1},{2,6},{6,2},{3,7},{7,3},{8,12},{12,8},{9,1... | collective-permute-start | bytes 835592 | tf_op jit(solution)/shard_map/ppermute | solution.py:548
  17.4 7.2 %collective-permute-start.4 = (f32[16,8,128]{2,1,0:T(8,128)S(1)}, f32[16,8,128]{2,1,0:T(8,128)S(1)}, u32[]{:S(2)}, u32[]{:S(2)}) collective-permute-start(f32[16,8,128]{2,1,0:T(8,128)S(1)} %get-tuple-element.29), channel_id=1, source_target_pairs={{0,4},{4,0},{1,5},{5,1},{2,6},{6,2},{3,7},{7,3},{8,12},{12,8},{9,1... | collective-permute-start | bytes 196616 | tf_op jit(solution)/shard_map/ppermute | solution.py:576
  17.9 6.7 %collective-permute-start.3 = (f32[16,24,128]{2,1,0:T(8,128)S(1)}, f32[16,24,128]{2,1,0:T(8,128)S(1)}, u32[]{:S(2)}, u32[]{:S(2)}) collective-permute-start(f32[16,24,128]{2,1,0:T(8,128)S(1)} %get-tuple-element.28), channel_id=1, source_target_pairs={{0,4},{4,0},{1,5},{5,1},{2,6},{6,2},{3,7},{7,3},{8,12},{12,8},{9,1... | collective-permute-start | bytes 589832 | tf_op jit(solution)/shard_map/ppermute | solution.py:575
  19.0 6.4 %collective-permute-start.6 = (f32[136,128]{1,0:T(8,128)S(1)}, f32[136,128]{1,0:T(8,128)S(1)}, u32[]{:S(2)}, u32[]{:S(2)}) collective-permute-start(f32[136,128]{1,0:T(8,128)S(1)} %get-tuple-element.38), channel_id=1, source_target_pairs={{0,8},{8,16},{16,24},{24,0},{1,9},{9,17},{17,25},{25,1},{2,10},{10... | collective-permute-start | bytes 208904 | tf_op jit(solution)/shard_map/ppermute | solution.py:555
  20.6 7.5 %collective-permute-start.7 = (f32[136,128]{1,0:T(8,128)S(1)}, f32[136,128]{1,0:T(8,128)S(1)}, u32[]{:S(2)}, u32[]{:S(2)}) collective-permute-start(f32[136,128]{1,0:T(8,128)S(1)} %get-tuple-element.37), channel_id=1, source_target_pairs={{0,16},{8,24},{16,0},{24,8},{1,17},{9,25},{17,1},{25,9},{2,18},{10... | collective-permute-start | bytes 208904 | tf_op jit(solution)/shard_map/ppermute | solution.py:555
  23.0 5.3 %collective-permute-start.8 = (f32[136,128]{1,0:T(8,128)S(1)}, f32[136,128]{1,0:T(8,128)S(1)}, u32[]{:S(2)}, u32[]{:S(2)}) collective-permute-start(f32[136,128]{1,0:T(8,128)S(1)} %get-tuple-element.36), channel_id=1, source_target_pairs={{0,24},{8,0},{16,8},{24,16},{1,25},{9,1},{17,9},{25,17},{2,26},{10... | collective-permute-start | bytes 208904 | tf_op jit(solution)/shard_map/ppermute | solution.py:555

commit v8 on v7

--- a/solution.py
+++ b/solution.py
@@ -142,8 +142,7 @@
     some = 2 * capacity
     slot = block * capacity + rank
     if chips == 4:
-        ahead = lax.rem(chip - along + chips, chips)
-        slot = slot + ahead * some
+        slot = slot + lax.rem(chip - along + 2 * chips - 1, chips) * some
     else:
         slot = slot + chip * some
     handler = owner_core
@@ -181,25 +180,26 @@
             half_buf[tile, z - 1] = jnp.where(wet, 0.5, 0.0)
 
 
-def advance(state, before_step, after_step, ZB):
+def advance(state, before_step, after_step, ZB, low_row=0, high_row=None):
     p_buf, w_buf, d_buf, wet_buf, scale_buf, half_buf, p_two, w_two = state
     layers = p_buf.shape[1]
     wide, cols = w_buf.shape[2:]
     groups = layers // ZB
-    lane = lanes_of((ZB, wide, cols))
-    last_lane = lane == cols - 1
-    first_lane = lane == 0
     zeros = jnp.zeros((SUB, cols), jnp.float32)
     for tile in range(2):
         for z in range(layers):
             for buf in (p_buf, p_two):
                 buf[tile, z, :SUB] = zeros
                 buf[tile, z, SUB + wide :] = zeros
-    here = slice(SUB, SUB + wide)
-    ahead = slice(SUB + 1, SUB + 1 + wide)
-    back_rows = slice(SUB - 1, SUB - 1 + wide)
-
-    def step(t, first, p_buf, w_buf, p_out, w_out):
+    def step(t, first, p_buf, w_buf, p_out, w_out, low_row=0, high_row=wide):
+        rows = slice(low_row, high_row)
+        here = slice(SUB + low_row, SUB + high_row)
+        ahead = slice(SUB + low_row + 1, SUB + high_row + 1)
+        back_rows = slice(SUB + low_row - 1, SUB + high_row - 1)
+        lane = lanes_of((ZB, high_row - low_row, cols))
+        last_lane = lane == cols - 1
+        first_lane = lane == 0
+        zero_layer = jnp.zeros((1, high_row - low_row, cols), jnp.float32)
         before_step(t, p_buf)
 
         def stage_a(g):
@@ -212,7 +212,7 @@
                 jnp.where(last_lane, turned[1], turned[0]),
                 jnp.where(last_lane, 0.0, turned[1]),
             ]
-            gy = [wet_buf[i, zs, SUB:] * (right[i] - p_buf[i, zs, here]) for i in range(2)]
+            gy = [wet_buf[i, zs, here] * (right[i] - p_buf[i, zs, here]) for i in range(2)]
             return gy, [pltpu.roll(gy[i], 1, 2) for i in range(2)]
 
         hz_last = [None, None]
@@ -226,27 +226,27 @@
             ]
             for i in range(2):
                 p = p_buf[i, zs, here]
-                w = w_buf[i, zs] - (gy[i] - before[i])
-                gx = wet_buf[i, zs, SUB:] * (p_buf[i, zs, ahead] - p)
-                behind = wet_buf[i, zs, SUB - 1 : SUB - 1 + wide] * (p - p_buf[i, zs, back_rows])
+                w = w_buf[i, zs, rows] - (gy[i] - before[i])
+                gx = wet_buf[i, zs, here] * (p_buf[i, zs, ahead] - p)
+                behind = wet_buf[i, zs, back_rows] * (p - p_buf[i, zs, back_rows])
                 w = w - (gx - behind)
-                w_out[i, zs] = w
+                w_out[i, zs, rows] = w
                 if g + 1 < groups:
-                    hz = half_buf[i, zs] * (p_buf[i, g * ZB + 1 : (g + 1) * ZB + 1, here] - p)
+                    hz = half_buf[i, zs, rows] * (p_buf[i, g * ZB + 1 : (g + 1) * ZB + 1, here] - p)
                 elif ZB > 1:
-                    hz = jnp.concatenate([half_buf[i, g * ZB :] * (p[1:] - p[:-1]), jnp.zeros((1, wide, cols), jnp.float32)], 0)
+                    hz = jnp.concatenate([half_buf[i, g * ZB :, rows] * (p[1:] - p[:-1]), zero_layer], 0)
                 else:
-                    hz = jnp.zeros((1, wide, cols), jnp.float32)
-                prev = jnp.zeros((1, wide, cols), jnp.float32) if g == 0 else hz_last[i]
+                    hz = zero_layer
+                prev = zero_layer if g == 0 else hz_last[i]
                 flux = w - (hz - (jnp.concatenate([prev, hz[:-1]], 0) if ZB > 1 else prev))
                 hz_last[i] = hz[-1:]
-                old = wet_buf[i, zs, SUB:] * p if first else p
-                new = old - scale_buf[i, zs] * flux
+                old = wet_buf[i, zs, here] * p if first else p
+                new = old - scale_buf[i, zs, rows] * flux
                 p_out[i, zs, here] = new
                 for k in range(ZB):
                     part = new[k]
                     z = g * ZB + k
-                    surface[i] = part if z == 0 else jnp.where(d_buf[i] > float(z), part, surface[i])
+                    surface[i] = part if z == 0 else jnp.where(d_buf[i, rows] > float(z), part, surface[i])
 
         turned = [stage_a(0), stage_a(1)]
         ready = stage_b(0, turned[0])
@@ -266,7 +266,9 @@
 
     step(0, True, p_buf, w_buf, p_two, w_two)
     step(1, False, p_two, w_two, p_buf, w_buf)
-    lax.fori_loop(1, STEPS // 2, two, 0)
+    lax.fori_loop(1, STEPS // 2 - 1, two, 0)
+    step(STEPS - 2, False, p_buf, w_buf, p_two, w_two)
+    step(STEPS - 1, False, p_two, w_two, p_buf, w_buf, low_row, high_row or wide)
 
 
 def state_buffers(layers, wide, cols):
@@ -317,9 +319,9 @@
                 )
 
     def after_step(t, i, surface):
-        trace_ref[t, i] = surface[SUB : SUB + inner_rows]
-
-    advance(state, before_step, after_step, 4)
+        trace_ref[t, i] = surface if surface.shape[0] == inner_rows else surface[SUB : SUB + inner_rows]
+
+    advance(state, before_step, after_step, 4, SUB, SUB + inner_rows)
     for z in range(layers):
         p_keep_ref[z] = p_buf[core, z, 2 * SUB : 2 * SUB + inner_rows]
         p_send_ref[z] = p_buf[1 - core, z, 2 * SUB : 2 * SUB + inner_rows]
@@ -327,7 +329,7 @@
 
 def outer_kernel(
     keep_ref, other_ref, halo_ref, place_ref, inner_ref, border_ref,
-    p_keep_ref, p_send_ref, panel_keep_ref, panel_send_ref, trace, *state,
+    p_keep_ref, p_send_ref, panel_keep_ref, panel_send_ref, panel_rest_ref, trace, *state,
 ):
     layers, cols = p_keep_ref.shape[0], p_keep_ref.shape[2]
     inner_rows = inner_ref.shape[2]
@@ -410,9 +412,8 @@
 
     width = cols // 2
     lane_rows = lanes_of((inner_rows + SUB, cols))
-    place = place_ref[...]
-    count = place.shape[0] // 2
     parts = STEPS // 2
+    wholes = []
     for j in range(parts):
         pieces = []
         for i in range(2):
@@ -420,16 +421,24 @@
             two = jnp.concatenate([trace[2 * j + 1, i], inner_ref[2 * j + 1, i]], 0)
             pieces.append(jnp.where(lane_rows < width, one, pltpu.roll(two, width, 1)))
             pieces.append(jnp.where(lane_rows < width, pltpu.roll(one, width, 1), two))
-        both = jnp.concatenate(pieces, 0)
-        part_a = both.astype(jnp.bfloat16)
-        rest = both - part_a.astype(jnp.float32)
-        part_b = rest.astype(jnp.bfloat16)
-        part_c = (rest - part_b.astype(jnp.float32)).astype(jnp.bfloat16)
-        total = jnp.dot(place, part_a, preferred_element_type=jnp.float32)
-        total += jnp.dot(place, part_b, preferred_element_type=jnp.float32)
-        total += jnp.dot(place, part_c, preferred_element_type=jnp.float32)
-        panel_keep_ref[pl.ds(j, count, stride=parts)] = total[:count]
-        panel_send_ref[pl.ds(j, count, stride=parts)] = total[count:]
+        wholes.append(jnp.concatenate(pieces, 0))
+    both = jnp.concatenate(wholes, 1)
+    part_a = both.astype(jnp.bfloat16)
+    rest = both - part_a.astype(jnp.float32)
+    part_b = rest.astype(jnp.bfloat16)
+    part_c = (rest - part_b.astype(jnp.float32)).astype(jnp.bfloat16)
+    total = jnp.dot(
+        jnp.concatenate([place_ref[...]] * 3, 1),
+        jnp.concatenate([part_a, part_b, part_c], 0),
+        preferred_element_type=jnp.float32,
+    )
+    for j in range(parts):
+        piece = total[:, j * cols : (j + 1) * cols]
+        at = 0
+        for ref in (panel_keep_ref, panel_send_ref, panel_rest_ref):
+            count = ref.shape[0] // parts
+            ref[pl.ds(j, count, stride=parts)] = piece[at : at + count]
+            at += count
 
 
 def shards(
@@ -534,30 +543,30 @@
         name="inner",
     )(keep, other)
     outer_shape = jax.ShapeDtypeStruct((layers, SUB, cols), f32)
-    panel_shape = jax.ShapeDtypeStruct((count * parts, cols), f32)
-    outer_keep, outer_send, panel_keep, panel_send = pl.pallas_call(
+    some = 2 * capacity * parts
+    outer_keep, outer_send, panel_keep, panel_send, panel_rest = pl.pallas_call(
         outer_kernel,
-        out_shape=[outer_shape, outer_shape, panel_shape, panel_shape],
+        out_shape=[outer_shape, outer_shape]
+        + [
+            jax.ShapeDtypeStruct((number, cols), f32)
+            for number in (along_count * some, some, (along_count - 1) * some)
+        ],
         in_specs=[spec] * 6,
-        out_specs=[spec] * 4,
+        out_specs=[spec] * 5,
         scratch_shapes=[VMEM((STEPS, 2, SUB, cols), f32)] + state_buffers(layers, 2 * SUB, cols),
         compiler_params=params,
         name="outer",
     )(keep, other, halo, place, inner_trace, border)
 
-    panels = panel_keep + lax.ppermute(panel_send, "cross", swap)
+    panel_first = panel_keep[:some] + lax.ppermute(panel_send, "cross", swap)
+    rest_other = lax.ppermute(panel_rest, "cross", swap)
+    panel_rest = panel_keep[some:] + rest_other
     if along_count == 4:
-        some = 2 * capacity * parts
-        ring = range(along_count)
-        pieces = [panels[:some]]
+        pieces = [panel_rest[2 * some :]]
         for k in range(1, along_count):
-            pieces.append(
-                lax.ppermute(
-                    panels[k * some : (k + 1) * some],
-                    "along",
-                    [(i, (i + k) % along_count) for i in ring],
-                )
-            )
+            piece = panel_first if k == 1 else panel_rest[(k - 2) * some : (k - 1) * some]
+            route = [(i, (i + k) % along_count) for i in range(along_count)]
+            pieces.append(lax.ppermute(piece, "along", route))
         received = pl.pallas_call(
             gather_kernel,
             out_shape=jax.ShapeDtypeStruct((count * parts, cols), f32),
@@ -568,7 +577,7 @@
             name="gather",
         )(*pieces)
     else:
-        panels = panels.reshape(along_count, 2 * capacity * parts, cols)
+        panels = jnp.concatenate([panel_first, panel_rest], 0).reshape(along_count, some, cols)
         received = lax.all_to_all(panels, "along", split_axis=0, concat_axis=0, tiled=True)
     received = received.reshape(1, count, 1, parts * cols)
 

time: 29.2 us -> 28.5 us (0.976)
  waiting for transfers between devices: 4.85 us -> 4.1 us
  starting transfers between devices: 11.7 us -> 12.2 us
  Pallas kernels: 10.7 us -> 10.3 us
    ppermute x4 -> x5, waiting for transfers between devices: 3.83 us -> 3.08 us  [the longest x3 2.84 us: shards(): pieces.append(lax.ppermute(piece, 'along', route))]
    ppermute x4 -> x5, starting transfers between devices: 5.62 us -> 6.18 us  [the longest x3 5.62 us: shards(): pieces.append(lax.ppermute(piece, 'along', route))]
    ppermute x1, starting transfers between devices: 0.49 us -> 0.08 us  [shards(): outer_other = lax.ppermute(outer_send, 'cross', swap)]
    ppermute x1, starting transfers between devices: 0.08 us -> 0.43 us  [shards(): inner_other = lax.ppermute(inner_send, 'cross', swap)]
  transfers between devices with their start and end apart: 9 -> 10, of which waited for: 4 -> 4; matrix products, arithmetic and copies ran while one was open for 4% -> 4% of each run, Pallas kernels for 18% -> 18%
where the time goes in v8:
time: 28.5 us; the launch traced here: 28.4 us
  starting transfers between devices  12.2 us (43%)
  Pallas kernels  10.3 us (36%)
  waiting for transfers between devices  4.1 us (14%)
  other arithmetic  0.89 us (3%)
  between operations  0.72 us (3%)
    ppermute x3, starting transfers between devices, shards(): pieces.append(lax.ppermute(piece, 'along', route))  5.62 us
    pallas_call x1, Pallas kernels, shards(): pl.pallas_call(inner_kernel, out_shape=[inner_shape, inner_shape, jax.Sha...  4.77 us
    ppermute x1, starting transfers between devices, shards(): halo = lax.ppermute(halo, pair, route)  4.64 us
    ppermute x3, waiting for transfers between devices, shards(): pieces.append(lax.ppermute(piece, 'along', route))  2.84 us
    pallas_call x1, Pallas kernels, shards(): pl.pallas_call(outer_kernel, out_shape=[outer_shape, outer_shape] + [jax....  2.72 us
    pallas_call x1, Pallas kernels, shards(): pl.pallas_call(edges_kernel, out_shape=[jax.ShapeDtypeStruct((pack_rows,...  1.89 us
    ppermute x1, waiting for transfers between devices, shards(): two = lax.ppermute(two, 'cross', swap)  1 us
    select_n x1, other arithmetic, shards(): jnp.where(low, jnp.concatenate([outer_keep, inner_keep, inner_other, oute...  0.84 us
  transfers between devices with their start and end apart: 10, of which 4 were waited for; matrix products, arithmetic and copies ran while one was open for 4% of the time, Pallas kernels for 18%

profile of v8, /device:TPU:0, one launch (start us, length us, event | category | flops | bytes accessed | tf_op | source)
XLA Modules:
  0.0 28.4 jit_solution(8005182586265703838)
XLA Ops:
  0.6 1.9 %edges.1 = (f32[1416,128]{1,0:T(8,128)S(1)}, f32[1424,128]{1,0:T(8,128)S(1)}, f32[280,128]{1,0:T(8,128)S(1)}, f32[280,128]{1,0:T(8,128)S(1)}, s32[1,512]{1,0:T(1,128)S(1)}, /*index=5*/f32[8,128]{1,0:T(8,128)S(1)}) custom-call(f32[16,64,128]{2,1,0:T(8,128)} %bitcast.14, f32[16,64,128]{2,1,0:T(8,128)} %bitcast.15, f32[16,64,128]{2,1,0:T(8,128)} %bitcast.16, ...), custom_call_target="tpu_custom_call" | custom-call | tf_op jit(solution)/shard_map/edges/pallas_call | solution.py:464
  2.5 0.5 %collective-permute-start = (f32[280,128]{1,0:T(8,128)S(1)}, f32[280,128]{1,0:T(8,128)S(1)}, u32[]{:S(2)}, u32[]{:S(2)}) collective-permute-start(f32[280,128]{1,0:T(8,128)S(1)} %get-tuple-element.20), channel_id=1, source_target_pairs={{0,4},{4,0},{1,5},{5,1},{2,6},{6,2},{3,7},{7,3},{8,12},{12,8},{9,1... | collective-permute-start | bytes 430088 | tf_op jit(solution)/shard_map/ppermute | solution.py:502
  3.0 1.0 %collective-permute-done = f32[280,128]{1,0:T(8,128)S(1)} collective-permute-done((f32[280,128]{1,0:T(8,128)S(1)}, f32[280,128]{1,0:T(8,128)S(1)}, u32[]{:S(2)}, u32[]{:S(2)}) %collective-permute-start) | collective-permute-done | bytes 143392 | tf_op jit(solution)/shard_map/ppermute | solution.py:502
  4.1 0.4 %collective-permute-start.1 = (f32[1424,128]{1,0:T(8,128)S(1)}, f32[1424,128]{1,0:T(8,128)S(1)}, u32[]{:S(2)}, u32[]{:S(2)}) collective-permute-start(f32[1424,128]{1,0:T(8,128)S(1)} %get-tuple-element.21), channel_id=1, source_target_pairs={{0,4},{4,0},{1,5},{5,1},{2,6},{6,2},{3,7},{7,3},{8,12},{12,8},{9,1... | collective-permute-start | bytes 2187272 | tf_op jit(solution)/shard_map/ppermute | solution.py:505
  4.4 4.6 %collective-permute-start.2 = (f32[560,128]{1,0:T(8,128)S(1)}, f32[560,128]{1,0:T(8,128)S(1)}, u32[]{:S(2)}, u32[]{:S(2)}) collective-permute-start(f32[560,128]{1,0:T(8,128)S(1)} %pad_maximum_fusion), channel_id=1, source_target_pairs={{0,8},{8,16},{16,24},{12,4},{20,12},{28,20},{1,9},{9,17},{17,25},{... | collective-permute-start | bytes 860168 | tf_op jit(solution)/shard_map/ppermute | solution.py:506
  9.1 0.1 copy.10
  9.2 0.0 collective-permute-done.1.other_ref
  9.2 0.2 place.1.place_ref
  9.4 4.8 %inner.1 = (f32[16,24,128]{2,1,0:T(8,128)S(1)}, f32[16,24,128]{2,1,0:T(8,128)S(1)}, f32[8,2,24,128]{3,2,1,0:T(8,128)S(1)}, f32[8,2,16,128]{3,2,1,0:T(8,128)S(1)}) custom-call(f32[1416,128]{1,0:T(8,128)S(1)} %get-tuple-element.18.keep_ref, f32[1424,128]{1,0:T(8,128)S(1)} %collective-permute-done.1.other_ref), custom_call_target="tpu_custom_call" | custom-call | flops 32768000 | bytes 16384000 | tf_op jit(solution)/shard_map/inner/pallas_call | solution.py:526
  14.2 0.0 collective-permute-done.2.halo_ref
  14.2 2.7 %outer.1 = (f32[16,8,128]{2,1,0:T(8,128)S(1)}, f32[16,8,128]{2,1,0:T(8,128)S(1)}, f32[544,128]{1,0:T(8,128)S(1)}, f32[136,128]{1,0:T(8,128)S(1)}, f32[408,128]{1,0:T(8,128)S(1)}) custom-call(f32[1416,128]{1,0:T(8,128)S(1)} %get-tuple-element.18.keep_ref, f32[1424,128]{1,0:T(8,128)S(1)} %collective-permute-done.1.other_ref, ...), custom_call_target="tpu_custom_call" | custom-call | tf_op jit(solution)/shard_map/outer/pallas_call | solution.py:547
  16.9 0.1 collective-permute-start.6
  17.0 0.5 %collective-permute-start.5 = (f32[408,128]{1,0:T(8,128)S(1)}, f32[408,128]{1,0:T(8,128)S(1)}, u32[]{:S(2)}, u32[]{:S(2)}) collective-permute-start(f32[408,128]{1,0:T(8,128)S(1)} %get-tuple-element.32), channel_id=1, source_target_pairs={{0,4},{4,0},{1,5},{5,1},{2,6},{6,2},{3,7},{7,3},{8,12},{12,8},{9,1... | collective-permute-start | bytes 626696 | tf_op jit(solution)/shard_map/ppermute | solution.py:562
  17.5 0.1 collective-permute-start.4
  17.6 0.4 %collective-permute-start.3 = (f32[16,24,128]{2,1,0:T(8,128)S(1)}, f32[16,24,128]{2,1,0:T(8,128)S(1)}, u32[]{:S(2)}, u32[]{:S(2)}) collective-permute-start(f32[16,24,128]{2,1,0:T(8,128)S(1)} %get-tuple-element.29), channel_id=1, source_target_pairs={{0,4},{4,0},{1,5},{5,1},{2,6},{6,2},{3,7},{7,3},{8,12},{12,8},{9,1... | collective-permute-start | bytes 589832 | tf_op jit(solution)/shard_map/ppermute | solution.py:584
  18.0 0.2 collective-permute-done.6
  18.3 1.6 %collective-permute-start.7 = (f32[136,128]{1,0:T(8,128)S(1)}, f32[136,128]{1,0:T(8,128)S(1)}, u32[]{:S(2)}, u32[]{:S(2)}) collective-permute-start(f32[136,128]{1,0:T(8,128)S(1)} %slice_add_fusion.1), channel_id=1, source_target_pairs={{0,8},{8,16},{16,24},{24,0},{1,9},{9,17},{17,25},{25,1},{2,10},{10... | collective-permute-start | bytes 208904 | tf_op jit(solution)/shard_map/ppermute | solution.py:569
  19.9 0.0 collective-permute-done.5
  19.9 2.6 %collective-permute-start.8 = (f32[136,128]{1,0:T(8,128)S(1)}, f32[136,128]{1,0:T(8,128)S(1)}, u32[]{:S(2)}, u32[]{:S(2)}) collective-permute-start(f32[136,128]{1,0:T(8,128)S(1)} %get-tuple-element.39), channel_id=1, source_target_pairs={{0,16},{8,24},{16,0},{24,8},{1,17},{9,25},{17,1},{25,9},{2,18},{10... | collective-permute-start | bytes 208904 | tf_op jit(solution)/shard_map/ppermute | solution.py:569
  22.5 1.4 %collective-permute-start.9 = (f32[136,128]{1,0:T(8,128)S(1)}, f32[136,128]{1,0:T(8,128)S(1)}, u32[]{:S(2)}, u32[]{:S(2)}) collective-permute-start(f32[136,128]{1,0:T(8,128)S(1)} %get-tuple-element.38), channel_id=1, source_target_pairs={{0,24},{8,0},{16,8},{24,16},{1,25},{9,1},{17,9},{25,17},{2,26},{10... | collective-permute-start | bytes 208904 | tf_op jit(solution)/shard_map/ppermute | solution.py:569
  23.9 0.0 collective-permute-done.4
  23.9 0.0 collective-permute-done.3
  23.9 0.8 %maximum_select_fusion = f32[1,16,64,128]{3,2,1,0:T(8,128)} fusion(f32[1,16,8,128]{3,2,1,0:T(8,128)S(1)} %bitcast.19, f32[1,16,24,128]{3,2,1,0:T(8,128)S(1)} %bitcast.18, f32[1,16,24,128]{3,2,1,0:T(8,128)S(1)} %bitcast.11, f32[1,16,8,128]{3,2,1,0:T(8,128)S(1)} %bitcast.12, pred[]{:T(512)S(6)} %eq.3), kind=kLoop, calls=%fused_computation | loop fusion | flops 917504 | bytes 1048577 | tf_op jit(solution)/shard_map/jit(_where)/select_n | solution.py:586
  24.8 0.0 collective-permute-done.7.one_ref
  24.8 2.6 %collective-permute-done.8.two_ref = f32[136,128]{1,0:T(8,128)S(1)} collective-permute-done((f32[136,128]{1,0:T(8,128)S(1)}, f32[136,128]{1,0:T(8,128)S(1)}, u32[]{:S(2)}, u32[]{:S(2)}) %collective-permute-start.8) | collective-permute-done | bytes 69664 | tf_op jit(solution)/shard_map/ppermute | solution.py:569
  27.4 0.2 collective-permute-done.9.three_ref
  27.6 0.7 %gather.1 = f32[544,128]{1,0:T(8,128)} custom-call(f32[136,128]{1,0:T(8,128)S(1)} %get-tuple-element.40.own_ref, f32[136,128]{1,0:T(8,128)S(1)} %collective-permute-done.7.one_ref, f32[136,128]{1,0:T(8,128)S(1)} %collective-permute-done.8.two_ref, f32[136,128]{1,0:T(8,128)S(1)} %collective-permute-done.9.three_ref), custom_call_target="tpu_custom_call" | custom-call | tf_op jit(solution)/shard_map/gather/pallas_call | solution.py:570
  (4 shorter events, 0.1 us)
Async XLA Ops:
  2.5 1.5 %collective-permute-start = (f32[280,128]{1,0:T(8,128)S(1)}, f32[280,128]{1,0:T(8,128)S(1)}, u32[]{:S(2)}, u32[]{:S(2)}) collective-permute-start(f32[280,128]{1,0:T(8,128)S(1)} %get-tuple-element.20), channel_id=1, source_target_pairs={{0,4},{4,0},{1,5},{5,1},{2,6},{6,2},{3,7},{7,3},{8,12},{12,8},{9,1... | collective-permute-start | bytes 430088 | tf_op jit(solution)/shard_map/ppermute | solution.py:502
  4.1 5.2 %collective-permute-start.1 = (f32[1424,128]{1,0:T(8,128)S(1)}, f32[1424,128]{1,0:T(8,128)S(1)}, u32[]{:S(2)}, u32[]{:S(2)}) collective-permute-start(f32[1424,128]{1,0:T(8,128)S(1)} %get-tuple-element.21), channel_id=1, source_target_pairs={{0,4},{4,0},{1,5},{5,1},{2,6},{6,2},{3,7},{7,3},{8,12},{12,8},{9,1... | collective-permute-start | bytes 2187272 | tf_op jit(solution)/shard_map/ppermute | solution.py:505
  4.4 9.8 %collective-permute-start.2 = (f32[560,128]{1,0:T(8,128)S(1)}, f32[560,128]{1,0:T(8,128)S(1)}, u32[]{:S(2)}, u32[]{:S(2)}) collective-permute-start(f32[560,128]{1,0:T(8,128)S(1)} %pad_maximum_fusion), channel_id=1, source_target_pairs={{0,8},{8,16},{16,24},{12,4},{20,12},{28,20},{1,9},{9,17},{17,25},{... | collective-permute-start | bytes 860168 | tf_op jit(solution)/shard_map/ppermute | solution.py:506
  16.9 1.3 %collective-permute-start.6 = (f32[136,128]{1,0:T(8,128)S(1)}, f32[136,128]{1,0:T(8,128)S(1)}, u32[]{:S(2)}, u32[]{:S(2)}) collective-permute-start(f32[136,128]{1,0:T(8,128)S(1)} %get-tuple-element.33), channel_id=1, source_target_pairs={{0,4},{4,0},{1,5},{5,1},{2,6},{6,2},{3,7},{7,3},{8,12},{12,8},{9,1... | collective-permute-start | bytes 208904 | tf_op jit(solution)/shard_map/ppermute | solution.py:561
  17.0 2.9 %collective-permute-start.5 = (f32[408,128]{1,0:T(8,128)S(1)}, f32[408,128]{1,0:T(8,128)S(1)}, u32[]{:S(2)}, u32[]{:S(2)}) collective-permute-start(f32[408,128]{1,0:T(8,128)S(1)} %get-tuple-element.32), channel_id=1, source_target_pairs={{0,4},{4,0},{1,5},{5,1},{2,6},{6,2},{3,7},{7,3},{8,12},{12,8},{9,1... | collective-permute-start | bytes 626696 | tf_op jit(solution)/shard_map/ppermute | solution.py:562
  17.5 6.4 %collective-permute-start.4 = (f32[16,8,128]{2,1,0:T(8,128)S(1)}, f32[16,8,128]{2,1,0:T(8,128)S(1)}, u32[]{:S(2)}, u32[]{:S(2)}) collective-permute-start(f32[16,8,128]{2,1,0:T(8,128)S(1)} %get-tuple-element.30), channel_id=1, source_target_pairs={{0,4},{4,0},{1,5},{5,1},{2,6},{6,2},{3,7},{7,3},{8,12},{12,8},{9,1... | collective-permute-start | bytes 196616 | tf_op jit(solution)/shard_map/ppermute | solution.py:585
  17.6 6.4 %collective-permute-start.3 = (f32[16,24,128]{2,1,0:T(8,128)S(1)}, f32[16,24,128]{2,1,0:T(8,128)S(1)}, u32[]{:S(2)}, u32[]{:S(2)}) collective-permute-start(f32[16,24,128]{2,1,0:T(8,128)S(1)} %get-tuple-element.29), channel_id=1, source_target_pairs={{0,4},{4,0},{1,5},{5,1},{2,6},{6,2},{3,7},{7,3},{8,12},{12,8},{9,1... | collective-permute-start | bytes 589832 | tf_op jit(solution)/shard_map/ppermute | solution.py:584
  18.3 6.5 %collective-permute-start.7 = (f32[136,128]{1,0:T(8,128)S(1)}, f32[136,128]{1,0:T(8,128)S(1)}, u32[]{:S(2)}, u32[]{:S(2)}) collective-permute-start(f32[136,128]{1,0:T(8,128)S(1)} %slice_add_fusion.1), channel_id=1, source_target_pairs={{0,8},{8,16},{16,24},{24,0},{1,9},{9,17},{17,25},{25,1},{2,10},{10... | collective-permute-start | bytes 208904 | tf_op jit(solution)/shard_map/ppermute | solution.py:569
  19.9 7.5 %collective-permute-start.8 = (f32[136,128]{1,0:T(8,128)S(1)}, f32[136,128]{1,0:T(8,128)S(1)}, u32[]{:S(2)}, u32[]{:S(2)}) collective-permute-start(f32[136,128]{1,0:T(8,128)S(1)} %get-tuple-element.39), channel_id=1, source_target_pairs={{0,16},{8,24},{16,0},{24,8},{1,17},{9,25},{17,1},{25,9},{2,18},{10... | collective-permute-start | bytes 208904 | tf_op jit(solution)/shard_map/ppermute | solution.py:569
  22.5 5.1 %collective-permute-start.9 = (f32[136,128]{1,0:T(8,128)S(1)}, f32[136,128]{1,0:T(8,128)S(1)}, u32[]{:S(2)}, u32[]{:S(2)}) collective-permute-start(f32[136,128]{1,0:T(8,128)S(1)} %get-tuple-element.38), channel_id=1, source_target_pairs={{0,24},{8,0},{16,8},{24,16},{1,25},{9,1},{17,9},{25,17},{2,26},{10... | collective-permute-start | bytes 208904 | tf_op jit(solution)/shard_map/ppermute | solution.py:569

commit v9 on v8

--- a/solution.py
+++ b/solution.py
@@ -25,25 +25,23 @@
     keep_ref, send_ref, one_ref, two_ref, ids_ref, owners_ref,
     p_ref, fa_ref, fc_ref, depth_ref, stiff_ref, owner_ref, sems,
 ):
+    layers, rows, cols = p_ref.shape
+    half = layers // 2
+    pairs = []
+    for part in (slice(0, half), slice(half, layers)):
+        for source, target in ((fa_hbm, fa_ref), (fc_hbm, fc_ref), (p_hbm, p_ref)):
+            pairs.append((source.at[part], target.at[part]))
+        if not part.start:
+            pairs += [
+                (depth_hbm, depth_ref), (stiff_hbm, stiff_ref), (owner_hbm, owner_ref), (ids_hbm, ids_ref)
+            ]
     copies = [
-        pltpu.make_async_copy(source, target, sems.at[i])
-        for i, (source, target) in enumerate(
-            (
-                (depth_hbm, depth_ref),
-                (stiff_hbm, stiff_ref),
-                (owner_hbm, owner_ref),
-                (ids_hbm, ids_ref),
-                (fa_hbm, fa_ref),
-                (fc_hbm, fc_ref),
-                (p_hbm, p_ref),
-            )
-        )
+        pltpu.make_async_copy(source, target, sems.at[i]) for i, (source, target) in enumerate(pairs)
     ]
     for copy in copies:
         copy.start()
-    for copy in copies:
+    for copy in copies[:7]:
         copy.wait()
-    layers, rows, cols = p_ref.shape
     low = lax.axis_index("cross") == 0
     span = rows // 2 + SUB
     last = rows - SUB
@@ -68,6 +66,9 @@
         return jnp.where(low, second, first), jnp.where(low, first, second)
 
     for z in range(layers):
+        if z == half:
+            for copy in copies[7:]:
+                copy.wait()
         wet = depth > z
         p = p_ref[z]
         va = jnp.where(wet, fa_ref[z], 0.0)
@@ -480,7 +481,7 @@
             VMEM((rows, cols), jnp.int32),
             VMEM((rows, cols), f32),
             VMEM(owner_map.shape, jnp.int32),
-            pltpu.SemaphoreType.DMA((7,)),
+            pltpu.SemaphoreType.DMA((10,)),
         ],
         compiler_params=params,
         name="edges",

time: 28.5 us -> 28.4 us (level)
  no operation moved by 1% of the time
where the time goes in v9:
time: 28.4 us; the launch traced here: 28.2 us
  starting transfers between devices  12.2 us (43%)
  Pallas kernels  10.2 us (36%)
  waiting for transfers between devices  4.1 us (14%)
  other arithmetic  0.89 us (3%)
  between operations  0.72 us (3%)
    ppermute x3, starting transfers between devices, shards(): pieces.append(lax.ppermute(piece, 'along', route))  5.62 us
    pallas_call x1, Pallas kernels, shards(): pl.pallas_call(inner_kernel, out_shape=[inner_shape, inner_shape, jax.Sha...  4.77 us
    ppermute x1, starting transfers between devices, shards(): halo = lax.ppermute(halo, pair, route)  4.64 us
    ppermute x3, waiting for transfers between devices, shards(): pieces.append(lax.ppermute(piece, 'along', route))  2.84 us
    pallas_call x1, Pallas kernels, shards(): pl.pallas_call(outer_kernel, out_shape=[outer_shape, outer_shape] + [jax....  2.72 us
    pallas_call x1, Pallas kernels, shards(): pl.pallas_call(edges_kernel, out_shape=[jax.ShapeDtypeStruct((pack_rows,...  1.73 us
    ppermute x1, waiting for transfers between devices, shards(): two = lax.ppermute(two, 'cross', swap)  1 us
    select_n x1, other arithmetic, shards(): jnp.where(low, jnp.concatenate([outer_keep, inner_keep, inner_other, oute...  0.84 us
  transfers between devices with their start and end apart: 10, of which 4 were waited for; matrix products, arithmetic and copies ran while one was open for 4% of the time, Pallas kernels for 18%

profile of v9, /device:TPU:0, one launch (start us, length us, event | category | flops | bytes accessed | tf_op | source)
XLA Modules:
  0.0 28.2 jit_solution(231388469768131786)
XLA Ops:
  0.6 1.7 %edges.1 = (f32[1416,128]{1,0:T(8,128)S(1)}, f32[1424,128]{1,0:T(8,128)S(1)}, f32[280,128]{1,0:T(8,128)S(1)}, f32[280,128]{1,0:T(8,128)S(1)}, s32[1,512]{1,0:T(1,128)S(1)}, /*index=5*/f32[8,128]{1,0:T(8,128)S(1)}) custom-call(f32[16,64,128]{2,1,0:T(8,128)} %bitcast.14, f32[16,64,128]{2,1,0:T(8,128)} %bitcast.15, f32[16,64,128]{2,1,0:T(8,128)} %bitcast.16, ...), custom_call_target="tpu_custom_call" | custom-call | tf_op jit(solution)/shard_map/edges/pallas_call | solution.py:465
  2.4 0.5 %collective-permute-start = (f32[280,128]{1,0:T(8,128)S(1)}, f32[280,128]{1,0:T(8,128)S(1)}, u32[]{:S(2)}, u32[]{:S(2)}) collective-permute-start(f32[280,128]{1,0:T(8,128)S(1)} %get-tuple-element.20), channel_id=1, source_target_pairs={{0,4},{4,0},{1,5},{5,1},{2,6},{6,2},{3,7},{7,3},{8,12},{12,8},{9,1... | collective-permute-start | bytes 430088 | tf_op jit(solution)/shard_map/ppermute | solution.py:503
  2.9 1.0 %collective-permute-done = f32[280,128]{1,0:T(8,128)S(1)} collective-permute-done((f32[280,128]{1,0:T(8,128)S(1)}, f32[280,128]{1,0:T(8,128)S(1)}, u32[]{:S(2)}, u32[]{:S(2)}) %collective-permute-start) | collective-permute-done | bytes 143392 | tf_op jit(solution)/shard_map/ppermute | solution.py:503
  3.9 0.4 %collective-permute-start.1 = (f32[1424,128]{1,0:T(8,128)S(1)}, f32[1424,128]{1,0:T(8,128)S(1)}, u32[]{:S(2)}, u32[]{:S(2)}) collective-permute-start(f32[1424,128]{1,0:T(8,128)S(1)} %get-tuple-element.21), channel_id=1, source_target_pairs={{0,4},{4,0},{1,5},{5,1},{2,6},{6,2},{3,7},{7,3},{8,12},{12,8},{9,1... | collective-permute-start | bytes 2187272 | tf_op jit(solution)/shard_map/ppermute | solution.py:506
  4.3 4.6 %collective-permute-start.2 = (f32[560,128]{1,0:T(8,128)S(1)}, f32[560,128]{1,0:T(8,128)S(1)}, u32[]{:S(2)}, u32[]{:S(2)}) collective-permute-start(f32[560,128]{1,0:T(8,128)S(1)} %pad_maximum_fusion), channel_id=1, source_target_pairs={{0,8},{8,16},{16,24},{12,4},{20,12},{28,20},{1,9},{9,17},{17,25},{... | collective-permute-start | bytes 860168 | tf_op jit(solution)/shard_map/ppermute | solution.py:507
  8.9 0.1 copy.10
  9.0 0.0 collective-permute-done.1.other_ref
  9.0 0.2 place.1.place_ref
  9.3 4.8 %inner.1 = (f32[16,24,128]{2,1,0:T(8,128)S(1)}, f32[16,24,128]{2,1,0:T(8,128)S(1)}, f32[8,2,24,128]{3,2,1,0:T(8,128)S(1)}, f32[8,2,16,128]{3,2,1,0:T(8,128)S(1)}) custom-call(f32[1416,128]{1,0:T(8,128)S(1)} %get-tuple-element.18.keep_ref, f32[1424,128]{1,0:T(8,128)S(1)} %collective-permute-done.1.other_ref), custom_call_target="tpu_custom_call" | custom-call | flops 32768000 | bytes 16384000 | tf_op jit(solution)/shard_map/inner/pallas_call | solution.py:527
  14.0 0.0 collective-permute-done.2.halo_ref
  14.0 2.7 %outer.1 = (f32[16,8,128]{2,1,0:T(8,128)S(1)}, f32[16,8,128]{2,1,0:T(8,128)S(1)}, f32[544,128]{1,0:T(8,128)S(1)}, f32[136,128]{1,0:T(8,128)S(1)}, f32[408,128]{1,0:T(8,128)S(1)}) custom-call(f32[1416,128]{1,0:T(8,128)S(1)} %get-tuple-element.18.keep_ref, f32[1424,128]{1,0:T(8,128)S(1)} %collective-permute-done.1.other_ref, ...), custom_call_target="tpu_custom_call" | custom-call | tf_op jit(solution)/shard_map/outer/pallas_call | solution.py:548
  16.8 0.1 collective-permute-start.6
  16.9 0.5 %collective-permute-start.5 = (f32[408,128]{1,0:T(8,128)S(1)}, f32[408,128]{1,0:T(8,128)S(1)}, u32[]{:S(2)}, u32[]{:S(2)}) collective-permute-start(f32[408,128]{1,0:T(8,128)S(1)} %get-tuple-element.32), channel_id=1, source_target_pairs={{0,4},{4,0},{1,5},{5,1},{2,6},{6,2},{3,7},{7,3},{8,12},{12,8},{9,1... | collective-permute-start | bytes 626696 | tf_op jit(solution)/shard_map/ppermute | solution.py:563
  17.3 0.1 collective-permute-start.4
  17.4 0.4 %collective-permute-start.3 = (f32[16,24,128]{2,1,0:T(8,128)S(1)}, f32[16,24,128]{2,1,0:T(8,128)S(1)}, u32[]{:S(2)}, u32[]{:S(2)}) collective-permute-start(f32[16,24,128]{2,1,0:T(8,128)S(1)} %get-tuple-element.29), channel_id=1, source_target_pairs={{0,4},{4,0},{1,5},{5,1},{2,6},{6,2},{3,7},{7,3},{8,12},{12,8},{9,1... | collective-permute-start | bytes 589832 | tf_op jit(solution)/shard_map/ppermute | solution.py:585
  17.9 0.2 collective-permute-done.6
  18.1 1.6 %collective-permute-start.7 = (f32[136,128]{1,0:T(8,128)S(1)}, f32[136,128]{1,0:T(8,128)S(1)}, u32[]{:S(2)}, u32[]{:S(2)}) collective-permute-start(f32[136,128]{1,0:T(8,128)S(1)} %slice_add_fusion.1), channel_id=1, source_target_pairs={{0,8},{8,16},{16,24},{24,0},{1,9},{9,17},{17,25},{25,1},{2,10},{10... | collective-permute-start | bytes 208904 | tf_op jit(solution)/shard_map/ppermute | solution.py:570
  19.7 0.0 collective-permute-done.5
  19.8 2.6 %collective-permute-start.8 = (f32[136,128]{1,0:T(8,128)S(1)}, f32[136,128]{1,0:T(8,128)S(1)}, u32[]{:S(2)}, u32[]{:S(2)}) collective-permute-start(f32[136,128]{1,0:T(8,128)S(1)} %get-tuple-element.39), channel_id=1, source_target_pairs={{0,16},{8,24},{16,0},{24,8},{1,17},{9,25},{17,1},{25,9},{2,18},{10... | collective-permute-start | bytes 208904 | tf_op jit(solution)/shard_map/ppermute | solution.py:570
  22.3 1.4 %collective-permute-start.9 = (f32[136,128]{1,0:T(8,128)S(1)}, f32[136,128]{1,0:T(8,128)S(1)}, u32[]{:S(2)}, u32[]{:S(2)}) collective-permute-start(f32[136,128]{1,0:T(8,128)S(1)} %get-tuple-element.38), channel_id=1, source_target_pairs={{0,24},{8,0},{16,8},{24,16},{1,25},{9,1},{17,9},{25,17},{2,26},{10... | collective-permute-start | bytes 208904 | tf_op jit(solution)/shard_map/ppermute | solution.py:570
  23.8 0.0 collective-permute-done.4
  23.8 0.0 collective-permute-done.3
  23.8 0.8 %maximum_select_fusion = f32[1,16,64,128]{3,2,1,0:T(8,128)} fusion(f32[1,16,8,128]{3,2,1,0:T(8,128)S(1)} %bitcast.19, f32[1,16,24,128]{3,2,1,0:T(8,128)S(1)} %bitcast.18, f32[1,16,24,128]{3,2,1,0:T(8,128)S(1)} %bitcast.11, f32[1,16,8,128]{3,2,1,0:T(8,128)S(1)} %bitcast.12, pred[]{:T(512)S(6)} %eq.3), kind=kLoop, calls=%fused_computation | loop fusion | flops 917504 | bytes 1048577 | tf_op jit(solution)/shard_map/jit(_where)/select_n | solution.py:587
  24.6 0.0 collective-permute-done.7.one_ref
  24.6 2.6 %collective-permute-done.8.two_ref = f32[136,128]{1,0:T(8,128)S(1)} collective-permute-done((f32[136,128]{1,0:T(8,128)S(1)}, f32[136,128]{1,0:T(8,128)S(1)}, u32[]{:S(2)}, u32[]{:S(2)}) %collective-permute-start.8) | collective-permute-done | bytes 69664 | tf_op jit(solution)/shard_map/ppermute | solution.py:570
  27.3 0.2 collective-permute-done.9.three_ref
  27.5 0.7 %gather.1 = f32[544,128]{1,0:T(8,128)} custom-call(f32[136,128]{1,0:T(8,128)S(1)} %get-tuple-element.40.own_ref, f32[136,128]{1,0:T(8,128)S(1)} %collective-permute-done.7.one_ref, f32[136,128]{1,0:T(8,128)S(1)} %collective-permute-done.8.two_ref, f32[136,128]{1,0:T(8,128)S(1)} %collective-permute-done.9.three_ref), custom_call_target="tpu_custom_call" | custom-call | tf_op jit(solution)/shard_map/gather/pallas_call | solution.py:571
  (4 shorter events, 0.1 us)
Async XLA Ops:
  2.4 1.5 %collective-permute-start = (f32[280,128]{1,0:T(8,128)S(1)}, f32[280,128]{1,0:T(8,128)S(1)}, u32[]{:S(2)}, u32[]{:S(2)}) collective-permute-start(f32[280,128]{1,0:T(8,128)S(1)} %get-tuple-element.20), channel_id=1, source_target_pairs={{0,4},{4,0},{1,5},{5,1},{2,6},{6,2},{3,7},{7,3},{8,12},{12,8},{9,1... | collective-permute-start | bytes 430088 | tf_op jit(solution)/shard_map/ppermute | solution.py:503
  3.9 5.2 %collective-permute-start.1 = (f32[1424,128]{1,0:T(8,128)S(1)}, f32[1424,128]{1,0:T(8,128)S(1)}, u32[]{:S(2)}, u32[]{:S(2)}) collective-permute-start(f32[1424,128]{1,0:T(8,128)S(1)} %get-tuple-element.21), channel_id=1, source_target_pairs={{0,4},{4,0},{1,5},{5,1},{2,6},{6,2},{3,7},{7,3},{8,12},{12,8},{9,1... | collective-permute-start | bytes 2187272 | tf_op jit(solution)/shard_map/ppermute | solution.py:506
  4.3 9.8 %collective-permute-start.2 = (f32[560,128]{1,0:T(8,128)S(1)}, f32[560,128]{1,0:T(8,128)S(1)}, u32[]{:S(2)}, u32[]{:S(2)}) collective-permute-start(f32[560,128]{1,0:T(8,128)S(1)} %pad_maximum_fusion), channel_id=1, source_target_pairs={{0,8},{8,16},{16,24},{12,4},{20,12},{28,20},{1,9},{9,17},{17,25},{... | collective-permute-start | bytes 860168 | tf_op jit(solution)/shard_map/ppermute | solution.py:507
  16.8 1.3 %collective-permute-start.6 = (f32[136,128]{1,0:T(8,128)S(1)}, f32[136,128]{1,0:T(8,128)S(1)}, u32[]{:S(2)}, u32[]{:S(2)}) collective-permute-start(f32[136,128]{1,0:T(8,128)S(1)} %get-tuple-element.33), channel_id=1, source_target_pairs={{0,4},{4,0},{1,5},{5,1},{2,6},{6,2},{3,7},{7,3},{8,12},{12,8},{9,1... | collective-permute-start | bytes 208904 | tf_op jit(solution)/shard_map/ppermute | solution.py:562
  16.9 2.9 %collective-permute-start.5 = (f32[408,128]{1,0:T(8,128)S(1)}, f32[408,128]{1,0:T(8,128)S(1)}, u32[]{:S(2)}, u32[]{:S(2)}) collective-permute-start(f32[408,128]{1,0:T(8,128)S(1)} %get-tuple-element.32), channel_id=1, source_target_pairs={{0,4},{4,0},{1,5},{5,1},{2,6},{6,2},{3,7},{7,3},{8,12},{12,8},{9,1... | collective-permute-start | bytes 626696 | tf_op jit(solution)/shard_map/ppermute | solution.py:563
  17.3 6.4 %collective-permute-start.4 = (f32[16,8,128]{2,1,0:T(8,128)S(1)}, f32[16,8,128]{2,1,0:T(8,128)S(1)}, u32[]{:S(2)}, u32[]{:S(2)}) collective-permute-start(f32[16,8,128]{2,1,0:T(8,128)S(1)} %get-tuple-element.30), channel_id=1, source_target_pairs={{0,4},{4,0},{1,5},{5,1},{2,6},{6,2},{3,7},{7,3},{8,12},{12,8},{9,1... | collective-permute-start | bytes 196616 | tf_op jit(solution)/shard_map/ppermute | solution.py:586
  17.4 6.4 %collective-permute-start.3 = (f32[16,24,128]{2,1,0:T(8,128)S(1)}, f32[16,24,128]{2,1,0:T(8,128)S(1)}, u32[]{:S(2)}, u32[]{:S(2)}) collective-permute-start(f32[16,24,128]{2,1,0:T(8,128)S(1)} %get-tuple-element.29), channel_id=1, source_target_pairs={{0,4},{4,0},{1,5},{5,1},{2,6},{6,2},{3,7},{7,3},{8,12},{12,8},{9,1... | collective-permute-start | bytes 589832 | tf_op jit(solution)/shard_map/ppermute | solution.py:585
  18.1 6.5 %collective-permute-start.7 = (f32[136,128]{1,0:T(8,128)S(1)}, f32[136,128]{1,0:T(8,128)S(1)}, u32[]{:S(2)}, u32[]{:S(2)}) collective-permute-start(f32[136,128]{1,0:T(8,128)S(1)} %slice_add_fusion.1), channel_id=1, source_target_pairs={{0,8},{8,16},{16,24},{24,0},{1,9},{9,17},{17,25},{25,1},{2,10},{10... | collective-permute-start | bytes 208904 | tf_op jit(solution)/shard_map/ppermute | solution.py:570
  19.8 7.5 %collective-permute-start.8 = (f32[136,128]{1,0:T(8,128)S(1)}, f32[136,128]{1,0:T(8,128)S(1)}, u32[]{:S(2)}, u32[]{:S(2)}) collective-permute-start(f32[136,128]{1,0:T(8,128)S(1)} %get-tuple-element.39), channel_id=1, source_target_pairs={{0,16},{8,24},{16,0},{24,8},{1,17},{9,25},{17,1},{25,9},{2,18},{10... | collective-permute-start | bytes 208904 | tf_op jit(solution)/shard_map/ppermute | solution.py:570
  22.3 5.1 %collective-permute-start.9 = (f32[136,128]{1,0:T(8,128)S(1)}, f32[136,128]{1,0:T(8,128)S(1)}, u32[]{:S(2)}, u32[]{:S(2)}) collective-permute-start(f32[136,128]{1,0:T(8,128)S(1)} %get-tuple-element.38), channel_id=1, source_target_pairs={{0,24},{8,0},{16,8},{24,16},{1,25},{9,1},{17,9},{25,17},{2,26},{10... | collective-permute-start | bytes 208904 | tf_op jit(solution)/shard_map/ppermute | solution.py:570

commit v10 on v9

--- a/solution.py
+++ b/solution.py
@@ -227,10 +227,10 @@
             ]
             for i in range(2):
                 p = p_buf[i, zs, here]
-                w = w_buf[i, zs, rows] - (gy[i] - before[i])
                 gx = wet_buf[i, zs, here] * (p_buf[i, zs, ahead] - p)
                 behind = wet_buf[i, zs, back_rows] * (p - p_buf[i, zs, back_rows])
-                w = w - (gx - behind)
+                w = w_buf[i, zs, rows] - (gx - behind)
+                w = w - (gy[i] - before[i])
                 w_out[i, zs, rows] = w
                 if g + 1 < groups:
                     hz = half_buf[i, zs, rows] * (p_buf[i, g * ZB + 1 : (g + 1) * ZB + 1, here] - p)

time: 28.4 us -> 28.3 us (level)
  no operation moved by 1% of the time
where the time goes in v10:
time: 28.3 us; the launch traced here: 28.1 us
  starting transfers between devices  12.2 us (43%)
  Pallas kernels  10.1 us (36%)
  waiting for transfers between devices  4.09 us (14%)
  other arithmetic  0.89 us (3%)
  between operations  0.72 us (3%)
    ppermute x3, starting transfers between devices, shards(): pieces.append(lax.ppermute(piece, 'along', route))  5.62 us
    pallas_call x1, Pallas kernels, shards(): pl.pallas_call(inner_kernel, out_shape=[inner_shape, inner_shape, jax.Sha...  4.78 us
    ppermute x1, starting transfers between devices, shards(): halo = lax.ppermute(halo, pair, route)  4.64 us
    ppermute x3, waiting for transfers between devices, shards(): pieces.append(lax.ppermute(piece, 'along', route))  2.84 us
    pallas_call x1, Pallas kernels, shards(): pl.pallas_call(outer_kernel, out_shape=[outer_shape, outer_shape] + [jax....  2.63 us
    pallas_call x1, Pallas kernels, shards(): pl.pallas_call(edges_kernel, out_shape=[jax.ShapeDtypeStruct((pack_rows,...  1.73 us
    ppermute x1, waiting for transfers between devices, shards(): two = lax.ppermute(two, 'cross', swap)  1 us
    select_n x1, other arithmetic, shards(): jnp.where(low, jnp.concatenate([outer_keep, inner_keep, inner_other, oute...  0.84 us
  transfers between devices with their start and end apart: 10, of which 4 were waited for; matrix products, arithmetic and copies ran while one was open for 4% of the time, Pallas kernels for 18%

profile of v10, /device:TPU:0, one launch (start us, length us, event | category | flops | bytes accessed | tf_op | source)
XLA Modules:
  0.0 28.1 jit_solution(13844742363157610890)
XLA Ops:
  0.6 1.7 %edges.1 = (f32[1416,128]{1,0:T(8,128)S(1)}, f32[1424,128]{1,0:T(8,128)S(1)}, f32[280,128]{1,0:T(8,128)S(1)}, f32[280,128]{1,0:T(8,128)S(1)}, s32[1,512]{1,0:T(1,128)S(1)}, /*index=5*/f32[8,128]{1,0:T(8,128)S(1)}) custom-call(f32[16,64,128]{2,1,0:T(8,128)} %bitcast.14, f32[16,64,128]{2,1,0:T(8,128)} %bitcast.15, f32[16,64,128]{2,1,0:T(8,128)} %bitcast.16, ...), custom_call_target="tpu_custom_call" | custom-call | tf_op jit(solution)/shard_map/edges/pallas_call | solution.py:465
  2.4 0.5 %collective-permute-start = (f32[280,128]{1,0:T(8,128)S(1)}, f32[280,128]{1,0:T(8,128)S(1)}, u32[]{:S(2)}, u32[]{:S(2)}) collective-permute-start(f32[280,128]{1,0:T(8,128)S(1)} %get-tuple-element.20), channel_id=1, source_target_pairs={{0,4},{4,0},{1,5},{5,1},{2,6},{6,2},{3,7},{7,3},{8,12},{12,8},{9,1... | collective-permute-start | bytes 430088 | tf_op jit(solution)/shard_map/ppermute | solution.py:503
  2.9 1.0 %collective-permute-done = f32[280,128]{1,0:T(8,128)S(1)} collective-permute-done((f32[280,128]{1,0:T(8,128)S(1)}, f32[280,128]{1,0:T(8,128)S(1)}, u32[]{:S(2)}, u32[]{:S(2)}) %collective-permute-start) | collective-permute-done | bytes 143392 | tf_op jit(solution)/shard_map/ppermute | solution.py:503
  3.9 0.4 %collective-permute-start.1 = (f32[1424,128]{1,0:T(8,128)S(1)}, f32[1424,128]{1,0:T(8,128)S(1)}, u32[]{:S(2)}, u32[]{:S(2)}) collective-permute-start(f32[1424,128]{1,0:T(8,128)S(1)} %get-tuple-element.21), channel_id=1, source_target_pairs={{0,4},{4,0},{1,5},{5,1},{2,6},{6,2},{3,7},{7,3},{8,12},{12,8},{9,1... | collective-permute-start | bytes 2187272 | tf_op jit(solution)/shard_map/ppermute | solution.py:506
  4.3 4.6 %collective-permute-start.2 = (f32[560,128]{1,0:T(8,128)S(1)}, f32[560,128]{1,0:T(8,128)S(1)}, u32[]{:S(2)}, u32[]{:S(2)}) collective-permute-start(f32[560,128]{1,0:T(8,128)S(1)} %pad_maximum_fusion), channel_id=1, source_target_pairs={{0,8},{8,16},{16,24},{12,4},{20,12},{28,20},{1,9},{9,17},{17,25},{... | collective-permute-start | bytes 860168 | tf_op jit(solution)/shard_map/ppermute | solution.py:507
  8.9 0.1 copy.10
  9.0 0.0 collective-permute-done.1.other_ref
  9.0 0.2 place.1.place_ref
  9.3 4.8 %inner.1 = (f32[16,24,128]{2,1,0:T(8,128)S(1)}, f32[16,24,128]{2,1,0:T(8,128)S(1)}, f32[8,2,24,128]{3,2,1,0:T(8,128)S(1)}, f32[8,2,16,128]{3,2,1,0:T(8,128)S(1)}) custom-call(f32[1416,128]{1,0:T(8,128)S(1)} %get-tuple-element.18.keep_ref, f32[1424,128]{1,0:T(8,128)S(1)} %collective-permute-done.1.other_ref), custom_call_target="tpu_custom_call" | custom-call | flops 32768000 | bytes 16384000 | tf_op jit(solution)/shard_map/inner/pallas_call | solution.py:527
  14.1 0.0 collective-permute-done.2.halo_ref
  14.1 2.6 %outer.1 = (f32[16,8,128]{2,1,0:T(8,128)S(1)}, f32[16,8,128]{2,1,0:T(8,128)S(1)}, f32[544,128]{1,0:T(8,128)S(1)}, f32[136,128]{1,0:T(8,128)S(1)}, f32[408,128]{1,0:T(8,128)S(1)}) custom-call(f32[1416,128]{1,0:T(8,128)S(1)} %get-tuple-element.18.keep_ref, f32[1424,128]{1,0:T(8,128)S(1)} %collective-permute-done.1.other_ref, ...), custom_call_target="tpu_custom_call" | custom-call | tf_op jit(solution)/shard_map/outer/pallas_call | solution.py:548
  16.7 0.1 collective-permute-start.6
  16.8 0.5 %collective-permute-start.5 = (f32[408,128]{1,0:T(8,128)S(1)}, f32[408,128]{1,0:T(8,128)S(1)}, u32[]{:S(2)}, u32[]{:S(2)}) collective-permute-start(f32[408,128]{1,0:T(8,128)S(1)} %get-tuple-element.32), channel_id=1, source_target_pairs={{0,4},{4,0},{1,5},{5,1},{2,6},{6,2},{3,7},{7,3},{8,12},{12,8},{9,1... | collective-permute-start | bytes 626696 | tf_op jit(solution)/shard_map/ppermute | solution.py:563
  17.3 0.1 collective-permute-start.4
  17.4 0.4 %collective-permute-start.3 = (f32[16,24,128]{2,1,0:T(8,128)S(1)}, f32[16,24,128]{2,1,0:T(8,128)S(1)}, u32[]{:S(2)}, u32[]{:S(2)}) collective-permute-start(f32[16,24,128]{2,1,0:T(8,128)S(1)} %get-tuple-element.29), channel_id=1, source_target_pairs={{0,4},{4,0},{1,5},{5,1},{2,6},{6,2},{3,7},{7,3},{8,12},{12,8},{9,1... | collective-permute-start | bytes 589832 | tf_op jit(solution)/shard_map/ppermute | solution.py:585
  17.8 0.2 collective-permute-done.6
  18.0 1.6 %collective-permute-start.7 = (f32[136,128]{1,0:T(8,128)S(1)}, f32[136,128]{1,0:T(8,128)S(1)}, u32[]{:S(2)}, u32[]{:S(2)}) collective-permute-start(f32[136,128]{1,0:T(8,128)S(1)} %slice_add_fusion.1), channel_id=1, source_target_pairs={{0,8},{8,16},{16,24},{24,0},{1,9},{9,17},{17,25},{25,1},{2,10},{10... | collective-permute-start | bytes 208904 | tf_op jit(solution)/shard_map/ppermute | solution.py:570
  19.7 0.0 collective-permute-done.5
  19.7 2.5 %collective-permute-start.8 = (f32[136,128]{1,0:T(8,128)S(1)}, f32[136,128]{1,0:T(8,128)S(1)}, u32[]{:S(2)}, u32[]{:S(2)}) collective-permute-start(f32[136,128]{1,0:T(8,128)S(1)} %get-tuple-element.39), channel_id=1, source_target_pairs={{0,16},{8,24},{16,0},{24,8},{1,17},{9,25},{17,1},{25,9},{2,18},{10... | collective-permute-start | bytes 208904 | tf_op jit(solution)/shard_map/ppermute | solution.py:570
  22.3 1.5 %collective-permute-start.9 = (f32[136,128]{1,0:T(8,128)S(1)}, f32[136,128]{1,0:T(8,128)S(1)}, u32[]{:S(2)}, u32[]{:S(2)}) collective-permute-start(f32[136,128]{1,0:T(8,128)S(1)} %get-tuple-element.38), channel_id=1, source_target_pairs={{0,24},{8,0},{16,8},{24,16},{1,25},{9,1},{17,9},{25,17},{2,26},{10... | collective-permute-start | bytes 208904 | tf_op jit(solution)/shard_map/ppermute | solution.py:570
  23.7 0.0 collective-permute-done.4
  23.7 0.0 collective-permute-done.3
  23.7 0.8 %maximum_select_fusion = f32[1,16,64,128]{3,2,1,0:T(8,128)} fusion(f32[1,16,8,128]{3,2,1,0:T(8,128)S(1)} %bitcast.19, f32[1,16,24,128]{3,2,1,0:T(8,128)S(1)} %bitcast.18, f32[1,16,24,128]{3,2,1,0:T(8,128)S(1)} %bitcast.11, f32[1,16,8,128]{3,2,1,0:T(8,128)S(1)} %bitcast.12, pred[]{:T(512)S(6)} %eq.3), kind=kLoop, calls=%fused_computation | loop fusion | flops 917504 | bytes 1048577 | tf_op jit(solution)/shard_map/jit(_where)/select_n | solution.py:587
  24.6 0.0 collective-permute-done.7.one_ref
  24.6 2.6 %collective-permute-done.8.two_ref = f32[136,128]{1,0:T(8,128)S(1)} collective-permute-done((f32[136,128]{1,0:T(8,128)S(1)}, f32[136,128]{1,0:T(8,128)S(1)}, u32[]{:S(2)}, u32[]{:S(2)}) %collective-permute-start.8) | collective-permute-done | bytes 69664 | tf_op jit(solution)/shard_map/ppermute | solution.py:570
  27.2 0.2 collective-permute-done.9.three_ref
  27.4 0.7 %gather.1 = f32[544,128]{1,0:T(8,128)} custom-call(f32[136,128]{1,0:T(8,128)S(1)} %get-tuple-element.40.own_ref, f32[136,128]{1,0:T(8,128)S(1)} %collective-permute-done.7.one_ref, f32[136,128]{1,0:T(8,128)S(1)} %collective-permute-done.8.two_ref, f32[136,128]{1,0:T(8,128)S(1)} %collective-permute-done.9.three_ref), custom_call_target="tpu_custom_call" | custom-call | tf_op jit(solution)/shard_map/gather/pallas_call | solution.py:571
  (4 shorter events, 0.1 us)
Async XLA Ops:
  2.4 1.5 %collective-permute-start = (f32[280,128]{1,0:T(8,128)S(1)}, f32[280,128]{1,0:T(8,128)S(1)}, u32[]{:S(2)}, u32[]{:S(2)}) collective-permute-start(f32[280,128]{1,0:T(8,128)S(1)} %get-tuple-element.20), channel_id=1, source_target_pairs={{0,4},{4,0},{1,5},{5,1},{2,6},{6,2},{3,7},{7,3},{8,12},{12,8},{9,1... | collective-permute-start | bytes 430088 | tf_op jit(solution)/shard_map/ppermute | solution.py:503
  3.9 5.2 %collective-permute-start.1 = (f32[1424,128]{1,0:T(8,128)S(1)}, f32[1424,128]{1,0:T(8,128)S(1)}, u32[]{:S(2)}, u32[]{:S(2)}) collective-permute-start(f32[1424,128]{1,0:T(8,128)S(1)} %get-tuple-element.21), channel_id=1, source_target_pairs={{0,4},{4,0},{1,5},{5,1},{2,6},{6,2},{3,7},{7,3},{8,12},{12,8},{9,1... | collective-permute-start | bytes 2187272 | tf_op jit(solution)/shard_map/ppermute | solution.py:506
  4.3 9.8 %collective-permute-start.2 = (f32[560,128]{1,0:T(8,128)S(1)}, f32[560,128]{1,0:T(8,128)S(1)}, u32[]{:S(2)}, u32[]{:S(2)}) collective-permute-start(f32[560,128]{1,0:T(8,128)S(1)} %pad_maximum_fusion), channel_id=1, source_target_pairs={{0,8},{8,16},{16,24},{12,4},{20,12},{28,20},{1,9},{9,17},{17,25},{... | collective-permute-start | bytes 860168 | tf_op jit(solution)/shard_map/ppermute | solution.py:507
  16.7 1.3 %collective-permute-start.6 = (f32[136,128]{1,0:T(8,128)S(1)}, f32[136,128]{1,0:T(8,128)S(1)}, u32[]{:S(2)}, u32[]{:S(2)}) collective-permute-start(f32[136,128]{1,0:T(8,128)S(1)} %get-tuple-element.33), channel_id=1, source_target_pairs={{0,4},{4,0},{1,5},{5,1},{2,6},{6,2},{3,7},{7,3},{8,12},{12,8},{9,1... | collective-permute-start | bytes 208904 | tf_op jit(solution)/shard_map/ppermute | solution.py:562
  16.8 2.9 %collective-permute-start.5 = (f32[408,128]{1,0:T(8,128)S(1)}, f32[408,128]{1,0:T(8,128)S(1)}, u32[]{:S(2)}, u32[]{:S(2)}) collective-permute-start(f32[408,128]{1,0:T(8,128)S(1)} %get-tuple-element.32), channel_id=1, source_target_pairs={{0,4},{4,0},{1,5},{5,1},{2,6},{6,2},{3,7},{7,3},{8,12},{12,8},{9,1... | collective-permute-start | bytes 626696 | tf_op jit(solution)/shard_map/ppermute | solution.py:563
  17.3 6.4 %collective-permute-start.4 = (f32[16,8,128]{2,1,0:T(8,128)S(1)}, f32[16,8,128]{2,1,0:T(8,128)S(1)}, u32[]{:S(2)}, u32[]{:S(2)}) collective-permute-start(f32[16,8,128]{2,1,0:T(8,128)S(1)} %get-tuple-element.30), channel_id=1, source_target_pairs={{0,4},{4,0},{1,5},{5,1},{2,6},{6,2},{3,7},{7,3},{8,12},{12,8},{9,1... | collective-permute-start | bytes 196616 | tf_op jit(solution)/shard_map/ppermute | solution.py:586
  17.4 6.4 %collective-permute-start.3 = (f32[16,24,128]{2,1,0:T(8,128)S(1)}, f32[16,24,128]{2,1,0:T(8,128)S(1)}, u32[]{:S(2)}, u32[]{:S(2)}) collective-permute-start(f32[16,24,128]{2,1,0:T(8,128)S(1)} %get-tuple-element.29), channel_id=1, source_target_pairs={{0,4},{4,0},{1,5},{5,1},{2,6},{6,2},{3,7},{7,3},{8,12},{12,8},{9,1... | collective-permute-start | bytes 589832 | tf_op jit(solution)/shard_map/ppermute | solution.py:585
  18.0 6.5 %collective-permute-start.7 = (f32[136,128]{1,0:T(8,128)S(1)}, f32[136,128]{1,0:T(8,128)S(1)}, u32[]{:S(2)}, u32[]{:S(2)}) collective-permute-start(f32[136,128]{1,0:T(8,128)S(1)} %slice_add_fusion.1), channel_id=1, source_target_pairs={{0,8},{8,16},{16,24},{24,0},{1,9},{9,17},{17,25},{25,1},{2,10},{10... | collective-permute-start | bytes 208904 | tf_op jit(solution)/shard_map/ppermute | solution.py:570
  19.7 7.5 %collective-permute-start.8 = (f32[136,128]{1,0:T(8,128)S(1)}, f32[136,128]{1,0:T(8,128)S(1)}, u32[]{:S(2)}, u32[]{:S(2)}) collective-permute-start(f32[136,128]{1,0:T(8,128)S(1)} %get-tuple-element.39), channel_id=1, source_target_pairs={{0,16},{8,24},{16,0},{24,8},{1,17},{9,25},{17,1},{25,9},{2,18},{10... | collective-permute-start | bytes 208904 | tf_op jit(solution)/shard_map/ppermute | solution.py:570
  22.3 5.1 %collective-permute-start.9 = (f32[136,128]{1,0:T(8,128)S(1)}, f32[136,128]{1,0:T(8,128)S(1)}, u32[]{:S(2)}, u32[]{:S(2)}) collective-permute-start(f32[136,128]{1,0:T(8,128)S(1)} %get-tuple-element.38), channel_id=1, source_target_pairs={{0,24},{8,0},{16,8},{24,16},{1,25},{9,1},{17,9},{25,17},{2,26},{10... | collective-permute-start | bytes 208904 | tf_op jit(solution)/shard_map/ppermute | solution.py:570

commit v11 on v10

--- a/solution.py
+++ b/solution.py
@@ -152,20 +152,26 @@
     place_ref[...] = jnp.where(rows_of(place_ref.shape) == slot, 1.0, 0.0).astype(jnp.bfloat16)
 
 
-def gather_kernel(own_ref, one_ref, two_ref, three_ref, out_ref, sems):
+def copy_blocks(blocks, out_ref, sems):
     chips = 4
     along = lax.axis_index("along")
     count = out_ref.shape[0] // chips
     copies = []
-    for i, (ref, ahead) in enumerate(
-        ((own_ref, 0), (one_ref, 3), (two_ref, 2), (three_ref, 1))
-    ):
+    for i, (ref, ahead) in enumerate(blocks):
         at = pl.multiple_of(lax.rem(along + ahead, chips) * count, SUB)
         copies.append(pltpu.make_async_copy(ref, out_ref.at[pl.ds(at, count)], sems.at[i]))
     for copy in copies:
         copy.start()
     for copy in copies:
         copy.wait()
+
+
+def gather_kernel(own_ref, one_ref, out_ref, sems):
+    copy_blocks(((own_ref, 0), (one_ref, 3)), out_ref, sems)
+
+
+def last_kernel(two_ref, three_ref, in_ref, out_ref, sems):
+    copy_blocks(((two_ref, 2), (three_ref, 1)), out_ref, sems)
 
 
 def masks(depth, stiff, d_buf, wet_buf, scale_buf, half_buf, tile):
@@ -568,15 +574,26 @@
             piece = panel_first if k == 1 else panel_rest[(k - 2) * some : (k - 1) * some]
             route = [(i, (i + k) % along_count) for i in range(along_count)]
             pieces.append(lax.ppermute(piece, "along", route))
+        out_shape = jax.ShapeDtypeStruct((count * parts, cols), f32)
         received = pl.pallas_call(
             gather_kernel,
-            out_shape=jax.ShapeDtypeStruct((count * parts, cols), f32),
-            in_specs=[spec] * 4,
+            out_shape=out_shape,
+            in_specs=[spec] * 2,
             out_specs=hbm,
-            scratch_shapes=[pltpu.SemaphoreType.DMA((4,))],
+            scratch_shapes=[pltpu.SemaphoreType.DMA((2,))],
             compiler_params=params,
             name="gather",
-        )(*pieces)
+        )(*pieces[:2])
+        received = pl.pallas_call(
+            last_kernel,
+            out_shape=out_shape,
+            in_specs=[spec, spec, hbm],
+            out_specs=hbm,
+            scratch_shapes=[pltpu.SemaphoreType.DMA((2,))],
+            input_output_aliases={2: 0},
+            compiler_params=params,
+            name="last",
+        )(pieces[2], pieces[3], pltpu.with_memory_space_constraint(received, pltpu.HBM))
     else:
         panels = jnp.concatenate([panel_first, panel_rest], 0).reshape(along_count, some, cols)
         received = lax.all_to_all(panels, "along", split_axis=0, concat_axis=0, tiled=True)

time: 28.3 us -> 28.2 us (level)
  waiting for transfers between devices: 4.09 us -> 3.41 us
  Pallas kernels: 10.1 us -> 10.7 us
    ppermute x3, waiting for transfers between devices: 2.84 us -> 2.16 us  [shards(): pieces.append(lax.ppermute(piece, 'along', route))]
    pallas_call x1 -> x2, Pallas kernels: 0.73 us -> 1.34 us  [the longest x1 0.67 us: shards(): pl.pallas_call(gather_kernel, out_shape=out_shape, in_specs=[spec] * 2, o...]
  transfers between devices with their start and end apart: 10 -> 10, of which waited for: 4 -> 4; matrix products, arithmetic and copies ran while one was open for 4% -> 4% of each run, Pallas kernels for 18% -> 20%
where the time goes in v11:
time: 28.2 us; the launch traced here: 28.1 us
  starting transfers between devices  12.2 us (43%)
  Pallas kernels  10.7 us (38%)
  waiting for transfers between devices  3.41 us (12%)
  other arithmetic  0.89 us (3%)
  between operations  0.73 us (3%)
    ppermute x3, starting transfers between devices, shards(): pieces.append(lax.ppermute(piece, 'along', route))  5.62 us
    pallas_call x1, Pallas kernels, shards(): pl.pallas_call(inner_kernel, out_shape=[inner_shape, inner_shape, jax.Sha...  4.78 us
    ppermute x1, starting transfers between devices, shards(): halo = lax.ppermute(halo, pair, route)  4.64 us
    pallas_call x1, Pallas kernels, shards(): pl.pallas_call(outer_kernel, out_shape=[outer_shape, outer_shape] + [jax....  2.63 us
    ppermute x3, waiting for transfers between devices, shards(): pieces.append(lax.ppermute(piece, 'along', route))  2.16 us
    pallas_call x1, Pallas kernels, shards(): pl.pallas_call(edges_kernel, out_shape=[jax.ShapeDtypeStruct((pack_rows,...  1.73 us
    ppermute x1, waiting for transfers between devices, shards(): two = lax.ppermute(two, 'cross', swap)  1 us
    select_n x1, other arithmetic, shards(): jnp.where(low, jnp.concatenate([outer_keep, inner_keep, inner_other, oute...  0.84 us
  transfers between devices with their start and end apart: 10, of which 4 were waited for; matrix products, arithmetic and copies ran while one was open for 4% of the time, Pallas kernels for 20%

profile of v11, /device:TPU:0, one launch (start us, length us, event | category | flops | bytes accessed | tf_op | source)
XLA Modules:
  0.0 28.1 jit_solution(5856682731470084300)
XLA Ops:
  0.6 1.7 %edges.1 = (f32[1416,128]{1,0:T(8,128)S(1)}, f32[1424,128]{1,0:T(8,128)S(1)}, f32[280,128]{1,0:T(8,128)S(1)}, f32[280,128]{1,0:T(8,128)S(1)}, s32[1,512]{1,0:T(1,128)S(1)}, /*index=5*/f32[8,128]{1,0:T(8,128)S(1)}) custom-call(f32[16,64,128]{2,1,0:T(8,128)} %bitcast.15, f32[16,64,128]{2,1,0:T(8,128)} %bitcast.16, f32[16,64,128]{2,1,0:T(8,128)} %bitcast.17, ...), custom_call_target="tpu_custom_call" | custom-call | tf_op jit(solution)/shard_map/edges/pallas_call | solution.py:471
  2.4 0.5 %collective-permute-start = (f32[280,128]{1,0:T(8,128)S(1)}, f32[280,128]{1,0:T(8,128)S(1)}, u32[]{:S(2)}, u32[]{:S(2)}) collective-permute-start(f32[280,128]{1,0:T(8,128)S(1)} %get-tuple-element.20), channel_id=1, source_target_pairs={{0,4},{4,0},{1,5},{5,1},{2,6},{6,2},{3,7},{7,3},{8,12},{12,8},{9,1... | collective-permute-start | bytes 430088 | tf_op jit(solution)/shard_map/ppermute | solution.py:509
  2.9 1.0 %collective-permute-done = f32[280,128]{1,0:T(8,128)S(1)} collective-permute-done((f32[280,128]{1,0:T(8,128)S(1)}, f32[280,128]{1,0:T(8,128)S(1)}, u32[]{:S(2)}, u32[]{:S(2)}) %collective-permute-start) | collective-permute-done | bytes 143392 | tf_op jit(solution)/shard_map/ppermute | solution.py:509
  3.9 0.4 %collective-permute-start.1 = (f32[1424,128]{1,0:T(8,128)S(1)}, f32[1424,128]{1,0:T(8,128)S(1)}, u32[]{:S(2)}, u32[]{:S(2)}) collective-permute-start(f32[1424,128]{1,0:T(8,128)S(1)} %get-tuple-element.21), channel_id=1, source_target_pairs={{0,4},{4,0},{1,5},{5,1},{2,6},{6,2},{3,7},{7,3},{8,12},{12,8},{9,1... | collective-permute-start | bytes 2187272 | tf_op jit(solution)/shard_map/ppermute | solution.py:512
  4.3 4.6 %collective-permute-start.2 = (f32[560,128]{1,0:T(8,128)S(1)}, f32[560,128]{1,0:T(8,128)S(1)}, u32[]{:S(2)}, u32[]{:S(2)}) collective-permute-start(f32[560,128]{1,0:T(8,128)S(1)} %pad_maximum_fusion), channel_id=1, source_target_pairs={{0,8},{8,16},{16,24},{12,4},{20,12},{28,20},{1,9},{9,17},{17,25},{... | collective-permute-start | bytes 860168 | tf_op jit(solution)/shard_map/ppermute | solution.py:513
  8.9 0.1 copy.11
  9.0 0.0 collective-permute-done.1.other_ref
  9.0 0.2 place.1.place_ref
  9.3 4.8 %inner.1 = (f32[16,24,128]{2,1,0:T(8,128)S(1)}, f32[16,24,128]{2,1,0:T(8,128)S(1)}, f32[8,2,24,128]{3,2,1,0:T(8,128)S(1)}, f32[8,2,16,128]{3,2,1,0:T(8,128)S(1)}) custom-call(f32[1416,128]{1,0:T(8,128)S(1)} %get-tuple-element.18.keep_ref, f32[1424,128]{1,0:T(8,128)S(1)} %collective-permute-done.1.other_ref), custom_call_target="tpu_custom_call" | custom-call | flops 32768000 | bytes 16384000 | tf_op jit(solution)/shard_map/inner/pallas_call | solution.py:533
  14.1 0.0 collective-permute-done.2.halo_ref
  14.1 2.6 %outer.1 = (f32[16,8,128]{2,1,0:T(8,128)S(1)}, f32[16,8,128]{2,1,0:T(8,128)S(1)}, f32[544,128]{1,0:T(8,128)S(1)}, f32[136,128]{1,0:T(8,128)S(1)}, f32[408,128]{1,0:T(8,128)S(1)}) custom-call(f32[1416,128]{1,0:T(8,128)S(1)} %get-tuple-element.18.keep_ref, f32[1424,128]{1,0:T(8,128)S(1)} %collective-permute-done.1.other_ref, ...), custom_call_target="tpu_custom_call" | custom-call | tf_op jit(solution)/shard_map/outer/pallas_call | solution.py:554
  16.7 0.1 collective-permute-start.8
  16.8 0.5 %collective-permute-start.5 = (f32[408,128]{1,0:T(8,128)S(1)}, f32[408,128]{1,0:T(8,128)S(1)}, u32[]{:S(2)}, u32[]{:S(2)}) collective-permute-start(f32[408,128]{1,0:T(8,128)S(1)} %get-tuple-element.32), channel_id=1, source_target_pairs={{0,4},{4,0},{1,5},{5,1},{2,6},{6,2},{3,7},{7,3},{8,12},{12,8},{9,1... | collective-permute-start | bytes 626696 | tf_op jit(solution)/shard_map/ppermute | solution.py:569
  17.3 0.1 collective-permute-start.4
  17.4 0.4 %collective-permute-start.3 = (f32[16,24,128]{2,1,0:T(8,128)S(1)}, f32[16,24,128]{2,1,0:T(8,128)S(1)}, u32[]{:S(2)}, u32[]{:S(2)}) collective-permute-start(f32[16,24,128]{2,1,0:T(8,128)S(1)} %get-tuple-element.29), channel_id=1, source_target_pairs={{0,4},{4,0},{1,5},{5,1},{2,6},{6,2},{3,7},{7,3},{8,12},{12,8},{9,1... | collective-permute-start | bytes 589832 | tf_op jit(solution)/shard_map/ppermute | solution.py:602
  17.8 0.2 collective-permute-done.8
  18.0 1.6 %collective-permute-start.9 = (f32[136,128]{1,0:T(8,128)S(1)}, f32[136,128]{1,0:T(8,128)S(1)}, u32[]{:S(2)}, u32[]{:S(2)}) collective-permute-start(f32[136,128]{1,0:T(8,128)S(1)} %slice_add_fusion.1), channel_id=1, source_target_pairs={{0,8},{8,16},{16,24},{24,0},{1,9},{9,17},{17,25},{25,1},{2,10},{10... | collective-permute-start | bytes 208904 | tf_op jit(solution)/shard_map/ppermute | solution.py:576
  19.7 0.0 collective-permute-done.5
  19.7 2.5 %collective-permute-start.6 = (f32[136,128]{1,0:T(8,128)S(1)}, f32[136,128]{1,0:T(8,128)S(1)}, u32[]{:S(2)}, u32[]{:S(2)}) collective-permute-start(f32[136,128]{1,0:T(8,128)S(1)} %get-tuple-element.40), channel_id=1, source_target_pairs={{0,16},{8,24},{16,0},{24,8},{1,17},{9,25},{17,1},{25,9},{2,18},{10... | collective-permute-start | bytes 208904 | tf_op jit(solution)/shard_map/ppermute | solution.py:576
  22.3 1.5 %collective-permute-start.7 = (f32[136,128]{1,0:T(8,128)S(1)}, f32[136,128]{1,0:T(8,128)S(1)}, u32[]{:S(2)}, u32[]{:S(2)}) collective-permute-start(f32[136,128]{1,0:T(8,128)S(1)} %get-tuple-element.39), channel_id=1, source_target_pairs={{0,24},{8,0},{16,8},{24,16},{1,25},{9,1},{17,9},{25,17},{2,26},{10... | collective-permute-start | bytes 208904 | tf_op jit(solution)/shard_map/ppermute | solution.py:576
  23.7 0.0 collective-permute-done.4
  23.7 0.0 collective-permute-done.3
  23.7 0.8 %maximum_select_fusion = f32[1,16,64,128]{3,2,1,0:T(8,128)} fusion(f32[1,16,8,128]{3,2,1,0:T(8,128)S(1)} %bitcast.19, f32[1,16,24,128]{3,2,1,0:T(8,128)S(1)} %bitcast.18, f32[1,16,24,128]{3,2,1,0:T(8,128)S(1)} %bitcast.11, f32[1,16,8,128]{3,2,1,0:T(8,128)S(1)} %bitcast.12, pred[]{:T(512)S(6)} %eq.3), kind=kLoop, calls=%fused_computation | loop fusion | flops 917504 | bytes 1048577 | tf_op jit(solution)/shard_map/jit(_where)/select_n | solution.py:604
  24.6 0.0 collective-permute-done.9.one_ref
  24.6 0.7 %gather.1.in_ref = f32[544,128]{1,0:T(8,128)} custom-call(f32[136,128]{1,0:T(8,128)S(1)} %get-tuple-element.38.own_ref, f32[136,128]{1,0:T(8,128)S(1)} %collective-permute-done.9.one_ref), custom_call_target="tpu_custom_call" | custom-call | tf_op jit(solution)/shard_map/gather/pallas_call | solution.py:578
  25.2 2.0 %collective-permute-done.6.two_ref = f32[136,128]{1,0:T(8,128)S(1)} collective-permute-done((f32[136,128]{1,0:T(8,128)S(1)}, f32[136,128]{1,0:T(8,128)S(1)}, u32[]{:S(2)}, u32[]{:S(2)}) %collective-permute-start.6) | collective-permute-done | bytes 69664 | tf_op jit(solution)/shard_map/ppermute | solution.py:576
  27.2 0.2 collective-permute-done.7.three_ref
  27.4 0.7 %last.1 = f32[544,128]{1,0:T(8,128)} custom-call(f32[136,128]{1,0:T(8,128)S(1)} %collective-permute-done.6.two_ref, f32[136,128]{1,0:T(8,128)S(1)} %collective-permute-done.7.three_ref, f32[544,128]{1,0:T(8,128)} %gather.1.in_ref), custom_call_target="tpu_custom_call", output_to_operand_aliasing={{}: (2, {})} | custom-call | tf_op jit(solution)/shard_map/last/pallas_call | solution.py:587
  (4 shorter events, 0.1 us)
Async XLA Ops:
  2.4 1.5 %collective-permute-start = (f32[280,128]{1,0:T(8,128)S(1)}, f32[280,128]{1,0:T(8,128)S(1)}, u32[]{:S(2)}, u32[]{:S(2)}) collective-permute-start(f32[280,128]{1,0:T(8,128)S(1)} %get-tuple-element.20), channel_id=1, source_target_pairs={{0,4},{4,0},{1,5},{5,1},{2,6},{6,2},{3,7},{7,3},{8,12},{12,8},{9,1... | collective-permute-start | bytes 430088 | tf_op jit(solution)/shard_map/ppermute | solution.py:509
  3.9 5.2 %collective-permute-start.1 = (f32[1424,128]{1,0:T(8,128)S(1)}, f32[1424,128]{1,0:T(8,128)S(1)}, u32[]{:S(2)}, u32[]{:S(2)}) collective-permute-start(f32[1424,128]{1,0:T(8,128)S(1)} %get-tuple-element.21), channel_id=1, source_target_pairs={{0,4},{4,0},{1,5},{5,1},{2,6},{6,2},{3,7},{7,3},{8,12},{12,8},{9,1... | collective-permute-start | bytes 2187272 | tf_op jit(solution)/shard_map/ppermute | solution.py:512
  4.3 9.8 %collective-permute-start.2 = (f32[560,128]{1,0:T(8,128)S(1)}, f32[560,128]{1,0:T(8,128)S(1)}, u32[]{:S(2)}, u32[]{:S(2)}) collective-permute-start(f32[560,128]{1,0:T(8,128)S(1)} %pad_maximum_fusion), channel_id=1, source_target_pairs={{0,8},{8,16},{16,24},{12,4},{20,12},{28,20},{1,9},{9,17},{17,25},{... | collective-permute-start | bytes 860168 | tf_op jit(solution)/shard_map/ppermute | solution.py:513
  16.7 1.3 %collective-permute-start.8 = (f32[136,128]{1,0:T(8,128)S(1)}, f32[136,128]{1,0:T(8,128)S(1)}, u32[]{:S(2)}, u32[]{:S(2)}) collective-permute-start(f32[136,128]{1,0:T(8,128)S(1)} %get-tuple-element.33), channel_id=1, source_target_pairs={{0,4},{4,0},{1,5},{5,1},{2,6},{6,2},{3,7},{7,3},{8,12},{12,8},{9,1... | collective-permute-start | bytes 208904 | tf_op jit(solution)/shard_map/ppermute | solution.py:568
  16.8 2.9 %collective-permute-start.5 = (f32[408,128]{1,0:T(8,128)S(1)}, f32[408,128]{1,0:T(8,128)S(1)}, u32[]{:S(2)}, u32[]{:S(2)}) collective-permute-start(f32[408,128]{1,0:T(8,128)S(1)} %get-tuple-element.32), channel_id=1, source_target_pairs={{0,4},{4,0},{1,5},{5,1},{2,6},{6,2},{3,7},{7,3},{8,12},{12,8},{9,1... | collective-permute-start | bytes 626696 | tf_op jit(solution)/shard_map/ppermute | solution.py:569
  17.3 6.4 %collective-permute-start.4 = (f32[16,8,128]{2,1,0:T(8,128)S(1)}, f32[16,8,128]{2,1,0:T(8,128)S(1)}, u32[]{:S(2)}, u32[]{:S(2)}) collective-permute-start(f32[16,8,128]{2,1,0:T(8,128)S(1)} %get-tuple-element.30), channel_id=1, source_target_pairs={{0,4},{4,0},{1,5},{5,1},{2,6},{6,2},{3,7},{7,3},{8,12},{12,8},{9,1... | collective-permute-start | bytes 196616 | tf_op jit(solution)/shard_map/ppermute | solution.py:603
  17.4 6.4 %collective-permute-start.3 = (f32[16,24,128]{2,1,0:T(8,128)S(1)}, f32[16,24,128]{2,1,0:T(8,128)S(1)}, u32[]{:S(2)}, u32[]{:S(2)}) collective-permute-start(f32[16,24,128]{2,1,0:T(8,128)S(1)} %get-tuple-element.29), channel_id=1, source_target_pairs={{0,4},{4,0},{1,5},{5,1},{2,6},{6,2},{3,7},{7,3},{8,12},{12,8},{9,1... | collective-permute-start | bytes 589832 | tf_op jit(solution)/shard_map/ppermute | solution.py:602
  18.0 6.5 %collective-permute-start.9 = (f32[136,128]{1,0:T(8,128)S(1)}, f32[136,128]{1,0:T(8,128)S(1)}, u32[]{:S(2)}, u32[]{:S(2)}) collective-permute-start(f32[136,128]{1,0:T(8,128)S(1)} %slice_add_fusion.1), channel_id=1, source_target_pairs={{0,8},{8,16},{16,24},{24,0},{1,9},{9,17},{17,25},{25,1},{2,10},{10... | collective-permute-start | bytes 208904 | tf_op jit(solution)/shard_map/ppermute | solution.py:576
  19.7 7.5 %collective-permute-start.6 = (f32[136,128]{1,0:T(8,128)S(1)}, f32[136,128]{1,0:T(8,128)S(1)}, u32[]{:S(2)}, u32[]{:S(2)}) collective-permute-start(f32[136,128]{1,0:T(8,128)S(1)} %get-tuple-element.40), channel_id=1, source_target_pairs={{0,16},{8,24},{16,0},{24,8},{1,17},{9,25},{17,1},{25,9},{2,18},{10... | collective-permute-start | bytes 208904 | tf_op jit(solution)/shard_map/ppermute | solution.py:576
  22.3 5.1 %collective-permute-start.7 = (f32[136,128]{1,0:T(8,128)S(1)}, f32[136,128]{1,0:T(8,128)S(1)}, u32[]{:S(2)}, u32[]{:S(2)}) collective-permute-start(f32[136,128]{1,0:T(8,128)S(1)} %get-tuple-element.39), channel_id=1, source_target_pairs={{0,24},{8,0},{16,8},{24,16},{1,25},{9,1},{17,9},{25,17},{2,26},{10... | collective-permute-start | bytes 208904 | tf_op jit(solution)/shard_map/ppermute | solution.py:576
